TPU v7x, 512 devices: a whole 4x8x8 slice. The times are simulated.
512 devices in a mesh: tile: 128 (over y, z, core), clip: 4 (over x).
Axes of the slice: x: 4, y: 8, z: 8, core: 2. Of those that a mesh axis runs over, the one named last changes fastest.
Arguments:
- features: bfloat16 [4, 128, 96, 3, 4096], P('clip', 'tile'), may hold values from -6 to 6
- conv_weight: bfloat16 [3, 9, 3, 96], replicated, may hold values from -0.125 to 0.125
- bias: float32 [3], replicated, may hold values from -2 to 2
- blend_profile: int32 [32], replicated, may hold values from 1 to 8
- tile_ids: int32 [4, 128], P('clip'), may hold values from 0 to 127, each once within a row
- reward_grad: bfloat16 [4, 128, 3, 4096], P('clip', 'tile'), may hold values from -6 to 6
Outputs:
- decoded: bfloat16 [4, 128, 3, 4096], P('clip', 'tile')
- feature_grad: bfloat16 [4, 128, 96, 3, 4096], P('clip', 'tile')
- weight_grad: float32 [3, 9, 3, 96], replicated
- bias_grad: float32 [3], replicated
Inputs may be any that keep to these rules, and one draw needn't show every extreme that they name: Each row of tile_ids names each of the 128 tiles of the window once; tile v lies in tile row v // 16 and tile column v % 16.
All inputs are finite; a program needn't handle non-finite values.
Results may differ from a plain program's by a relative error of at most 0.023.
Values may be sent and summed in bfloat16 or wider, within the bound.
No kernel may reach another device: no remote copies, remote signals or barrier semaphores. Data moves between devices by JAX's collectives and lax.ppermute only.
A program may use at most 64 MiB of HBM per device.

v0:
```python
import math

import jax
import jax.numpy as jnp
from jax import lax
from jax.sharding import PartitionSpec as P

neighbour_steps = [(-1, -1), (-1, 0), (-1, 1), (0, -1), (0, 1), (1, -1), (1, 0), (1, 1)]


def cut_region(tile_block, step_y, step_x, intersection):
    edge = tile_block.shape[-1]
    if step_y == 1:
        tile_block = tile_block[..., :intersection, :]
    elif step_y == -1:
        tile_block = tile_block[..., edge - intersection :, :]
    if step_x == 1:
        tile_block = tile_block[..., :intersection]
    elif step_x == -1:
        tile_block = tile_block[..., edge - intersection :]
    return tile_block


def place_region(region, step_y, step_x, stride):
    pad_y = (stride, 0) if step_y == 1 else (0, stride) if step_y == -1 else (0, 0)
    pad_x = (stride, 0) if step_x == 1 else (0, stride) if step_x == -1 else (0, 0)
    return jnp.pad(region, ((0, 0),) * (region.ndim - 2) + (pad_y, pad_x))


def pick_regions(gathered, neighbours, intersection, edge):
    regions = []
    for step_y, step_x, present, holder in neighbours:
        whole_tile = lax.dynamic_index_in_dim(gathered, holder, keepdims=False)
        whole_tile = whole_tile.reshape(whole_tile.shape[0], edge, edge)
        regions.append(cut_region(whole_tile, step_y, step_x, intersection))
    return regions


def per_device(features, conv_weight, bias, blend_profile, tile_ids, reward_grad):
    pixels = features.shape[-1]
    edge = math.isqrt(pixels)
    intersection = blend_profile.shape[0]
    stride = edge - intersection
    colours = conv_weight.shape[2]
    channels = conv_weight.shape[3]
    slots = tile_ids.shape[1]
    own_index = lax.axis_index("tile")
    peer_count = lax.axis_size("tile")
    tiles_across = min(16, peer_count)
    tile_count_rows = slots // tiles_across
    tile_list = tile_ids[0]
    mine = lax.dynamic_index_in_dim(tile_list, own_index, keepdims=False)
    my_row = mine // tiles_across
    my_col = mine % tiles_across
    places = jnp.arange(slots, dtype=jnp.int32)
    neighbours = []
    for step_y, step_x in neighbour_steps:
        tile_row = my_row + step_y
        tile_col = my_col + step_x
        present = (
            (tile_row >= 0)
            & (tile_row < tile_count_rows)
            & (tile_col >= 0)
            & (tile_col < tiles_across)
        )
        target = tile_row * tiles_across + tile_col
        holder = jnp.sum(jnp.where(tile_list == target, places, 0))
        neighbours.append((step_y, step_x, present, holder))
    distance_range = jnp.arange(edge)
    distance = jnp.minimum(jnp.minimum(distance_range, edge - 1 - distance_range), intersection - 1)
    lookup = (distance[:, None] == jnp.arange(intersection)[None, :]).astype(jnp.float32)
    factor = jnp.dot(lookup, blend_profile.astype(jnp.float32))
    weight_map = factor[:, None] * factor[None, :]
    frames = features[0, 0]
    kernel = conv_weight.reshape(conv_weight.shape[0], 9 * colours, channels)
    tap_sums = jnp.einsum("tjc,ctp->jp", kernel, frames, preferred_element_type=jnp.float32)
    tap_sums = tap_sums.reshape(3, 3, colours, edge, edge)
    padded = jnp.pad(tap_sums, ((0, 0), (0, 0), (0, 0), (1, 1), (1, 1)))
    tile_image = jnp.broadcast_to(bias[:, None, None], (colours, edge, edge))
    for shift_y in range(3):
        for shift_x in range(3):
            tile_image = (
                tile_image
                + padded[shift_y, shift_x, :, shift_y : shift_y + edge, shift_x : shift_x + edge]
            )
    tile_image = tile_image.astype(jnp.bfloat16)
    cotangent = reward_grad[0, 0]
    gathered_images = lax.all_gather(
        tile_image.reshape(1, colours, pixels), "tile", axis=0, tiled=True
    )
    gathered_grads = lax.all_gather(
        cotangent.reshape(1, colours, pixels), "tile", axis=0, tiled=True
    )
    forward_regions = pick_regions(gathered_images, neighbours, intersection, edge)
    backward_regions = pick_regions(gathered_grads, neighbours, intersection, edge)
    numerator = weight_map * tile_image.astype(jnp.float32)
    weight_total = weight_map
    summed = cotangent.astype(jnp.float32).reshape(colours, edge, edge)
    for (step_y, step_x, present, holder), image_part, grad_part in zip(
        neighbours, forward_regions, backward_regions
    ):
        present_mask = present.astype(jnp.float32)
        part_weight = place_region(
            cut_region(weight_map, step_y, step_x, intersection), step_y, step_x, stride
        )
        numerator = numerator + present_mask * part_weight * place_region(
            image_part.astype(jnp.float32), step_y, step_x, stride
        )
        weight_total = weight_total + present_mask * part_weight
        summed = summed + present_mask * place_region(
            grad_part.astype(jnp.float32), step_y, step_x, stride
        )
    decoded = (numerator / weight_total).astype(jnp.bfloat16).reshape(1, 1, colours, pixels)
    image_grad = (weight_map / weight_total * summed).astype(jnp.bfloat16)
    grad_padded = jnp.pad(image_grad, ((0, 0), (1, 1), (1, 1)))
    shifted = []
    for shift_y in range(3):
        for shift_x in range(3):
            shifted.append(
                grad_padded[:, 2 - shift_y : 2 - shift_y + edge, 2 - shift_x : 2 - shift_x + edge]
            )
    grad_stack = jnp.stack(shifted, 0).reshape(9 * colours, pixels)
    value_grad = jnp.einsum("tjc,jp->ctp", kernel, grad_stack, preferred_element_type=jnp.float32)
    feature_grad = value_grad.astype(jnp.bfloat16).reshape(1, 1, channels, frames.shape[1], pixels)
    kernel_local = jnp.einsum("jp,ctp->tjc", grad_stack, frames, preferred_element_type=jnp.float32)
    bias_local = jnp.sum(image_grad.astype(jnp.float32), axis=(1, 2))
    kernel_total, bias_total = lax.psum((kernel_local, bias_local), ("tile", "clip"))
    grad_scale = 1.0 / math.sqrt(lax.axis_size("clip") * lax.axis_size("tile") * pixels)
    weight_grad = (kernel_total * grad_scale).reshape(conv_weight.shape[0], 9, colours, channels)
    bias_grad = bias_total * grad_scale
    return (decoded, feature_grad, weight_grad, bias_grad)


def solution(mesh):
    return jax.shard_map(
        per_device,
        mesh=mesh,
        in_specs=(
            P("clip", "tile", None, None, None),
            P(),
            P(),
            P(),
            P("clip", None),
            P("clip", "tile", None, None),
        ),
        out_specs=(P("clip", "tile", None, None), P("clip", "tile", None, None, None), P(), P()),
        check_vma=False,
    )
```

profile of v0, /device:TPU:1, one launch (start us, length us, event | category | flops | bytes accessed | tf_op | source)
XLA Modules:
  0.0 295.1 jit_solution(15663109818594018392)
XLA Ops:
  7.2 0.7 all-gather.6.cloned.1.call-update
  8.0 4.5 %copy.34 = bf16[1,1,96,3,4096]{2,4,3,1,0:T(8,128)(2,1)} copy(bf16[1,1,96,3,4096]{4,2,3,1,0:T(8,128)(2,1)} %param.6) | data formatting | bytes 4718592 | tf_op args[0]
  12.6 0.6 copy-done.3
  13.1 4.0 %fusion.5 = f32[3,3,3,64,64]{4,2,3,1,0:T(4,128)S(1)} fusion(bf16[64,64,96,3,1,1]{2,1,0,3,5,4:T(8,128)(2,1)} %bitcast.182, bf16[3,3,3,96,3]{3,2,1,0,4:T(4,128)(2,1)S(1)} %dot_general.22), kind=kOutput, calls=%fused_computation.6 | convolution fusion | flops 63700992 | bytes 2817216 | tf_op jit(solution)/shard_map/tjc,ctp->jp/dot_general | solution.py:76
  17.2 0.5 pad_slice_fusion.7
  17.7 0.1 squeeze.90
  17.8 0.1 squeeze.89
  18.0 0.1 squeeze.88
  18.1 0.1 squeeze.87
  18.2 0.1 squeeze.86
  18.4 0.1 squeeze.85
  18.5 0.1 squeeze.84
  18.6 0.1 squeeze.83
  18.8 0.1 squeeze.82
  18.9 0.2 add_convert_fusion
  19.1 0.6 copy.46
  19.8 0.6 constant_dynamic-slice_fusion.16
  23.1 0.8 fusion.16
  33.8 0.7 reshape.284
  39.6 0.2 convolution_bitcast_fusion
  39.9 0.7 pad_multiply_fusion
  40.6 0.7 pad_multiply_fusion.1
  41.4 0.7 multiply_divide_fusion
  42.1 59.6 %all-gather.6.cloned.1.call-done = bf16[128,1,3,4096]{3,2,1,0:T(4,128)(2,1)} async-done(((bf16[1,1,3,4096]{3,2,1,0:T(4,128)(2,1)}), bf16[128,1,3,4096]{3,2,1,0:T(4,128)(2,1)}) %all-gather.6.cloned.1.call-update) | async-done | bytes 3145744 | tf_op jit(solution)/shard_map/all_gather | solution.py:91
  101.8 1.0 constant_dynamic-slice_fusion.7
  102.7 0.1 reshape.280
  102.8 0.6 slice.214
  103.6 0.6 slice.213
  104.2 0.1 reshape.278
  104.3 0.7 slice.212
  104.9 0.7 reshape.277
  105.8 0.7 slice.210
  106.6 0.6 slice.209
  107.3 0.6 slice.208
  107.9 0.7 reshape.273
  108.6 1.0 slice.207
  109.6 1.3 convert_reduce_fusion
  110.8 0.7 bitcast_dynamic-update-slice_fusion.8
  111.6 0.6 bitcast_dynamic-update-slice_fusion.7
  112.2 0.7 bitcast_dynamic-update-slice_fusion.6
  112.9 0.7 bitcast_dynamic-update-slice_fusion.5
  113.6 0.6 bitcast_dynamic-update-slice_fusion.4
  114.2 0.7 bitcast_dynamic-update-slice_fusion.3
  114.9 0.7 bitcast_dynamic-update-slice_fusion.2
  115.7 0.6 bitcast_dynamic-update-slice_fusion.1
  116.3 0.7 bitcast_dynamic-update-slice_fusion
  117.0 2.1 reshape.307
  119.1 3.2 %fusion = bf16[1,1,96,3,4096]{4,2,3,1,0:T(8,128)(2,1)} fusion(bf16[27,4096,1]{1,0,2:T(8,128)(2,1)} %reshape.307, bf16[3,27,96]{2,1,0:T(8,128)(2,1)} %copy-done.3), kind=kOutput, calls=%fused_computation.1 | convolution fusion | flops 64880640 | bytes 2596032 | tf_op jit(solution)/shard_map/tjc,jp->ctp/dot_general | solution.py:123
  122.3 1.5 fusion.8
  123.8 62.6 %all-gather.4.cloned.1.call-done = bf16[128,3,4096]{2,1,0:T(4,128)(2,1)} async-done(((bf16[1,3,4096]{2,1,0:T(4,128)(2,1)}), bf16[128,3,4096]{2,1,0:T(4,128)(2,1)}) %all-gather.4.cloned.1.call-update) | async-done | bytes 3145744 | tf_op jit(solution)/shard_map/all_gather | solution.py:88
  186.4 1.0 constant_dynamic-slice_fusion.15
  187.4 0.1 reshape.271
  187.5 0.1 reshape.270
  187.6 0.1 reshape.269
  187.9 0.1 reshape.268
  188.0 0.1 reshape.267
  188.3 0.1 reshape.266
  188.4 0.1 reshape.265
  188.5 0.1 reshape.264
  188.7 1.5 fusion.12
  190.3 0.7 reshape.272
  191.0 96.1 %all-reduce.26 = (f32[3,27,96]{2,1,0:T(8,128)S(1)}, f32[3]{0:T(128)S(1)}) all-reduce(f32[3,27,96]{2,1,0:T(8,128)S(1)} %copy-done.4, f32[3]{0:T(128)S(1)} %get-tuple-element.14), channel_id=1, replica_groups=mesh['tile'=128,'clip'=4] {'tile','clip'}, use_global_device_ids=true, to_apply=%region_8.9 | all-reduce | flops 7779 | bytes 62232 | tf_op jit(solution)/shard_map/psum | solution.py:127
  287.1 0.6 reshape.283
  287.7 0.5 broadcast_multiply_fusion.2
  (59 shorter events, 1.4 us)
Async XLA Ops:
  7.2 94.6 %all-gather.6.cloned.1.call-start = ((), (), s32[]{:S(2)}) async-start(), calls=%async_computation.1 | async-start | bytes 4227072 | tf_op jit(solution)/shard_map/all_gather | solution.py:91
  7.9 4.6 %copy-start.6 = (bf16[3,9,3,96]{3,2,1,0:T(4,128)(2,1)S(1)}, bf16[3,9,3,96]{3,2,1,0:T(4,128)(2,1)}, u32[]{:S(2)}) copy-start(bf16[3,9,3,96]{3,2,1,0:T(4,128)(2,1)} %param.7) | copy-start | bytes 46660
  7.9 178.5 %all-gather.4.cloned.1.call-start = ((), (), s32[]{:S(2)}) async-start(), calls=%async_computation | async-start | bytes 4227072 | tf_op jit(solution)/shard_map/all_gather | solution.py:88
  12.5 0.6 copy-start.3
  17.1 1.7 copy-start.7
  17.6 2.2 copy-start.8
  17.7 16.2 %copy-start.5 = (bf16[1,1,3,4096]{3,2,1,0:T(4,128)(2,1)S(1)}, bf16[1,1,3,4096]{3,2,1,0:T(4,128)(2,1)}, u32[]{:S(2)}) copy-start(bf16[1,1,3,4096]{3,2,1,0:T(4,128)(2,1)} %param.11) | copy-start | bytes 73732
  17.7 21.9 %copy-start.9 = (s32[32]{0:T(128)S(1)}, s32[32]{0:T(128)}, u32[]{:S(2)}) copy-start(s32[32]{0:T(128)} %param.9) | copy-start | bytes 388
  39.9 1.4 copy-start.2
  108.6 13.7 %copy-start = (bf16[1,1,96,3,4096]{4,2,3,1,0:T(8,128)(2,1)S(1)}, bf16[1,1,96,3,4096]{4,2,3,1,0:T(8,128)(2,1)}, u32[]{:S(2)}) copy-start(bf16[1,1,96,3,4096]{4,2,3,1,0:T(8,128)(2,1)} %param.6) | copy-start | bytes 7077892
  119.1 3.3 %copy-start.1 = (bf16[27,4096,1]{1,0,2:T(8,128)(2,1)S(1)}, bf16[27,4096,1]{1,0,2:T(8,128)(2,1)}, u32[]{:S(2)}) copy-start(bf16[27,4096,1]{1,0,2:T(8,128)(2,1)} %reshape.307) | copy-start | bytes 663556
  123.8 67.2 %copy-start.4 = (f32[3,27,96]{2,1,0:T(8,128)S(1)}, f32[3,27,96]{2,1,0:T(8,128)}, u32[]{:S(2)}) copy-start(f32[3,27,96]{2,1,0:T(8,128)} %fusion.8) | copy-start | bytes 93316
Sparse Core Ops, SparseCore 0:
  11.1 90.5 all-gather.5
  104.9 81.4 all-gather.3
where the time goes:
time: 296 us; the launch traced here: 295 us
  waiting for transfers between devices  123 us (42%)
  blocking collectives  96.1 us (32%)
  between operations  32 us (11%)
  local copies, waits for them, and re-layouts  28.5 us (10%)
  matrix products  8.93 us (3%)
  other arithmetic  6.52 us (2%)
    psum x1, blocking collectives, per_device(): lax.psum((kernel_local, bias_local), ('tile', 'clip'))  96.1 us
    all_gather x1, waiting for transfers between devices, per_device(): lax.all_gather(tile_image.reshape(1, colours, pixels), 'tile', axis=0, ti...  62.6 us
    all_gather x1, waiting for transfers between devices, per_device(): lax.all_gather(cotangent.reshape(1, colours, pixels), 'tile', axis=0, til...  59.6 us
    unnamed x37, local copies, waits for them, and re-layouts  10.8 us
  transfers between devices with their start and end apart: 2, of which 2 were waited for; matrix products, arithmetic and copies ran while one was open for 13% of the time, Pallas kernels for 0%

commit v1 on v0

v1 whole, which is shorter than its diff:
```python
import functools
import math

import jax
import jax.numpy as jnp
from jax import lax
from jax.experimental import pallas as pl
from jax.experimental.pallas import tpu as pltpu
from jax.sharding import PartitionSpec as P

EDGE = 64
OV = 32
PIX = EDGE * EDGE
SLOTS = 128
TX = 16
TY = SLOTS // TX
CH = 96
RGB = 3
TIN = 3
LANES = 128
ROWS = PIX // LANES
BOTH = 2 * SLOTS


f32 = jnp.float32
bf16 = jnp.bfloat16


def iota(shape, dim):
    return lax.broadcasted_iota(jnp.int32, shape, dim)


def lane_of_row():
    row = iota((LANES, LANES), 0)
    lane = iota((LANES, LANES), 1)
    target = (row // 64) * 64 + (row % 2) * 32 + (row // 2) % 32
    return (lane == target).astype(f32).astype(bf16)


def rows_of_half(rh):
    return [qy * 16 + rh * 8 + r8 for qy in range(2) for r8 in range(8)]


def pack_half(pieces):
    block = jnp.concatenate(pieces, axis=0).astype(bf16)
    return lax.dot_general(lane_of_row(), block, (((1,), (1,)), ((), ())), preferred_element_type=f32)


def unpack_half(block):
    return lax.dot_general(block, lane_of_row(), (((0,), (0,)), ((), ())), preferred_element_type=f32)


def shift_lanes(value, amount):
    size = value.shape[1]
    amount = amount % size
    return value if amount == 0 else pltpu.roll(value, size - amount, 1)


def profile_at(index, profile_ref):
    out = jnp.zeros(index.shape, f32)
    for m in range(OV):
        out = jnp.where(index == m, profile_ref[m].astype(f32), out)
    return out


def blend_parts(ids_ref, profile_ref, own):
    ids = ids_ref[...].astype(f32)
    slot_row = iota((BOTH, SLOTS), 0) // 2
    spread = slot_row == iota((BOTH, SLOTS), 1)
    id_col = jnp.sum(jnp.where(spread, jnp.broadcast_to(ids, (BOTH, SLOTS)), 0.0), axis=1, keepdims=True)
    onehot = (iota((SLOTS, BOTH), 1) // 2 == iota((SLOTS, BOTH), 0)).astype(f32).astype(bf16)
    id_row = jnp.dot(
        jnp.broadcast_to(ids, (8, SLOTS)).astype(bf16), onehot, preferred_element_type=f32
    )[0:1]
    qx_col = iota((BOTH, 1), 0) % 2
    side = (2 * qx_col - 1).astype(f32)
    tile_row = jnp.floor(id_col * (1.0 / TX))
    tile_col = id_col - tile_row * TX
    to_edge = jnp.where(qx_col == 1, TX - 1.0 - tile_col, tile_col)
    col_there = jnp.minimum(to_edge, 1.0)
    beside = jnp.where(to_edge > 0.5, id_col + side, 999.0)
    same = (iota((BOTH, BOTH), 0) - iota((BOTH, BOTH), 1)) % 2 == 0
    gap = id_row - jnp.where(same, id_col, beside)
    mats = [(gap == step).astype(f32).astype(bf16) for step in (0.0, -float(TX), float(TX))]
    rh = own // 64
    par = (own // 32) % 2
    rx = own % 32
    lane = iota((1, LANES), 1)
    lower = lane >= 64
    ry = 2 * (8 * rh + (lane // 8) % 8) + par
    fy = profile_at(jnp.where(lower, OV - 1 - ry, ry), profile_ref)
    fy_other = pltpu.roll(jnp.broadcast_to(fy, (8, LANES)), 64, 1)[0:1]
    left = profile_ref[rx].astype(f32)
    right = profile_ref[OV - 1 - rx].astype(f32)
    fx = jnp.where(qx_col == 0, left, right)
    fx_other = jnp.where(qx_col == 0, right, left)
    row_there = jnp.minimum(jnp.where(lower, TY - 1.0 - tile_row, tile_row), 1.0)
    weight = fx * fy
    coverage = (fx + col_there * fx_other) * (fy + row_there * fy_other)
    return mats, weight, coverage


def overlap_sum(mats, parts):
    total = []
    for mat in mats:
        got = jnp.dot(mat, parts[0], preferred_element_type=f32)
        for part in parts[1:]:
            got = got + jnp.dot(mat, part, preferred_element_type=f32)
        total.append(got)
    lower = iota((BOTH, LANES), 1) >= 64
    return total[0] + pltpu.roll(jnp.where(lower, total[1], total[2]), 64, 1)


def slot_of_lane(shape):
    return iota(shape, 1) % 8


def pack_grads_kernel(grad_ref, out_ref, held):
    held[...] = jnp.zeros_like(held)
    held[0:RGB, :] = grad_ref[...].astype(f32)
    for rh in range(2):
        pieces = [held[:, r * LANES : (r + 1) * LANES] for r in rows_of_half(rh)]
        out_ref[rh * LANES : (rh + 1) * LANES, :] = pack_half(pieces).astype(bf16)


def conv_kernel(chunk, feat_ref, weight_ref, bias_ref, out_ref, taps):
    step = pl.program_id(0)
    total = jnp.zeros((72, chunk), f32)
    for t in range(TIN):
        total += jnp.dot(weight_ref[t], feat_ref[t], preferred_element_type=f32)
    taps[:, pl.ds(pl.multiple_of(step * chunk, chunk), chunk)] = total

    @pl.when(step == pl.num_programs(0) - 1)
    def _():
        lane = iota((8, PIX), 1)
        image = jnp.zeros((8, PIX), f32)
        for kx in range(3):
            column = jnp.zeros((8, PIX), f32)
            for ky in range(3):
                tap = 3 * ky + kx
                moved = shift_lanes(taps[tap * 8 : tap * 8 + 8, :], (ky - 1) * EDGE)
                if ky == 0:
                    moved = jnp.where(lane >= EDGE, moved, 0.0)
                elif ky == 2:
                    moved = jnp.where(lane < PIX - EDGE, moved, 0.0)
                column = column + moved
            moved = shift_lanes(column, kx - 1)
            if kx == 0:
                moved = jnp.where(lane % EDGE != 0, moved, 0.0)
            elif kx == 2:
                moved = jnp.where(lane % EDGE != EDGE - 1, moved, 0.0)
            image = image + moved
        row = iota((8, 1), 0)
        shift = jnp.zeros((8, 1), f32)
        for o in range(RGB):
            shift = jnp.where(row == o, bias_ref[o], shift)
        image = pltpu.roll(image + shift, RGB, 0)
        for rh in range(2):
            pieces = [image[:, r * LANES : (r + 1) * LANES] for r in rows_of_half(rh)]
            out_ref[rh * LANES : (rh + 1) * LANES, :] = pack_half(pieces).astype(bf16)


def blend_grads_kernel(got_ref, image_ref, ids_ref, profile_ref, own_ref, out_ref):
    mats, weight, coverage = blend_parts(ids_ref, profile_ref, own_ref[0])
    summed = overlap_sum(mats, [got_ref[...]])
    grads = weight / coverage * summed
    slot = slot_of_lane((BOTH, LANES))
    out_ref[...] = jnp.where(slot < RGB, grads, image_ref[...].astype(f32)).astype(bf16)


def grad_stack(grad, taps):
    lane = iota((8, PIX), 1)
    for kx in range(3):
        moved_x = shift_lanes(grad, 1 - kx)
        if kx == 0:
            moved_x = jnp.where(lane % EDGE != EDGE - 1, moved_x, 0.0)
        elif kx == 2:
            moved_x = jnp.where(lane % EDGE != 0, moved_x, 0.0)
        for ky in range(3):
            moved = shift_lanes(moved_x, (1 - ky) * EDGE)
            if ky == 0:
                moved = jnp.where(lane < PIX - EDGE, moved, 0.0)
            elif ky == 2:
                moved = jnp.where(lane >= EDGE, moved, 0.0)
            tap = 3 * ky + kx
            taps[tap * 8 : tap * 8 + 8, :] = moved


def weight_grad_kernel(chunk, got_ref, feat_ref, out_ref, grad_ref, feats, taps, sem):
    copy = pltpu.make_async_copy(feat_ref, feats, sem)
    copy.start()
    row = iota((8, LANES), 0)
    for rh in range(2):
        block = unpack_half(got_ref[rh * LANES : (rh + 1) * LANES, :])
        for n, r in enumerate(rows_of_half(rh)):
            piece = block[n * 8 : n * 8 + 8, :]
            grad_ref[:, r * LANES : (r + 1) * LANES] = jnp.where(row < RGB, piece, 0.0)
    grad = grad_ref[...]
    grad_stack(grad, taps)
    bias = lax.dot_general(
        jnp.ones((8, PIX), bf16), grad.astype(bf16), (((1,), (1,)), ((), ())), preferred_element_type=f32
    )
    copy.wait()
    sums = [jnp.zeros((CH, 72), f32) for _ in range(TIN)]
    for at in range(0, PIX, chunk):
        part = taps[:, at : at + chunk].astype(bf16)
        for t in range(TIN):
            sums[t] += lax.dot_general(
                feats[t, :, at : at + chunk], part, (((1,), (1,)), ((), ())), preferred_element_type=f32
            )
    rows = []
    side = jnp.zeros((8, LANES - CH), f32)
    for t in range(TIN):
        turned = sums[t].T
        for tap in range(9):
            rows.append(jnp.concatenate([turned[tap * 8 : tap * 8 + 8, :], side], axis=1))
    rows.append(jnp.concatenate([bias, jnp.zeros((8, LANES - 8), f32)], axis=1))
    while len(rows) < ROWS:
        rows.append(jnp.zeros((8, LANES), f32))
    for rh in range(2):
        pieces = [rows[r] for r in rows_of_half(rh)]
        out_ref[rh * LANES : (rh + 1) * LANES, :] = pack_half(pieces).astype(bf16)


def feature_grad_kernel(chunk, grad_ref, weight_ref, out_ref, taps):
    step = pl.program_id(0)

    @pl.when(step == 0)
    def _():
        grad_stack(grad_ref[...], taps)

    part = taps[:, pl.ds(pl.multiple_of(step * chunk, chunk), chunk)].astype(bf16)
    for t in range(TIN):
        out_ref[t] = lax.dot_general(
            weight_ref[t], part, (((0,), (0,)), ((), ())), preferred_element_type=f32
        ).astype(bf16)


def blend_images_kernel(got_ref, ids_ref, profile_ref, own_ref, out_ref):
    mats, weight, coverage = blend_parts(ids_ref, profile_ref, own_ref[0])
    slot = slot_of_lane((BOTH, LANES))
    weighted = weight * jnp.where(slot >= RGB, got_ref[...].astype(f32), 0.0)
    high = weighted.astype(bf16)
    low = (weighted - high.astype(f32)).astype(bf16)
    out_ref[...] = (overlap_sum(mats, [high, low]) / coverage).astype(bf16)


def sum_tiles_kernel(got_ref, out_ref):
    pick = (iota((8, BOTH), 0) == iota((8, BOTH), 1) % 2).astype(f32).astype(bf16)
    total = jnp.dot(pick, got_ref[...], preferred_element_type=f32)
    for c in range(4):
        out_ref[c] = total


def spread_kernel(got_ref, image_ref, out_ref):
    total = got_ref[0] + got_ref[1] + got_ref[2] + got_ref[3]
    even = iota((BOTH, LANES), 0) % 2 == 0
    both = jnp.where(even, total[0:1], total[1:2])
    slot = slot_of_lane((BOTH, LANES))
    out_ref[...] = jnp.where(slot < RGB, both, image_ref[...].astype(f32)).astype(bf16)


def finish_kernel(scale, got_ref, weight_ref, bias_ref, image_ref):
    for rh in range(2):
        block = unpack_half(got_ref[rh * LANES : (rh + 1) * LANES, :])
        for n, r in enumerate(rows_of_half(rh)):
            piece = block[n * 8 : n * 8 + 8, :]
            image_ref[:, r * LANES : (r + 1) * LANES] = piece[RGB : 2 * RGB].astype(bf16)
            if r < 9 * TIN:
                weight_ref[r // 9, r % 9] = piece[0:RGB, 0:CH] * scale
            elif r == 9 * TIN:
                bias_ref[...] = piece[0:1, 0:RGB] * scale


VM = pl.BlockSpec(memory_space=pltpu.VMEM)
SM = pl.BlockSpec(memory_space=pltpu.SMEM)
ANY = pl.BlockSpec(memory_space=pl.ANY)
LIMIT = 40 * 1024 * 1024
message = jax.ShapeDtypeStruct((BOTH, LANES), bf16)


def cost(flops, size):
    return pl.CostEstimate(flops=flops, bytes_accessed=size, transcendentals=0)


def params():
    return pltpu.CompilerParams(vmem_limit_bytes=LIMIT)


def exchange(rows, axis):
    return lax.all_to_all(rows, axis, 0, 0, tiled=True)


def exchange_tiles(rows):
    return exchange(rows.reshape(SLOTS, 2, LANES), "tile").reshape(BOTH, LANES)


def per_device(features, conv_weight, bias, blend_profile, tile_ids, reward_grad):
    chunk = 1024
    own = lax.axis_index("tile").reshape(1).astype(jnp.int32)
    feats = jnp.transpose(features[0, 0], (1, 0, 2))
    weights = jnp.pad(conv_weight, ((0, 0), (0, 0), (0, 8 - RGB), (0, 0))).reshape(TIN, 72, CH)

    grads_out = pl.pallas_call(
        pack_grads_kernel,
        out_shape=message,
        in_specs=[VM],
        out_specs=VM,
        scratch_shapes=[pltpu.VMEM((8, PIX), f32)],
        compiler_params=params(),
        cost_estimate=cost(1 << 20, 1 << 17),
        name="pack_grads",
    )(reward_grad[0, 0])
    grads_got = exchange_tiles(grads_out)

    images_out = pl.pallas_call(
        functools.partial(conv_kernel, chunk),
        out_shape=message,
        grid=(PIX // chunk,),
        in_specs=[
            pl.BlockSpec((TIN, CH, chunk), lambda i: (0, 0, i)),
            pl.BlockSpec((TIN, 72, CH), lambda i: (0, 0, 0)),
            SM,
        ],
        out_specs=pl.BlockSpec((BOTH, LANES), lambda i: (0, 0)),
        scratch_shapes=[pltpu.VMEM((72, PIX), f32)],
        compiler_params=params(),
        cost_estimate=cost(2 * 72 * 288 * PIX, 1 << 22),
        name="conv",
    )(feats, weights, bias)

    back_out = pl.pallas_call(
        blend_grads_kernel,
        out_shape=message,
        in_specs=[VM, VM, VM, SM, SM],
        out_specs=VM,
        compiler_params=params(),
        cost_estimate=cost(1 << 26, 1 << 18),
        name="blend_grads",
    )(grads_got, images_out, tile_ids, blend_profile, own)
    back_got = exchange_tiles(back_out)

    weight_out, grad_rows = pl.pallas_call(
        functools.partial(weight_grad_kernel, chunk),
        out_shape=(message, jax.ShapeDtypeStruct((8, PIX), f32)),
        in_specs=[VM, ANY],
        out_specs=(VM, VM),
        scratch_shapes=[
            pltpu.VMEM((TIN, CH, PIX), bf16),
            pltpu.VMEM((72, PIX), f32),
            pltpu.SemaphoreType.DMA,
        ],
        compiler_params=params(),
        cost_estimate=cost(2 * 72 * 288 * PIX, 1 << 22),
        name="weight_grad",
    )(back_got, feats)
    weight_got = exchange_tiles(weight_out)

    feature_rows = pl.pallas_call(
        functools.partial(feature_grad_kernel, chunk),
        out_shape=jax.ShapeDtypeStruct((TIN, CH, PIX), bf16),
        grid=(PIX // chunk,),
        in_specs=[
            pl.BlockSpec((8, PIX), lambda i: (0, 0)),
            pl.BlockSpec((TIN, 72, CH), lambda i: (0, 0, 0)),
        ],
        out_specs=pl.BlockSpec((TIN, CH, chunk), lambda i: (0, 0, i)),
        scratch_shapes=[pltpu.VMEM((72, PIX), f32)],
        compiler_params=params(),
        cost_estimate=cost(2 * 72 * 288 * PIX, 1 << 22),
        name="feature_grad",
    )(grad_rows, weights)
    feature_grad = jnp.transpose(feature_rows, (1, 0, 2))[None, None]

    blended = pl.pallas_call(
        blend_images_kernel,
        out_shape=message,
        in_specs=[VM, VM, SM, SM],
        out_specs=VM,
        compiler_params=params(),
        cost_estimate=cost(1 << 27, 1 << 18),
        name="blend_images",
    )(back_got, tile_ids, blend_profile, own)

    tile_sum = pl.pallas_call(
        sum_tiles_kernel,
        out_shape=jax.ShapeDtypeStruct((4, 8, LANES), f32),
        in_specs=[VM],
        out_specs=VM,
        compiler_params=params(),
        cost_estimate=cost(1 << 20, 1 << 17),
        name="sum_tiles",
    )(weight_got)
    clip_got = exchange(tile_sum, "clip")

    spread_out = pl.pallas_call(
        spread_kernel,
        out_shape=message,
        in_specs=[VM, VM],
        out_specs=VM,
        compiler_params=params(),
        cost_estimate=cost(1 << 20, 1 << 17),
        name="spread",
    )(clip_got, blended)
    spread_got = exchange_tiles(spread_out)

    scale = 1.0 / math.sqrt(lax.axis_size("clip") * lax.axis_size("tile") * PIX)
    weight_grad, bias_grad, decoded = pl.pallas_call(
        functools.partial(finish_kernel, scale),
        out_shape=(
            jax.ShapeDtypeStruct((TIN, 9, RGB, CH), f32),
            jax.ShapeDtypeStruct((1, RGB), f32),
            jax.ShapeDtypeStruct((RGB, PIX), bf16),
        ),
        in_specs=[VM],
        out_specs=(VM, VM, VM),
        compiler_params=params(),
        cost_estimate=cost(1 << 20, 1 << 17),
        name="finish",
    )(spread_got)
    return (decoded[None, None], feature_grad, weight_grad, bias_grad.reshape(RGB))


def solution(mesh):
    return jax.shard_map(
        per_device,
        mesh=mesh,
        in_specs=(
            P("clip", "tile", None, None, None),
            P(),
            P(),
            P(),
            P("clip", None),
            P("clip", "tile", None, None),
        ),
        out_specs=(P("clip", "tile", None, None), P("clip", "tile", None, None, None), P(), P()),
        check_vma=False,
    )
```

time: 296 us -> 100 us (0.34)
  waiting for transfers between devices: 123 us -> 17.6 us
  blocking collectives: 96.1 us -> 35.8 us
  between operations: 32 us -> 0.72 us
  starting transfers between devices: 0.08 us -> 29.5 us
  local copies, waits for them, and re-layouts: 28.5 us -> 3.86 us
  Pallas kernels: 0 us -> 12.3 us
  matrix products: 8.93 us -> 0 us
  other arithmetic: 6.52 us -> 0 us
    all_gather x2 -> x0, waiting for transfers between devices: 122 us -> none  [the longest x1 62.6 us: per_device(): lax.all_gather(tile_image.reshape(1, colours, pixels), 'tile', axis=0, ti...]
    psum x1 -> x0, blocking collectives: 96.1 us -> none  [per_device(): lax.psum((kernel_local, bias_local), ('tile', 'clip'))]
    all_to_all x0 -> x2, blocking collectives: none -> 35.8 us  [exchange(): return lax.all_to_all(rows, axis, 0, 0, tiled=True)]
    all_to_all x0 -> x3, starting transfers between devices: none -> 29.5 us  [exchange(): return lax.all_to_all(rows, axis, 0, 0, tiled=True)]
    all_to_all x0 -> x3, waiting for transfers between devices: none -> 17.6 us  [exchange(): return lax.all_to_all(rows, axis, 0, 0, tiled=True)]
    pallas_call x0 -> x9, Pallas kernels: none -> 12.3 us  [the longest x1 2.97 us: per_device(): pl.pallas_call(functools.partial(feature_grad_kernel, chunk), out_shape=j...]
    dot_general x4 -> x0, matrix products: 8.93 us -> none  [the longest x1 4.01 us: per_device(): jnp.einsum('tjc,ctp->jp', kernel, frames, preferred_element_type=jnp.floa...]
    unnamed x37 -> x12, local copies, waits for them, and re-layouts: 10.8 us -> 3.09 us
  transfers between devices with their start and end apart: 2 -> 3, of which waited for: 2 -> 3; matrix products, arithmetic and copies ran while one was open for 13% -> 1% of each run, Pallas kernels for 0% -> 7%
where the time goes in v1:
time: 100 us; the launch traced here: 99.8 us
  blocking collectives  35.8 us (36%)
  starting transfers between devices  29.5 us (30%)
  waiting for transfers between devices  17.6 us (18%)
  Pallas kernels  12.3 us (12%)
  local copies, waits for them, and re-layouts  3.86 us (4%)
    all_to_all x2, blocking collectives, exchange(): return lax.all_to_all(rows, axis, 0, 0, tiled=True)  35.8 us
    all_to_all x3, starting transfers between devices, exchange(): return lax.all_to_all(rows, axis, 0, 0, tiled=True)  29.5 us
    all_to_all x3, waiting for transfers between devices, exchange(): return lax.all_to_all(rows, axis, 0, 0, tiled=True)  17.6 us
    unnamed x12, local copies, waits for them, and re-layouts  3.09 us
    pallas_call x1, Pallas kernels, per_device(): pl.pallas_call(functools.partial(feature_grad_kernel, chunk), out_shape=j...  2.97 us
    pallas_call x1, Pallas kernels, per_device(): pl.pallas_call(functools.partial(conv_kernel, chunk), out_shape=message,...  2.3 us
  transfers between devices with their start and end apart: 3, of which 3 were waited for; matrix products, arithmetic and copies ran while one was open for 1% of the time, Pallas kernels for 7%

profile of v1, /device:TPU:1, one launch (start us, length us, event | category | flops | bytes accessed | tf_op | source)
XLA Modules:
  0.0 99.8 jit_solution(10456099967809011275)
XLA Ops:
  0.6 0.0 copy-start.4
  0.6 0.0 copy-start.5
  0.7 0.0 copy-start.2
  0.7 0.8 copy-done.2
  1.4 0.8 pack_grads.1
  2.2 18.4 %all-to-all-start = ((bf16[128,2,128]{2,1,0:T(2,128)(2,1)}), bf16[128,2,128]{2,1,0:T(2,128)(2,1)S(1)}, u32[]{:S(2)}, u32[]{:S(2)}) async-start(bf16[128,2,128]{2,1,0:T(2,128)(2,1)} %bitcast.1), calls=%async_computation | async-start | bytes 131072 | tf_op jit(solution)/shard_map/all_to_all | solution.py:291
  20.7 0.8 pad_bitcast_fusion.weight_ref
  21.4 0.0 copy-start
  21.5 1.7 %copy-done = bf16[1,1,96,3,4096]{4,2,3,1,0:T(8,128)(2,1)S(1)} copy-done((bf16[1,1,96,3,4096]{4,2,3,1,0:T(8,128)(2,1)S(1)}, bf16[1,1,96,3,4096]{4,2,3,1,0:T(8,128)(2,1)}, u32[]{:S(2)}) %copy-start) | copy-done | bytes 2359320
  23.1 0.0 copy-start.3
  23.1 0.7 copy-done.3
  23.8 0.0 copy-start.1
  23.8 2.3 %conv.1.image_ref = bf16[256,128]{1,0:T(8,128)(2,1)S(1)} custom-call(bf16[3,96,4096]{2,1,0:T(8,128)(2,1)S(1)} %bitcast.20, bf16[3,72,96]{2,1,0:T(8,128)(2,1)S(1)} %pad_bitcast_fusion.weight_ref, f32[3]{0:T(128)S(1)} %copy-done.3), custom_call_target="tpu_custom_call" | custom-call | flops 169869312 | bytes 4194304 | tf_op jit(solution)/shard_map/conv/pallas_call | solution.py:316
  26.1 6.0 %all-to-all-done = bf16[128,2,128]{2,1,0:T(2,128)(2,1)S(1)} async-done(((bf16[128,2,128]{2,1,0:T(2,128)(2,1)}), bf16[128,2,128]{2,1,0:T(2,128)(2,1)S(1)}, u32[]{:S(2)}, u32[]{:S(2)}) %all-to-all-start) | async-done | bytes 65568 | tf_op jit(solution)/shard_map/all_to_all | solution.py:291
  32.1 0.0 copy-done.4
  32.1 0.0 copy-done.5
  32.1 1.1 %blend_grads.1 = bf16[256,128]{1,0:T(8,128)(2,1)S(1)} custom-call(bf16[256,128]{1,0:T(8,128)(2,1)S(1)} %bitcast.26, bf16[256,128]{1,0:T(8,128)(2,1)S(1)} %conv.1.image_ref, s32[1,128]{1,0:T(1,128)S(1)} %copy-done.4, s32[32]{0:T(128)S(1)} %copy-done.5, s32[1]{0:T(128)} %bitcast.6.own_ref), custom_call_target="tpu_custom_call" | custom-call | flops 67108864 | bytes 262144 | tf_op jit(solution)/shard_map/blend_grads/pallas_call | solution.py:332
  33.2 19.0 %all_to_all.25 = bf16[128,2,128]{2,1,0:T(2,128)(2,1)S(1)} all-to-all(bf16[128,2,128]{2,1,0:T(2,128)(2,1)S(1)} %bitcast.27), channel_id=1, replica_groups=mesh['tile'=128,'clip'=4] {'tile'}, dimensions={0} | all-to-all | bytes 131072 | tf_op jit(solution)/shard_map/all_to_all | solution.py:291
  52.2 0.0 copy-done.1
  52.2 1.6 %weight_grad.1 = (bf16[256,128]{1,0:T(8,128)(2,1)S(1)}, f32[8,4096]{1,0:T(8,128)S(1)}) custom-call(bf16[256,128]{1,0:T(8,128)(2,1)S(1)} %bitcast.22, bf16[3,96,4096]{2,1,0:T(8,128)(2,1)S(1)} %bitcast.21), custom_call_target="tpu_custom_call" | custom-call | flops 169869312 | bytes 4194304 | tf_op jit(solution)/shard_map/weight_grad/pallas_call | solution.py:343
  53.9 16.8 %all_to_all.26 = bf16[128,2,128]{2,1,0:T(2,128)(2,1)S(1)} all-to-all(bf16[128,2,128]{2,1,0:T(2,128)(2,1)S(1)} %bitcast.28), channel_id=1, replica_groups=mesh['tile'=128,'clip'=4] {'tile'}, dimensions={0} | all-to-all | bytes 131072 | tf_op jit(solution)/shard_map/all_to_all | solution.py:291
  70.6 0.7 sum_tiles.1
  71.4 4.0 %all-to-all-start.3 = ((f32[4,8,128]{2,1,0:T(8,128)}), f32[4,8,128]{2,1,0:T(8,128)S(1)}, u32[]{:S(2)}, u32[]{:S(2)}) async-start(f32[4,8,128]{2,1,0:T(8,128)} %sum_tiles.1), calls=%async_computation.3 | async-start | bytes 32768 | tf_op jit(solution)/shard_map/all_to_all | solution.py:291
  75.4 1.3 %blend_images.1.image_ref = bf16[256,128]{1,0:T(8,128)(2,1)S(1)} custom-call(bf16[256,128]{1,0:T(8,128)(2,1)S(1)} %bitcast.23, s32[1,128]{1,0:T(1,128)S(1)} %copy-done.4, s32[32]{0:T(128)S(1)} %copy-done.5, s32[1]{0:T(128)} %bitcast.6.own_ref), custom_call_target="tpu_custom_call" | custom-call | flops 134217728 | bytes 262144 | tf_op jit(solution)/shard_map/blend_images/pallas_call | solution.py:375
  76.6 2.9 %all-to-all-done.3.got_ref = f32[4,8,128]{2,1,0:T(8,128)S(1)} async-done(((f32[4,8,128]{2,1,0:T(8,128)}), f32[4,8,128]{2,1,0:T(8,128)S(1)}, u32[]{:S(2)}, u32[]{:S(2)}) %all-to-all-start.3) | async-done | bytes 16416 | tf_op jit(solution)/shard_map/all_to_all | solution.py:291
  79.6 0.7 spread.1
  80.2 7.1 %all-to-all-start.4 = ((bf16[128,2,128]{2,1,0:T(2,128)(2,1)}), bf16[128,2,128]{2,1,0:T(2,128)(2,1)S(1)}, u32[]{:S(2)}, u32[]{:S(2)}) async-start(bf16[128,2,128]{2,1,0:T(2,128)(2,1)} %bitcast.11), calls=%async_computation.4 | async-start | bytes 131072 | tf_op jit(solution)/shard_map/all_to_all | solution.py:291
  87.3 3.0 %feature_grad.1 = bf16[3,96,4096]{2,1,0:T(8,128)(2,1)} custom-call(f32[8,4096]{1,0:T(8,128)S(1)} %get-tuple-element.11.grad_ref, bf16[3,72,96]{2,1,0:T(8,128)(2,1)S(1)} %pad_bitcast_fusion.weight_ref), custom_call_target="tpu_custom_call" | custom-call | flops 169869312 | bytes 4194304 | tf_op jit(solution)/shard_map/feature_grad/pallas_call | solution.py:359
  90.3 8.6 %all-to-all-done.4 = bf16[128,2,128]{2,1,0:T(2,128)(2,1)S(1)} async-done(((bf16[128,2,128]{2,1,0:T(2,128)(2,1)}), bf16[128,2,128]{2,1,0:T(2,128)(2,1)S(1)}, u32[]{:S(2)}, u32[]{:S(2)}) %all-to-all-start.4) | async-done | bytes 65568 | tf_op jit(solution)/shard_map/all_to_all | solution.py:291
  98.9 0.9 finish.1
Async XLA Ops:
  0.6 31.5 %copy-start.4 = (s32[1,128]{1,0:T(1,128)S(1)}, s32[1,128]{1,0:T(1,128)}, u32[]{:S(2)}) copy-start(s32[1,128]{1,0:T(1,128)} %ids_ref.3) | copy-start | bytes 1540
  0.6 31.5 %copy-start.5 = (s32[32]{0:T(128)S(1)}, s32[32]{0:T(128)}, u32[]{:S(2)}) copy-start(s32[32]{0:T(128)} %profile_ref.3) | copy-start | bytes 388
  0.7 0.8 copy-start.2
  2.2 29.9 %all-to-all-start = ((bf16[128,2,128]{2,1,0:T(2,128)(2,1)}), bf16[128,2,128]{2,1,0:T(2,128)(2,1)S(1)}, u32[]{:S(2)}, u32[]{:S(2)}) async-start(bf16[128,2,128]{2,1,0:T(2,128)(2,1)} %bitcast.1), calls=%async_computation | async-start | bytes 131072 | tf_op jit(solution)/shard_map/all_to_all | solution.py:291
  21.4 1.7 %copy-start = (bf16[1,1,96,3,4096]{4,2,3,1,0:T(8,128)(2,1)S(1)}, bf16[1,1,96,3,4096]{4,2,3,1,0:T(8,128)(2,1)}, u32[]{:S(2)}) copy-start(bf16[1,1,96,3,4096]{4,2,3,1,0:T(8,128)(2,1)} %param.6) | copy-start | bytes 7077892
  23.1 0.7 copy-start.3
  23.8 28.5 %copy-start.1 = (bf16[1,1,96,3,4096]{4,2,3,1,0:T(8,128)(2,1)S(1)}, bf16[1,1,96,3,4096]{4,2,3,1,0:T(8,128)(2,1)}, u32[]{:S(2)}) copy-start(bf16[1,1,96,3,4096]{4,2,3,1,0:T(8,128)(2,1)} %param.6) | copy-start | bytes 7077892
  71.4 8.2 %all-to-all-start.3 = ((f32[4,8,128]{2,1,0:T(8,128)}), f32[4,8,128]{2,1,0:T(8,128)S(1)}, u32[]{:S(2)}, u32[]{:S(2)}) async-start(f32[4,8,128]{2,1,0:T(8,128)} %sum_tiles.1), calls=%async_computation.3 | async-start | bytes 32768 | tf_op jit(solution)/shard_map/all_to_all | solution.py:291
  80.2 18.7 %all-to-all-start.4 = ((bf16[128,2,128]{2,1,0:T(2,128)(2,1)}), bf16[128,2,128]{2,1,0:T(2,128)(2,1)S(1)}, u32[]{:S(2)}, u32[]{:S(2)}) async-start(bf16[128,2,128]{2,1,0:T(2,128)(2,1)} %bitcast.11), calls=%async_computation.4 | async-start | bytes 131072 | tf_op jit(solution)/shard_map/all_to_all | solution.py:291

commit v2 on v1

v2 whole, which is shorter than its diff:
```python
import functools
import math

import jax
import jax.numpy as jnp
from jax import lax
from jax.experimental import pallas as pl
from jax.experimental.pallas import tpu as pltpu
from jax.sharding import Mesh
from jax.sharding import PartitionSpec as P

EDGE = 64
OV = 32
PIX = EDGE * EDGE
SLOTS = 128
TX = 16
TY = SLOTS // TX
CH = 96
RGB = 3
TIN = 3
LANES = 128
ROWS = PIX // LANES
BOTH = 2 * SLOTS
TAPS = 9
STACK = TAPS * 8
HALF = 32
MAIN = 30
BIAS_ROW = 30


f32 = jnp.float32
bf16 = jnp.bfloat16


def iota(shape, dim):
    return lax.broadcasted_iota(jnp.int32, shape, dim)


def lane_of_row():
    row = iota((LANES, LANES), 0)
    lane = iota((LANES, LANES), 1)
    target = (row // 64) * 64 + (row % 2) * 32 + (row // 2) % 32
    return (lane == target).astype(f32).astype(bf16)


def rows_of_half(rh):
    return [qy * 16 + rh * 8 + r8 for qy in range(2) for r8 in range(8)]


def pack_half(pieces):
    block = jnp.concatenate(pieces, axis=0).astype(bf16)
    return lax.dot_general(lane_of_row(), block, (((1,), (1,)), ((), ())), preferred_element_type=f32)


def unpack_half(block):
    return lax.dot_general(block, lane_of_row(), (((0,), (0,)), ((), ())), preferred_element_type=f32)


def shift_lanes(value, amount):
    size = value.shape[1]
    amount = amount % size
    return value if amount == 0 else pltpu.roll(value, size - amount, 1)


def profile_at(index, profile_ref):
    out = jnp.zeros(index.shape, f32)
    for m in range(OV):
        out = jnp.where(index == m, profile_ref[m].astype(f32), out)
    return out


def blend_prep_kernel(ids_ref, profile_ref, own_ref, feat_ref, mats_ref, before_ref, after_ref, held_ref, sem):
    copy = pltpu.make_async_copy(feat_ref, held_ref, sem)
    copy.start()
    own = own_ref[0]
    ids = ids_ref[...].astype(f32)
    slot_row = iota((BOTH, SLOTS), 0) // 2
    spread = slot_row == iota((BOTH, SLOTS), 1)
    id_col = jnp.sum(jnp.where(spread, jnp.broadcast_to(ids, (BOTH, SLOTS)), 0.0), axis=1, keepdims=True)
    onehot = (iota((SLOTS, BOTH), 1) // 2 == iota((SLOTS, BOTH), 0)).astype(f32).astype(bf16)
    id_row = jnp.dot(
        jnp.broadcast_to(ids, (8, SLOTS)).astype(bf16), onehot, preferred_element_type=f32
    )[0:1]
    qx_col = iota((BOTH, 1), 0) % 2
    side = (2 * qx_col - 1).astype(f32)
    tile_row = jnp.floor(id_col * (1.0 / TX))
    tile_col = id_col - tile_row * TX
    to_edge = jnp.where(qx_col == 1, TX - 1.0 - tile_col, tile_col)
    col_there = jnp.minimum(to_edge, 1.0)
    beside = jnp.where(to_edge > 0.5, id_col + side, 999.0)
    same = (iota((BOTH, BOTH), 0) - iota((BOTH, BOTH), 1)) % 2 == 0
    gap = id_row - jnp.where(same, id_col, beside)
    for n, step in enumerate((0.0, -float(TX), float(TX))):
        mats_ref[n * BOTH : (n + 1) * BOTH, :] = (gap == step).astype(f32).astype(bf16)
    rh = own // 64
    par = (own // 32) % 2
    rx = own % 32
    lane = iota((1, LANES), 1)
    lower = lane >= 64
    ry = 2 * (8 * rh + (lane // 8) % 8) + par
    fy = profile_at(jnp.where(lower, OV - 1 - ry, ry), profile_ref)
    fy_other = pltpu.roll(jnp.broadcast_to(fy, (8, LANES)), 64, 1)[0:1]
    left = profile_ref[rx].astype(f32)
    right = profile_ref[OV - 1 - rx].astype(f32)
    fx = jnp.where(qx_col == 0, left, right)
    fx_other = jnp.where(qx_col == 0, right, left)
    row_there = jnp.minimum(jnp.where(lower, TY - 1.0 - tile_row, tile_row), 1.0)
    weight = fx * fy
    coverage = (fx + col_there * fx_other) * (fy + row_there * fy_other)
    grads = iota((BOTH, LANES), 1) % 8 < RGB
    before_ref[...] = jnp.where(grads, 1.0, weight)
    after_ref[...] = jnp.where(grads, weight, 1.0) / coverage
    copy.wait()


def blend_kernel(got_ref, mats_ref, before_ref, after_ref, out_ref):
    source = got_ref[...].astype(f32) * before_ref[...]
    high = source.astype(bf16)
    low = (source - high.astype(f32)).astype(bf16)
    total = []
    for n in range(3):
        mat = mats_ref[n * BOTH : (n + 1) * BOTH, :]
        total.append(
            jnp.dot(mat, high, preferred_element_type=f32) + jnp.dot(mat, low, preferred_element_type=f32)
        )
    lower = iota((BOTH, LANES), 1) >= 64
    summed = total[0] + pltpu.roll(jnp.where(lower, total[1], total[2]), 64, 1)
    out_ref[...] = (summed * after_ref[...]).astype(bf16)


def stack_weights(weight_ref, held):
    held[...] = jnp.zeros_like(held)
    for t in range(TIN):
        for tap in range(TAPS):
            held[t, tap * 8 : tap * 8 + RGB, :] = weight_ref[t, tap].astype(f32)


def conv_kernel(chunk, feat_ref, weight_ref, bias_ref, grad_ref, out_ref, feats, held, taps, sems):
    copies = []
    for n in range(PIX // chunk):
        part = pl.ds(n * chunk, chunk)
        copies.append(pltpu.make_async_copy(feat_ref.at[:, :, part], feats.at[:, :, part], sems.at[n]))
        copies[-1].start()
    stack_weights(weight_ref, held)
    kernels = [held[t].astype(bf16) for t in range(TIN)]
    for n in range(PIX // chunk):
        copies[n].wait()
        total = jnp.zeros((STACK, chunk), f32)
        for t in range(TIN):
            total += jnp.dot(kernels[t], feats[t, :, n * chunk : (n + 1) * chunk], preferred_element_type=f32)
        taps[:, n * chunk : (n + 1) * chunk] = total
    lane = iota((8, PIX), 1)
    image = jnp.zeros((8, PIX), f32)
    for kx in range(3):
        column = jnp.zeros((8, PIX), f32)
        for ky in range(3):
            tap = 3 * ky + kx
            moved = shift_lanes(taps[tap * 8 : tap * 8 + 8, :], (ky - 1) * EDGE)
            if ky == 0:
                moved = jnp.where(lane >= EDGE, moved, 0.0)
            elif ky == 2:
                moved = jnp.where(lane < PIX - EDGE, moved, 0.0)
            column = column + moved
        moved = shift_lanes(column, kx - 1)
        if kx == 0:
            moved = jnp.where(lane % EDGE != 0, moved, 0.0)
        elif kx == 2:
            moved = jnp.where(lane % EDGE != EDGE - 1, moved, 0.0)
        image = image + moved
    row = iota((8, 1), 0)
    shift = jnp.zeros((8, 1), f32)
    for o in range(RGB):
        shift = jnp.where(row == o, bias_ref[o], shift)
    taps[0:8, :] = pltpu.roll(image + shift, RGB, 0)
    taps[0:RGB, :] = grad_ref[...].astype(f32)
    for rh in range(2):
        pieces = [taps[0:8, r * LANES : (r + 1) * LANES] for r in rows_of_half(rh)]
        out_ref[rh * LANES : (rh + 1) * LANES, :] = pack_half(pieces).astype(bf16)


def grad_stack(grad, taps):
    lane = iota((8, PIX), 1)
    for kx in range(3):
        moved_x = shift_lanes(grad, 1 - kx)
        if kx == 0:
            moved_x = jnp.where(lane % EDGE != EDGE - 1, moved_x, 0.0)
        elif kx == 2:
            moved_x = jnp.where(lane % EDGE != 0, moved_x, 0.0)
        for ky in range(3):
            moved = shift_lanes(moved_x, (1 - ky) * EDGE)
            if ky == 0:
                moved = jnp.where(lane < PIX - EDGE, moved, 0.0)
            elif ky == 2:
                moved = jnp.where(lane >= EDGE, moved, 0.0)
            tap = 3 * ky + kx
            taps[tap * 8 : tap * 8 + 8, :] = moved


def split_bias(half):
    at = iota((HALF, LANES), 0) == BIAS_ROW
    lane = iota((HALF, LANES), 1)
    total = half + pltpu.roll(half, LANES - RGB, 1)
    high = total.astype(bf16).astype(f32)
    low = pltpu.roll(total - high, RGB, 1)
    pair = jnp.where(lane < RGB, high, jnp.where(lane < 2 * RGB, low, half))
    return jnp.where(at, pair, half).astype(bf16)


def weight_grad_kernel(chunk, got_ref, feat_ref, out_ref, grad_ref, taps):
    row = iota((8, LANES), 0)
    for rh in range(2):
        block = unpack_half(got_ref[rh * LANES : (rh + 1) * LANES, :])
        for n, r in enumerate(rows_of_half(rh)):
            piece = block[n * 8 : n * 8 + 8, :]
            grad_ref[:, r * LANES : (r + 1) * LANES] = jnp.where(row < RGB, piece, 0.0)
    grad = grad_ref[...]
    grad_stack(grad, taps)
    bias = lax.dot_general(
        jnp.ones((8, PIX), bf16), grad.astype(bf16), (((1,), (1,)), ((), ())), preferred_element_type=f32
    )
    sums = [jnp.zeros((CH, STACK), f32) for _ in range(TIN)]
    for at in range(0, PIX, chunk):
        part = taps[:, at : at + chunk].astype(bf16)
        for t in range(TIN):
            sums[t] += lax.dot_general(
                feat_ref[t, :, at : at + chunk], part, (((1,), (1,)), ((), ())), preferred_element_type=f32
            )
    rows = jnp.concatenate([total.T for total in sums], axis=0)
    rows = jnp.concatenate([rows, jnp.zeros((TIN * STACK, LANES - CH), f32)], axis=1).astype(bf16)
    for h in range(2):
        place = iota((HALF, TIN * STACK), 0)
        source = iota((HALF, TIN * STACK), 1)
        rank = jnp.where(source % 8 < RGB, (source // 8) * RGB + source % 8, -1)
        main = (rank == h * MAIN + place) & (place < MAIN)
        side = rank == 2 * MAIN + (h * HALF + place) // 3
        front = jnp.dot(main.astype(f32).astype(bf16), rows, preferred_element_type=f32)
        back = jnp.dot(side.astype(f32).astype(bf16), rows, preferred_element_type=f32)
        third = (h * HALF + iota((HALF, LANES), 0)) % 3
        tail = jnp.zeros((HALF, LANES), f32)
        for c in range(3):
            tail = jnp.where(third == c, pltpu.roll(back, CH - 32 * c, 1), tail)
        half = jnp.where(iota((HALF, LANES), 1) < CH, front, tail)
        at_bias = (iota((HALF, LANES), 0) == BIAS_ROW) & (iota((HALF, LANES), 1) < CH)
        bias_wide = jnp.concatenate([bias, jnp.zeros((8, LANES - 8), f32)], axis=1)[0:1]
        bias_wide = jnp.where(iota((1, LANES), 1) < RGB, bias_wide, 0.0)
        half = split_bias(jnp.where(at_bias, bias_wide, half))
        for y in range(8):
            out_ref[2 * y + h] = half


def feature_grad_kernel(chunk, grad_ref, weight_ref, out_ref, taps, held):
    step = pl.program_id(0)

    @pl.when(step == 0)
    def _():
        stack_weights(weight_ref, held)
        grad_stack(grad_ref[...], taps)

    part = taps[:, pl.ds(pl.multiple_of(step * chunk, chunk), chunk)].astype(bf16)
    for t in range(TIN):
        out_ref[t] = lax.dot_general(
            held[t].astype(bf16), part, (((0,), (0,)), ((), ())), preferred_element_type=f32
        ).astype(bf16)


def decode_kernel(got_ref, image_ref):
    for rh in range(2):
        block = unpack_half(got_ref[rh * LANES : (rh + 1) * LANES, :])
        for n, r in enumerate(rows_of_half(rh)):
            image_ref[:, r * LANES : (r + 1) * LANES] = block[n * 8 + RGB : n * 8 + 2 * RGB].astype(bf16)


def add_up(got_ref, first, count):
    total = got_ref[first].astype(f32)
    for n in range(first + 1, first + count):
        total = total + got_ref[n].astype(f32)
    return total


def sum_kernel(got_ref, out_ref):
    half = split_bias(add_up(got_ref, 0, got_ref.shape[0]))
    for n in range(out_ref.shape[0]):
        out_ref[n] = half


def finish_kernel(scale, got_ref, weight_ref, bias_ref, held, others):
    for h in range(2):
        held[h * HALF : (h + 1) * HALF, :] = add_up(got_ref, 4 * h, 4) * scale
    bias = held[BIAS_ROW : BIAS_ROW + 1, :]
    bias_ref[...] = bias[:, 0:RGB] + bias[:, RGB : 2 * RGB]
    count = TIN * TAPS * RGB - 2 * MAIN
    lane = iota((count, LANES), 1)
    tail = jnp.zeros((count, LANES), f32)
    for c in range(3):
        turned = pltpu.roll(held[pl.ds(c, count, stride=3), :], (32 + 32 * c) % LANES, 1)
        tail = jnp.where(lane // 32 == c, turned, tail)
    others[0:count, :] = tail
    for n in range(TIN * TAPS):
        at = n * RGB
        if at < 2 * MAIN:
            at = (at // MAIN) * HALF + at % MAIN
            value = held[at : at + RGB, 0:CH]
        else:
            at -= 2 * MAIN
            value = others[at : at + RGB, 0:CH]
        weight_ref[n // TAPS, n % TAPS] = value


VM = pl.BlockSpec(memory_space=pltpu.VMEM)
SM = pl.BlockSpec(memory_space=pltpu.SMEM)
HBM = pl.BlockSpec(memory_space=pltpu.HBM)
LIMIT = 40 * 1024 * 1024
FULL = 64 * 1024 * 1024
message = jax.ShapeDtypeStruct((BOTH, LANES), bf16)


def call(body, out_shape, in_specs, scratch=(), flops=1 << 20, size=1 << 17, name=None, limit=LIMIT, **rest):
    return pl.pallas_call(
        body,
        out_shape=out_shape,
        in_specs=in_specs,
        scratch_shapes=list(scratch),
        compiler_params=pltpu.CompilerParams(vmem_limit_bytes=limit),
        cost_estimate=pl.CostEstimate(flops=flops, bytes_accessed=size, transcendentals=0),
        name=name,
        **rest,
    )


def exchange(rows, axes):
    return lax.all_to_all(rows, axes, 0, 0, tiled=True)


def exchange_tiles(rows):
    return exchange(rows.reshape(SLOTS, 2, LANES), ("y", "z", "c")).reshape(BOTH, LANES)


def per_device(features, conv_weight, bias, blend_profile, tile_ids, reward_grad):
    chunk = 1024
    conv_flops = 2 * STACK * TIN * CH * PIX
    own = lax.axis_index(("y", "z", "c")).reshape(1).astype(jnp.int32)
    feats = jnp.transpose(features[0, 0], (1, 0, 2))

    parts_out = call(
        functools.partial(conv_kernel, chunk),
        message,
        [HBM, VM, SM, VM],
        [
            pltpu.VMEM((TIN, CH, PIX), bf16),
            pltpu.VMEM((TIN, STACK, CH), f32),
            pltpu.VMEM((STACK, PIX), f32),
            pltpu.SemaphoreType.DMA((PIX // chunk,)),
        ],
        conv_flops,
        1 << 22,
        "conv",
        FULL,
        out_specs=VM,
    )(feats, conv_weight, bias, reward_grad[0, 0])
    parts_got = exchange_tiles(parts_out)

    factors = jax.ShapeDtypeStruct((BOTH, LANES), f32)
    mats, before, after, feats_held = call(
        blend_prep_kernel,
        (
            jax.ShapeDtypeStruct((3 * BOTH, BOTH), bf16),
            factors,
            factors,
            jax.ShapeDtypeStruct((TIN, CH, PIX), bf16),
        ),
        [VM, SM, SM, HBM],
        [pltpu.SemaphoreType.DMA],
        1 << 25,
        1 << 22,
        "blend_prep",
        out_specs=(VM, VM, VM, VM),
    )(tile_ids, blend_profile, own, feats)
    blend_out = call(
        blend_kernel, message, [VM, VM, VM, VM], (), 1 << 27, 1 << 20, "blend", out_specs=VM
    )(parts_got, mats, before, after)
    blend_got = exchange_tiles(blend_out)

    sums, grad_rows = call(
        functools.partial(weight_grad_kernel, chunk),
        (
            jax.ShapeDtypeStruct((16, HALF, LANES), bf16),
            jax.ShapeDtypeStruct((8, PIX), f32),
        ),
        [VM, VM],
        [pltpu.VMEM((STACK, PIX), f32)],
        conv_flops,
        1 << 22,
        "weight_grad",
        out_specs=(VM, VM),
    )(blend_got, feats_held)
    feature_rows = call(
        functools.partial(feature_grad_kernel, chunk),
        jax.ShapeDtypeStruct((TIN, CH, PIX), bf16),
        [
            pl.BlockSpec((8, PIX), lambda i: (0, 0)),
            pl.BlockSpec((TIN, TAPS, RGB, CH), lambda i: (0, 0, 0, 0)),
        ],
        [pltpu.VMEM((STACK, PIX), f32), pltpu.VMEM((TIN, STACK, CH), f32)],
        conv_flops,
        1 << 22,
        "feature_grad",
        grid=(PIX // chunk,),
        out_specs=pl.BlockSpec((TIN, CH, chunk), lambda i: (0, 0, i)),
    )(grad_rows, conv_weight)
    feature_grad = jnp.transpose(feature_rows, (1, 0, 2))[None, None]
    decoded = call(
        decode_kernel, jax.ShapeDtypeStruct((RGB, PIX), bf16), [VM], name="decode", out_specs=VM
    )(blend_got)
    sums = exchange(sums, ("y", "c"))
    sums, feature_grad = lax.optimization_barrier((sums, feature_grad))
    sums = call(
        sum_kernel, jax.ShapeDtypeStruct((8, HALF, LANES), bf16), [VM], name="sum_y", out_specs=VM
    )(sums)
    sums = exchange(sums, "z")
    sums, decoded = lax.optimization_barrier((sums, decoded))
    sums = call(
        sum_kernel, jax.ShapeDtypeStruct((8, HALF, LANES), bf16), [VM], name="sum_z", out_specs=VM
    )(sums)
    sums = exchange(sums, ("c", "clip"))
    scale = 1.0 / math.sqrt(4 * SLOTS * PIX)
    weight_grad, bias_grad = call(
        functools.partial(finish_kernel, scale),
        (
            jax.ShapeDtypeStruct((TIN, TAPS, RGB, CH), f32),
            jax.ShapeDtypeStruct((1, RGB), f32),
        ),
        [VM],
        [pltpu.VMEM((2 * HALF, LANES), f32), pltpu.VMEM((24, LANES), f32)],
        name="finish",
        out_specs=(VM, VM),
    )(sums)

    return (decoded[None, None], feature_grad, weight_grad, bias_grad.reshape(RGB))


def solution(mesh):
    parts = Mesh(mesh.devices.reshape(8, 8, 2, 4), ("y", "z", "c", "clip"))
    tile = ("y", "z", "c")
    return jax.shard_map(
        per_device,
        mesh=parts,
        in_specs=(
            P("clip", tile, None, None, None),
            P(),
            P(),
            P(),
            P("clip", None),
            P("clip", tile, None, None),
        ),
        out_specs=(P("clip", tile, None, None), P("clip", tile, None, None, None), P(), P()),
        check_vma=False,
    )
```

time: 100 us -> 91.3 us (0.913)
  blocking collectives: 35.8 us -> 27.6 us
  starting transfers between devices: 29.5 us -> 25.6 us
  waiting for transfers between devices: 17.6 us -> 20.4 us
  Pallas kernels: 12.3 us -> 13.4 us
    all_to_all x2, blocking collectives: 35.8 us -> 27.6 us  [exchange(): return lax.all_to_all(rows, axes, 0, 0, tiled=True)]
    all_to_all x3, starting transfers between devices: 29.5 us -> 25.6 us  [exchange(): return lax.all_to_all(rows, axes, 0, 0, tiled=True)]
    all_to_all x3, waiting for transfers between devices: 17.6 us -> 20.4 us  [exchange(): return lax.all_to_all(rows, axes, 0, 0, tiled=True)]
    pallas_call x9, Pallas kernels: 12.3 us -> 13.4 us  [the longest x1 3.97 us: per_device(): call(functools.partial(conv_kernel, chunk), message, [HBM, VM, SM, VM], [...]
    unnamed x12 -> x8, local copies, waits for them, and re-layouts: 3.09 us -> 2.98 us
  transfers between devices with their start and end apart: 3 -> 3, of which waited for: 3 -> 3; matrix products, arithmetic and copies ran while one was open for 1% -> 0% of each run, Pallas kernels for 7% -> 5%
where the time goes in v2:
time: 91.3 us; the launch traced here: 90.8 us
  blocking collectives  27.6 us (30%)
  starting transfers between devices  25.6 us (28%)
  waiting for transfers between devices  20.4 us (22%)
  Pallas kernels  13.4 us (15%)
  local copies, waits for them, and re-layouts  2.98 us (3%)
    all_to_all x2, blocking collectives, exchange(): return lax.all_to_all(rows, axes, 0, 0, tiled=True)  27.6 us
    all_to_all x3, starting transfers between devices, exchange(): return lax.all_to_all(rows, axes, 0, 0, tiled=True)  25.6 us
    all_to_all x3, waiting for transfers between devices, exchange(): return lax.all_to_all(rows, axes, 0, 0, tiled=True)  20.4 us
    pallas_call x1, Pallas kernels, per_device(): call(functools.partial(conv_kernel, chunk), message, [HBM, VM, SM, VM], [...  3.97 us
    unnamed x8, local copies, waits for them, and re-layouts  2.98 us
    pallas_call x1, Pallas kernels, per_device(): call(functools.partial(feature_grad_kernel, chunk), jax.ShapeDtypeStruct(...  2.97 us
    pallas_call x1, Pallas kernels, per_device(): call(functools.partial(weight_grad_kernel, chunk), (jax.ShapeDtypeStruct(...  2.43 us
  transfers between devices with their start and end apart: 3, of which 3 were waited for; matrix products, arithmetic and copies ran while one was open for 0% of the time, Pallas kernels for 5%

profile of v2, /device:TPU:1, one launch (start us, length us, event | category | flops | bytes accessed | tf_op | source)
XLA Modules:
  0.0 90.8 jit_solution(4702519023649212815)
XLA Ops:
  0.6 4.0 %conv.1 = bf16[256,128]{1,0:T(8,128)(2,1)} custom-call(bf16[3,96,4096]{2,1,0:T(8,128)(2,1)} %bitcast.14, bf16[3,9,3,96]{3,2,1,0:T(4,128)(2,1)} %weight_ref.3, f32[3]{0:T(128)} %bias_ref.1, bf16[3,4096]{1,0:T(4,128)(2,1)} %bitcast.22), custom_call_target="tpu_custom_call" | custom-call | flops 169869312 | bytes 4194304 | tf_op jit(solution)/shard_map/conv/pallas_call | solution.py:344
  4.6 18.4 %all-to-all-start = ((bf16[128,2,128]{2,1,0:T(2,128)(2,1)}), bf16[128,2,128]{2,1,0:T(2,128)(2,1)S(1)}, u32[]{:S(2)}, u32[]{:S(2)}) async-start(bf16[128,2,128]{2,1,0:T(2,128)(2,1)} %bitcast.21), calls=%async_computation | async-start | bytes 131072 | tf_op jit(solution)/shard_map/all_to_all | solution.py:331
  23.1 0.0 copy-start
  23.1 1.7 %copy-done = bf16[1,1,96,3,4096]{4,2,3,1,0:T(8,128)(2,1)S(1)} copy-done((bf16[1,1,96,3,4096]{4,2,3,1,0:T(8,128)(2,1)S(1)}, bf16[1,1,96,3,4096]{4,2,3,1,0:T(8,128)(2,1)}, u32[]{:S(2)}) %copy-start) | copy-done | bytes 2359320
  24.7 0.0 copy-start.2
  24.7 0.7 copy-done.2
  25.4 0.0 copy-start.3
  25.4 0.7 copy-done.3
  26.0 1.1 %blend_prep.1 = (bf16[768,256]{1,0:T(8,128)(2,1)S(1)}, f32[256,128]{1,0:T(8,128)S(1)}, f32[256,128]{1,0:T(8,128)S(1)}, bf16[3,96,4096]{2,1,0:T(8,128)(2,1)S(1)}) custom-call(s32[1,128]{1,0:T(1,128)S(1)} %copy-done.2, s32[32]{0:T(128)S(1)} %copy-done.3, s32[1]{0:T(128)} %bitcast.5.own_ref, bf16[3,96,4096]{2,1,0:T(8,128)(2,1)S(1)} %bitcast.15), custom_call_target="tpu_custom_call" | custom-call | flops 33554432 | bytes 4194304 | tf_op jit(solution)/shard_map/blend_prep/pallas_call | solution.py:363
  27.1 0.0 copy-start.1
  27.1 7.4 %all-to-all-done = bf16[128,2,128]{2,1,0:T(2,128)(2,1)S(1)} async-done(((bf16[128,2,128]{2,1,0:T(2,128)(2,1)}), bf16[128,2,128]{2,1,0:T(2,128)(2,1)S(1)}, u32[]{:S(2)}, u32[]{:S(2)}) %all-to-all-start) | async-done | bytes 65568 | tf_op jit(solution)/shard_map/all_to_all | solution.py:331
  34.5 0.4 blend.1
  34.9 17.7 %all_to_all.25 = bf16[128,2,128]{2,1,0:T(2,128)(2,1)S(1)} all-to-all(bf16[128,2,128]{2,1,0:T(2,128)(2,1)S(1)} %bitcast.19), channel_id=1, replica_groups=mesh['y'=8,'z'=8,'c'=2,'clip'=4] {'y','z','c'}, dimensions={0} | all-to-all | bytes 131072 | tf_op jit(solution)/shard_map/all_to_all | solution.py:331
  52.6 2.4 %weight_grad.1 = (bf16[16,32,128]{2,1,0:T(8,128)(2,1)}, f32[8,4096]{1,0:T(8,128)S(1)}) custom-call(bf16[256,128]{1,0:T(8,128)(2,1)S(1)} %bitcast.16, bf16[3,96,4096]{2,1,0:T(8,128)(2,1)S(1)} %get-tuple-element.19.feat_ref), custom_call_target="tpu_custom_call" | custom-call | flops 169869312 | bytes 4194304 | tf_op jit(solution)/shard_map/weight_grad/pallas_call | solution.py:383
  55.1 3.9 %all-to-all-start.2 = ((bf16[16,32,128]{2,1,0:T(8,128)(2,1)}), bf16[16,32,128]{2,1,0:T(8,128)(2,1)S(1)}, u32[]{:S(2)}, u32[]{:S(2)}) async-start(bf16[16,32,128]{2,1,0:T(8,128)(2,1)} %get-tuple-element.20), calls=%async_computation.2 | async-start | bytes 262144 | tf_op jit(solution)/shard_map/all_to_all | solution.py:331
  58.9 0.0 copy-done.1
  58.9 3.0 %feature_grad.1 = bf16[3,96,4096]{2,1,0:T(8,128)(2,1)} custom-call(f32[8,4096]{1,0:T(8,128)S(1)} %get-tuple-element.21.grad_ref, bf16[3,9,3,96]{3,2,1,0:T(4,128)(2,1)S(1)} %copy-done.1), custom_call_target="tpu_custom_call" | custom-call | flops 169869312 | bytes 4194304 | tf_op jit(solution)/shard_map/feature_grad/pallas_call | solution.py:396
  61.9 6.2 %all-to-all-done.2.got_ref = bf16[16,32,128]{2,1,0:T(8,128)(2,1)S(1)} async-done(((bf16[16,32,128]{2,1,0:T(8,128)(2,1)}), bf16[16,32,128]{2,1,0:T(8,128)(2,1)S(1)}, u32[]{:S(2)}, u32[]{:S(2)}) %all-to-all-start.2) | async-done | bytes 131104 | tf_op jit(solution)/shard_map/all_to_all | solution.py:331
  68.1 0.8 sum_y.1
  68.9 3.3 %all-to-all-start.3 = ((bf16[8,32,128]{2,1,0:T(8,128)(2,1)}), bf16[8,32,128]{2,1,0:T(8,128)(2,1)S(1)}, u32[]{:S(2)}, u32[]{:S(2)}) async-start(bf16[8,32,128]{2,1,0:T(8,128)(2,1)} %sum_y.1), calls=%async_computation.3 | async-start | bytes 131072 | tf_op jit(solution)/shard_map/all_to_all | solution.py:331
  72.3 0.9 decode.1
  73.2 6.8 %all-to-all-done.3.got_ref = bf16[8,32,128]{2,1,0:T(8,128)(2,1)S(1)} async-done(((bf16[8,32,128]{2,1,0:T(8,128)(2,1)}), bf16[8,32,128]{2,1,0:T(8,128)(2,1)S(1)}, u32[]{:S(2)}, u32[]{:S(2)}) %all-to-all-start.3) | async-done | bytes 65568 | tf_op jit(solution)/shard_map/all_to_all | solution.py:331
  80.0 0.2 sum_z.1
  80.2 9.9 %all_to_all.26.got_ref = bf16[8,32,128]{2,1,0:T(8,128)(2,1)S(1)} all-to-all(bf16[8,32,128]{2,1,0:T(8,128)(2,1)S(1)} %sum_z.1), channel_id=1, replica_groups=mesh['y'=8,'z'=8,'c'=2,'clip'=4] {'c','clip'}, dimensions={0} | all-to-all | bytes 131072 | tf_op jit(solution)/shard_map/all_to_all | solution.py:331
  90.0 0.7 finish.1
Async XLA Ops:
  4.6 29.9 %all-to-all-start = ((bf16[128,2,128]{2,1,0:T(2,128)(2,1)}), bf16[128,2,128]{2,1,0:T(2,128)(2,1)S(1)}, u32[]{:S(2)}, u32[]{:S(2)}) async-start(bf16[128,2,128]{2,1,0:T(2,128)(2,1)} %bitcast.21), calls=%async_computation | async-start | bytes 131072 | tf_op jit(solution)/shard_map/all_to_all | solution.py:331
  23.1 1.7 %copy-start = (bf16[1,1,96,3,4096]{4,2,3,1,0:T(8,128)(2,1)S(1)}, bf16[1,1,96,3,4096]{4,2,3,1,0:T(8,128)(2,1)}, u32[]{:S(2)}) copy-start(bf16[1,1,96,3,4096]{4,2,3,1,0:T(8,128)(2,1)} %param.6) | copy-start | bytes 7077892
  24.7 0.7 copy-start.2
  25.4 0.7 copy-start.3
  27.1 31.8 %copy-start.1 = (bf16[3,9,3,96]{3,2,1,0:T(4,128)(2,1)S(1)}, bf16[3,9,3,96]{3,2,1,0:T(4,128)(2,1)}, u32[]{:S(2)}) copy-start(bf16[3,9,3,96]{3,2,1,0:T(4,128)(2,1)} %weight_ref.3) | copy-start | bytes 46660
  55.1 13.1 %all-to-all-start.2 = ((bf16[16,32,128]{2,1,0:T(8,128)(2,1)}), bf16[16,32,128]{2,1,0:T(8,128)(2,1)S(1)}, u32[]{:S(2)}, u32[]{:S(2)}) async-start(bf16[16,32,128]{2,1,0:T(8,128)(2,1)} %get-tuple-element.20), calls=%async_computation.2 | async-start | bytes 262144 | tf_op jit(solution)/shard_map/all_to_all | solution.py:331
  68.9 11.1 %all-to-all-start.3 = ((bf16[8,32,128]{2,1,0:T(8,128)(2,1)}), bf16[8,32,128]{2,1,0:T(8,128)(2,1)S(1)}, u32[]{:S(2)}, u32[]{:S(2)}) async-start(bf16[8,32,128]{2,1,0:T(8,128)(2,1)} %sum_y.1), calls=%async_computation.3 | async-start | bytes 131072 | tf_op jit(solution)/shard_map/all_to_all | solution.py:331

commit v3 on v2

--- a/solution.py
+++ b/solution.py
@@ -69,11 +69,7 @@
     return out
 
 
-def blend_prep_kernel(ids_ref, profile_ref, own_ref, feat_ref, mats_ref, before_ref, after_ref, held_ref, sem):
-    copy = pltpu.make_async_copy(feat_ref, held_ref, sem)
-    copy.start()
-    own = own_ref[0]
-    ids = ids_ref[...].astype(f32)
+def blend_prep(ids, profile_ref, own, mats_ref, before_ref, after_ref):
     slot_row = iota((BOTH, SLOTS), 0) // 2
     spread = slot_row == iota((BOTH, SLOTS), 1)
     id_col = jnp.sum(jnp.where(spread, jnp.broadcast_to(ids, (BOTH, SLOTS)), 0.0), axis=1, keepdims=True)
@@ -110,7 +106,6 @@
     grads = iota((BOTH, LANES), 1) % 8 < RGB
     before_ref[...] = jnp.where(grads, 1.0, weight)
     after_ref[...] = jnp.where(grads, weight, 1.0) / coverage
-    copy.wait()
 
 
 def blend_kernel(got_ref, mats_ref, before_ref, after_ref, out_ref):
@@ -135,14 +130,44 @@
             held[t, tap * 8 : tap * 8 + RGB, :] = weight_ref[t, tap].astype(f32)
 
 
-def conv_kernel(chunk, feat_ref, weight_ref, bias_ref, grad_ref, out_ref, feats, held, taps, sems):
+def conv_kernel(
+    chunk,
+    feat_ref,
+    weight_hbm,
+    bias_hbm,
+    grad_hbm,
+    ids_hbm,
+    profile_hbm,
+    own_ref,
+    out_ref,
+    mats_ref,
+    before_ref,
+    after_ref,
+    feats,
+    weight_ref,
+    bias_ref,
+    grad_ref,
+    ids_ref,
+    profile_ref,
+    held,
+    taps,
+    small_sems,
+    sems,
+):
+    small = [(ids_hbm, ids_ref), (profile_hbm, profile_ref), (weight_hbm, weight_ref), (grad_hbm, grad_ref), (bias_hbm, bias_ref)]
+    moves = [pltpu.make_async_copy(src, dst, small_sems.at[n]) for n, (src, dst) in enumerate(small)]
+    for move in moves:
+        move.start()
     copies = []
     for n in range(PIX // chunk):
         part = pl.ds(n * chunk, chunk)
         copies.append(pltpu.make_async_copy(feat_ref.at[:, :, part], feats.at[:, :, part], sems.at[n]))
         copies[-1].start()
+    for move in moves:
+        move.wait()
     stack_weights(weight_ref, held)
     kernels = [held[t].astype(bf16) for t in range(TIN)]
+    blend_prep(ids_ref[...].astype(f32), profile_ref, own_ref[0], mats_ref, before_ref, after_ref)
     for n in range(PIX // chunk):
         copies[n].wait()
         total = jnp.zeros((STACK, chunk), f32)
@@ -341,40 +366,36 @@
     own = lax.axis_index(("y", "z", "c")).reshape(1).astype(jnp.int32)
     feats = jnp.transpose(features[0, 0], (1, 0, 2))
 
-    parts_out = call(
+    factors = pltpu.VMEM((BOTH, LANES), f32)
+    here = [pltpu.with_memory_space_constraint(x, pltpu.HBM) for x in (feats, conv_weight, bias, reward_grad[0, 0], tile_ids, blend_profile)]
+    parts_out, mats, before, after, feats_held = call(
         functools.partial(conv_kernel, chunk),
-        message,
-        [HBM, VM, SM, VM],
+        (
+            pltpu.VMEM((BOTH, LANES), bf16),
+            pltpu.VMEM((3 * BOTH, BOTH), bf16),
+            factors,
+            factors,
+            pltpu.VMEM((TIN, CH, PIX), bf16),
+        ),
+        [HBM, HBM, HBM, HBM, HBM, HBM, SM],
         [
-            pltpu.VMEM((TIN, CH, PIX), bf16),
+            pltpu.VMEM((TIN, TAPS, RGB, CH), bf16),
+            pltpu.SMEM((RGB,), f32),
+            pltpu.VMEM((RGB, PIX), bf16),
+            pltpu.VMEM((1, SLOTS), jnp.int32),
+            pltpu.SMEM((OV,), jnp.int32),
             pltpu.VMEM((TIN, STACK, CH), f32),
             pltpu.VMEM((STACK, PIX), f32),
+            pltpu.SemaphoreType.DMA((5,)),
             pltpu.SemaphoreType.DMA((PIX // chunk,)),
         ],
         conv_flops,
         1 << 22,
         "conv",
-        FULL,
-        out_specs=VM,
-    )(feats, conv_weight, bias, reward_grad[0, 0])
+        out_specs=(VM, VM, VM, VM, VM),
+    )(*here, own)
     parts_got = exchange_tiles(parts_out)
 
-    factors = jax.ShapeDtypeStruct((BOTH, LANES), f32)
-    mats, before, after, feats_held = call(
-        blend_prep_kernel,
-        (
-            jax.ShapeDtypeStruct((3 * BOTH, BOTH), bf16),
-            factors,
-            factors,
-            jax.ShapeDtypeStruct((TIN, CH, PIX), bf16),
-        ),
-        [VM, SM, SM, HBM],
-        [pltpu.SemaphoreType.DMA],
-        1 << 25,
-        1 << 22,
-        "blend_prep",
-        out_specs=(VM, VM, VM, VM),
-    )(tile_ids, blend_profile, own, feats)
     blend_out = call(
         blend_kernel, message, [VM, VM, VM, VM], (), 1 << 27, 1 << 20, "blend", out_specs=VM
     )(parts_got, mats, before, after)
@@ -412,12 +433,11 @@
         decode_kernel, jax.ShapeDtypeStruct((RGB, PIX), bf16), [VM], name="decode", out_specs=VM
     )(blend_got)
     sums = exchange(sums, ("y", "c"))
-    sums, feature_grad = lax.optimization_barrier((sums, feature_grad))
     sums = call(
         sum_kernel, jax.ShapeDtypeStruct((8, HALF, LANES), bf16), [VM], name="sum_y", out_specs=VM
     )(sums)
     sums = exchange(sums, "z")
-    sums, decoded = lax.optimization_barrier((sums, decoded))
+    sums, decoded, feature_grad = lax.optimization_barrier((sums, decoded, feature_grad))
     sums = call(
         sum_kernel, jax.ShapeDtypeStruct((8, HALF, LANES), bf16), [VM], name="sum_z", out_specs=VM
     )(sums)

time: 91.3 us -> 87.7 us (0.961)
  blocking collectives: 27.6 us -> 68.5 us
  starting transfers between devices: 25.6 us -> 3.35 us
  waiting for transfers between devices: 20.4 us -> 3.9 us
  local copies, waits for them, and re-layouts: 2.98 us -> 0.01 us
  Pallas kernels: 13.4 us -> 10.8 us
    all_to_all x2 -> x4, blocking collectives: 27.6 us -> 68.5 us  [exchange(): return lax.all_to_all(rows, axes, 0, 0, tiled=True)]
    all_to_all x3 -> x1, starting transfers between devices: 25.6 us -> 3.35 us  [exchange(): return lax.all_to_all(rows, axes, 0, 0, tiled=True)]
    all_to_all x3 -> x1, waiting for transfers between devices: 20.4 us -> 3.9 us  [exchange(): return lax.all_to_all(rows, axes, 0, 0, tiled=True)]
    unnamed x8 -> x2, local copies, waits for them, and re-layouts: 2.98 us -> 0.01 us
    pallas_call x2 -> x1, Pallas kernels: 5.05 us -> 3.09 us  [per_device(): call(functools.partial(conv_kernel, chunk), (pltpu.VMEM((BOTH, LANES), bf...]
  transfers between devices with their start and end apart: 3 -> 1, of which waited for: 3 -> 1; matrix products, arithmetic and copies ran while one was open for 0% -> 0% of each run, Pallas kernels for 5% -> 4%
where the time goes in v3:
time: 87.7 us; the launch traced here: 87.3 us
  blocking collectives  68.5 us (78%)
  Pallas kernels  10.8 us (12%)
  waiting for transfers between devices  3.9 us (4%)
  starting transfers between devices  3.35 us (4%)
    all_to_all x4, blocking collectives, exchange(): return lax.all_to_all(rows, axes, 0, 0, tiled=True)  68.5 us
    all_to_all x1, waiting for transfers between devices, exchange(): return lax.all_to_all(rows, axes, 0, 0, tiled=True)  3.9 us
    all_to_all x1, starting transfers between devices, exchange(): return lax.all_to_all(rows, axes, 0, 0, tiled=True)  3.35 us
    pallas_call x1, Pallas kernels, per_device(): call(functools.partial(conv_kernel, chunk), (pltpu.VMEM((BOTH, LANES), bf...  3.09 us
    pallas_call x1, Pallas kernels, per_device(): call(functools.partial(feature_grad_kernel, chunk), jax.ShapeDtypeStruct(...  2.95 us
    pallas_call x1, Pallas kernels, per_device(): call(functools.partial(weight_grad_kernel, chunk), (jax.ShapeDtypeStruct(...  1.79 us
  transfers between devices with their start and end apart: 1, of which 1 were waited for; matrix products, arithmetic and copies ran while one was open for 0% of the time, Pallas kernels for 4%

profile of v3, /device:TPU:1, one launch (start us, length us, event | category | flops | bytes accessed | tf_op | source)
XLA Modules:
  0.0 87.3 jit_solution(15146120961414364167)
XLA Ops:
  0.6 3.1 %conv.1 = (bf16[256,128]{1,0:T(8,128)(2,1)S(1)}, bf16[768,256]{1,0:T(8,128)(2,1)S(1)}, f32[256,128]{1,0:T(8,128)S(1)}, f32[256,128]{1,0:T(8,128)S(1)}, bf16[3,96,4096]{2,1,0:T(8,128)(2,1)S(1)}) custom-call(bf16[3,96,4096]{2,1,0:T(8,128)(2,1)} %bitcast.19, bf16[3,9,3,96]{3,2,1,0:T(4,128)(2,1)} %weight_ref.1, f32[3]{0:T(128)} %bias_hbm.1, ...), custom_call_target="tpu_custom_call" | custom-call | flops 169869312 | bytes 4194304 | tf_op jit(solution)/shard_map/conv/pallas_call | solution.py:371
  3.7 0.0 copy-start
  3.8 29.7 %all_to_all.25 = bf16[128,2,128]{2,1,0:T(2,128)(2,1)S(1)} all-to-all(bf16[128,2,128]{2,1,0:T(2,128)(2,1)S(1)} %bitcast.18), channel_id=1, replica_groups=mesh['y'=8,'z'=8,'c'=2,'clip'=4] {'y','z','c'}, dimensions={0} | all-to-all | bytes 131072 | tf_op jit(solution)/shard_map/all_to_all | solution.py:356
  33.5 0.4 blend.1
  33.9 16.8 %all_to_all.26 = bf16[128,2,128]{2,1,0:T(2,128)(2,1)S(1)} all-to-all(bf16[128,2,128]{2,1,0:T(2,128)(2,1)S(1)} %bitcast.17), channel_id=1, replica_groups=mesh['y'=8,'z'=8,'c'=2,'clip'=4] {'y','z','c'}, dimensions={0} | all-to-all | bytes 131072 | tf_op jit(solution)/shard_map/all_to_all | solution.py:356
  50.7 1.8 %weight_grad.1 = (bf16[16,32,128]{2,1,0:T(8,128)(2,1)S(1)}, f32[8,4096]{1,0:T(8,128)S(1)}) custom-call(bf16[256,128]{1,0:T(8,128)(2,1)S(1)} %bitcast.14, bf16[3,96,4096]{2,1,0:T(8,128)(2,1)S(1)} %get-tuple-element.20.feat_ref), custom_call_target="tpu_custom_call" | custom-call | flops 169869312 | bytes 4194304 | tf_op jit(solution)/shard_map/weight_grad/pallas_call | solution.py:404
  52.5 12.2 %all_to_all.27.got_ref = bf16[16,32,128]{2,1,0:T(8,128)(2,1)S(1)} all-to-all(bf16[16,32,128]{2,1,0:T(8,128)(2,1)S(1)} %get-tuple-element.21), channel_id=1, replica_groups=mesh['y'=8,'z'=8,'c'=2,'clip'=4] {'y','c'}, dimensions={0} | all-to-all | bytes 262144 | tf_op jit(solution)/shard_map/all_to_all | solution.py:356
  64.7 0.8 sum_y.1
  65.5 3.3 %all-to-all-start.3 = ((bf16[8,32,128]{2,1,0:T(8,128)(2,1)}), bf16[8,32,128]{2,1,0:T(8,128)(2,1)S(1)}, u32[]{:S(2)}, u32[]{:S(2)}) async-start(bf16[8,32,128]{2,1,0:T(8,128)(2,1)} %sum_y.1), calls=%async_computation.3 | async-start | bytes 131072 | tf_op jit(solution)/shard_map/all_to_all | solution.py:356
  68.8 0.9 decode.1
  69.7 0.0 copy-done
  69.7 3.0 %feature_grad.1 = bf16[3,96,4096]{2,1,0:T(8,128)(2,1)} custom-call(f32[8,4096]{1,0:T(8,128)S(1)} %get-tuple-element.22.grad_ref, bf16[3,9,3,96]{3,2,1,0:T(4,128)(2,1)S(1)} %copy-done), custom_call_target="tpu_custom_call" | custom-call | flops 169869312 | bytes 4194304 | tf_op jit(solution)/shard_map/feature_grad/pallas_call | solution.py:417
  72.6 3.9 %all-to-all-done.3.got_ref = bf16[8,32,128]{2,1,0:T(8,128)(2,1)S(1)} async-done(((bf16[8,32,128]{2,1,0:T(8,128)(2,1)}), bf16[8,32,128]{2,1,0:T(8,128)(2,1)S(1)}, u32[]{:S(2)}, u32[]{:S(2)}) %all-to-all-start.3) | async-done | bytes 65568 | tf_op jit(solution)/shard_map/all_to_all | solution.py:356
  76.5 0.2 sum_z.1
  76.7 9.9 %all_to_all.28.got_ref = bf16[8,32,128]{2,1,0:T(8,128)(2,1)S(1)} all-to-all(bf16[8,32,128]{2,1,0:T(8,128)(2,1)S(1)} %sum_z.1), channel_id=1, replica_groups=mesh['y'=8,'z'=8,'c'=2,'clip'=4] {'c','clip'}, dimensions={0} | all-to-all | bytes 131072 | tf_op jit(solution)/shard_map/all_to_all | solution.py:356
  86.5 0.7 finish.1
Async XLA Ops:
  3.7 65.9 %copy-start = (bf16[3,9,3,96]{3,2,1,0:T(4,128)(2,1)S(1)}, bf16[3,9,3,96]{3,2,1,0:T(4,128)(2,1)}, u32[]{:S(2)}) copy-start(bf16[3,9,3,96]{3,2,1,0:T(4,128)(2,1)} %weight_ref.1) | copy-start | bytes 46660
  65.5 11.1 %all-to-all-start.3 = ((bf16[8,32,128]{2,1,0:T(8,128)(2,1)}), bf16[8,32,128]{2,1,0:T(8,128)(2,1)S(1)}, u32[]{:S(2)}, u32[]{:S(2)}) async-start(bf16[8,32,128]{2,1,0:T(8,128)(2,1)} %sum_y.1), calls=%async_computation.3 | async-start | bytes 131072 | tf_op jit(solution)/shard_map/all_to_all | solution.py:356

commit v4 on v3

v4 whole, which is shorter than its diff:
```python
import functools
import math

import jax
import jax.numpy as jnp
from jax import lax
from jax.experimental import pallas as pl
from jax.experimental.pallas import tpu as pltpu
from jax.sharding import Mesh
from jax.sharding import PartitionSpec as P

EDGE = 64
OV = 32
PIX = EDGE * EDGE
SLOTS = 128
TX = 16
TY = SLOTS // TX
CH = 96
RGB = 3
TIN = 3
LANES = 128
ROWS = PIX // LANES
BOTH = 2 * SLOTS
TAPS = 9
STACK = TAPS * 8
HALF = 32
MAIN = 30
BIAS_ROW = 30

BOTH = 2 * SLOTS
TAPS = 9
STACK = TAPS * 8
PEERS = 16
GRAD_ROWS = RGB * 16
HALF = 32
MAIN = 30
BIAS_ROW = 30

f32 = jnp.float32
bf16 = jnp.bfloat16


def iota(shape, dim):
    return lax.broadcasted_iota(jnp.int32, shape, dim)


def onehot(mask):
    return jnp.where(mask, 1.0, 0.0).astype(bf16)


def pick_rows(mask, rows):
    return jnp.dot(onehot(mask), rows.astype(bf16), preferred_element_type=f32)


def shift_lanes(value, amount):
    size = value.shape[1]
    amount = amount % size
    return value if amount == 0 else pltpu.roll(value, size - amount, 1)


def profile_at(index, profile_ref):
    out = jnp.zeros(index.shape, f32)
    for m in range(OV):
        out = jnp.where(index == m, profile_ref[m].astype(f32), out)
    return out


def no_further(room):
    return jnp.minimum(room, 1.0)


def route_prep(ids, y, z, mats_ref):
    row = iota((BOTH, 1), 0)
    place = iota((BOTH, SLOTS), 0) // 16
    to_slot = (place // 2) * 16 + z * 2 + place % 2
    spread = iota((BOTH, SLOTS), 1) == to_slot
    target = jnp.sum(jnp.where(spread, jnp.broadcast_to(ids, (BOTH, SLOTS)), 0.0), axis=1, keepdims=True)
    from_slot = y * 16 + iota((SLOTS, BOTH), 1) // 16
    source = jnp.dot(
        jnp.broadcast_to(ids, (8, SLOTS)).astype(bf16),
        onehot(iota((SLOTS, BOTH), 0) == from_slot),
        preferred_element_type=f32,
    )[0:1]
    col = target - jnp.floor(target * (1.0 / TX)) * TX
    lane = iota((1, BOTH), 1)
    want = target + (TX * ((row // 8) % 2) + 1024 * (row % 8)).astype(f32)
    have = source + (TX * ((lane // 8) % 2) + 1024 * (lane % 8)).astype(f32)
    right = jnp.where(col < TX - 1.5, want + 1.0, -9999.0)
    left = jnp.where(col > 0.5, want - 1.0, -9999.0)
    for n, key in enumerate((want, left, right)):
        mats_ref[n * BOTH : (n + 1) * BOTH, :] = onehot(have == key)


def class_prep(ids, profile_ref, k, mats_ref, before_ref, after_ref):
    place = iota((SLOTS, SLOTS), 0)
    spread = iota((SLOTS, SLOTS), 1) == (place % 8) * 16 + place // 8
    own = jnp.sum(jnp.where(spread, jnp.broadcast_to(ids, (SLOTS, SLOTS)), 0.0), axis=1, keepdims=True)
    row = jnp.floor(own * (1.0 / TX))
    col = own - row * TX
    right = jnp.where(col < TX - 1.5, own + 1.0, -9999.0)
    left = jnp.where(col > 0.5, own - 1.0, -9999.0)
    n = 0
    for key in (own, left, right):
        gap = ids - key
        for step in (0.0, -float(TX), float(TX)):
            mats_ref[n * SLOTS : (n + 1) * SLOTS, :] = onehot(gap == step)
            n += 1
    h, par, rx = k // 64, (k // 32) % 2, k % 32
    lane = iota((1, LANES), 1)
    east = lane >= 64
    south = (lane // 8) % 2 == 1
    ry = 2 * (8 * h + lane % 8) + par
    fy = profile_at(jnp.where(south, OV - 1 - ry, ry), profile_ref)
    fy_other = profile_at(jnp.where(south, ry, OV - 1 - ry), profile_ref)
    near = profile_ref[rx].astype(f32)
    far = profile_ref[OV - 1 - rx].astype(f32)
    fx = jnp.where(east, far, near)
    fx_other = jnp.where(east, near, far)
    col_there = no_further(jnp.where(east, TX - 1.0 - col, col))
    row_there = no_further(jnp.where(south, TY - 1.0 - row, row))
    before_ref[...] = jnp.broadcast_to(fx * fy, (8, LANES))
    after_ref[...] = 1.0 / ((fx + col_there * fx_other) * (fy + row_there * fy_other))


def ratio_prep(ids, profile_ref, own_slot, ratio_ref):
    own = jnp.sum(jnp.where(iota((1, SLOTS), 1) == own_slot, ids, 0.0), axis=1, keepdims=True)
    row = jnp.floor(own * (1.0 / TX))
    col = own - row * TX
    lane = iota((1, LANES), 1)
    x = lane % EDGE
    y = 2 * iota((ROWS, LANES), 0) + iota((ROWS, LANES), 1) // EDGE
    at_x = jnp.minimum(x, EDGE - 1 - x)
    at_y = jnp.minimum(y, EDGE - 1 - y)
    fx = profile_at(at_x, profile_ref)
    fx_other = profile_at(OV - 1 - at_x, profile_ref)
    fy = profile_at(at_y, profile_ref)
    fy_other = profile_at(OV - 1 - at_y, profile_ref)
    col_there = no_further(jnp.where(x >= OV, TX - 1.0 - col, col))
    row_there = no_further(jnp.where(y >= OV, TY - 1.0 - row, row))
    ratio_ref[...] = fx * fy / ((fx + col_there * fx_other) * (fy + row_there * fy_other))


def swap_rows(slabs):
    block = jnp.concatenate(slabs, axis=0)
    row = iota((SLOTS, SLOTS), 0)
    return pick_rows(iota((SLOTS, SLOTS), 1) == (row % 16) * 8 + row // 16, block)


def route_kernel(got_ref, mats_ref, out_ref):
    slabs = [got_ref[p].astype(f32) for p in range(PEERS)]
    east = iota((BOTH, LANES), 1) % EDGE >= OV
    totals = []
    for o in range(RGB):
        block = jnp.concatenate([slab[o * 16 : o * 16 + 16] for slab in slabs], axis=0).astype(bf16)
        part = [
            jnp.dot(mats_ref[n * BOTH : (n + 1) * BOTH, :], block, preferred_element_type=f32) for n in range(3)
        ]
        side = jnp.where(east, pltpu.roll(part[2], OV, 1), pltpu.roll(part[1], LANES - OV, 1))
        totals.append(part[0] + side)
    images = swap_rows([slab[GRAD_ROWS : GRAD_ROWS + 8] for slab in slabs])
    for t in range(PEERS):
        rows = [total[t * 16 : t * 16 + 16] for total in totals]
        rows.append(images[(t // 2) * 16 : (t // 2) * 16 + 16])
        out_ref[t] = jnp.concatenate(rows, axis=0).astype(bf16)


def blend_classes(images, mats_ref, before_ref, after_ref):
    source = images * before_ref[0:1, :]
    high = source.astype(bf16)
    low = (source - high.astype(f32)).astype(bf16)
    lane = iota((SLOTS, LANES), 1)
    south = (lane // 8) % 2 == 1
    columns = []
    for d in range(3):
        part = []
        for step in range(3):
            mat = mats_ref[(3 * d + step) * SLOTS : (3 * d + step + 1) * SLOTS, :]
            part.append(
                jnp.dot(mat, high, preferred_element_type=f32) + jnp.dot(mat, low, preferred_element_type=f32)
            )
        across = jnp.where(south, part[1], part[2])
        columns.append(part[0] + jnp.where(south, pltpu.roll(across, 8, 1), pltpu.roll(across, LANES - 8, 1)))
    total = columns[0] + pltpu.roll(jnp.where(lane >= 64, columns[1], columns[2]), 64, 1)
    return total * after_ref[...]


def stack_weights(weight_ref, held):
    held[...] = jnp.zeros_like(held)
    for t in range(TIN):
        for tap in range(TAPS):
            held[t, tap * 8 : tap * 8 + RGB, :] = weight_ref[t, tap].astype(f32)


def conv_kernel(
    chunk,
    feat_ref,
    weight_hbm,
    bias_hbm,
    grad_hbm,
    ids_hbm,
    profile_hbm,
    own_ref,
    out_ref,
    route_ref,
    mats_ref,
    before_ref,
    after_ref,
    ratio_ref,
    feats,
    weight_ref,
    bias_ref,
    grad_ref,
    ids_ref,
    profile_ref,
    held,
    taps,
    turned,
    small_sems,
    sems,
):
    small = [(ids_hbm, ids_ref), (profile_hbm, profile_ref), (weight_hbm, weight_ref), (grad_hbm, grad_ref), (bias_hbm, bias_ref)]
    moves = [pltpu.make_async_copy(src, dst, small_sems.at[n]) for n, (src, dst) in enumerate(small)]
    for move in moves:
        move.start()
    copies = []
    for n in range(PIX // chunk):
        part = pl.ds(n * chunk, chunk)
        copies.append(pltpu.make_async_copy(feat_ref.at[:, :, part], feats.at[:, :, part], sems.at[n]))
        copies[-1].start()
    for move in moves:
        move.wait()
    stack_weights(weight_ref, held)
    kernels = [held[t].astype(bf16) for t in range(TIN)]
    ids = ids_ref[...].astype(f32)
    own = own_ref[0]
    y, z, c = own // 16, (own // 2) % 8, own % 2
    route_prep(ids, y, z, route_ref)
    class_prep(ids, profile_ref, (2 * z + c) * 8 + y, mats_ref, before_ref, after_ref)
    ratio_prep(ids, profile_ref, own, ratio_ref)
    taps[0:8, :] = jnp.zeros((8, PIX), f32)
    taps[0:RGB, :] = grad_ref[...].astype(f32)
    halves = []
    for r in range(ROWS):
        turned[r] = taps[0:8, r * LANES : (r + 1) * LANES]
    for h in range(2):
        halves.append(jnp.concatenate(half_rows(turned, h, RGB), axis=0))
    for n in range(PIX // chunk):
        copies[n].wait()
        total = jnp.zeros((STACK, chunk), f32)
        for t in range(TIN):
            total += jnp.dot(kernels[t], feats[t, :, n * chunk : (n + 1) * chunk], preferred_element_type=f32)
        taps[:, n * chunk : (n + 1) * chunk] = total
    lane = iota((8, PIX), 1)
    image = jnp.zeros((8, PIX), f32)
    for kx in range(3):
        column = jnp.zeros((8, PIX), f32)
        for ky in range(3):
            tap = 3 * ky + kx
            moved = shift_lanes(taps[tap * 8 : tap * 8 + 8, :], (ky - 1) * EDGE)
            if ky == 0:
                moved = jnp.where(lane >= EDGE, moved, 0.0)
            elif ky == 2:
                moved = jnp.where(lane < PIX - EDGE, moved, 0.0)
            column = column + moved
        moved = shift_lanes(column, kx - 1)
        if kx == 0:
            moved = jnp.where(lane % EDGE != 0, moved, 0.0)
        elif kx == 2:
            moved = jnp.where(lane % EDGE != EDGE - 1, moved, 0.0)
        image = image + moved
    row = iota((8, 1), 0)
    shift = jnp.zeros((8, 1), f32)
    for o in range(RGB):
        shift = jnp.where(row == o, bias_ref[o], shift)
    image = image + shift
    for r in range(ROWS):
        turned[r] = image[:, r * LANES : (r + 1) * LANES]
    place = iota((LANES, LANES), 0)
    lanes = onehot(iota((LANES, LANES), 1) == ((place // 32) % 2) * 64 + (place // 64) * 32 + place % 32)
    classes = []
    for h in range(2):
        block = half_rows(turned, h, RGB) + [jnp.zeros((16, LANES), f32)]
        block = jnp.concatenate(block, axis=0).astype(bf16)
        both = lax.dot_general(lanes, block, (((1,), (1,)), ((), ())), preferred_element_type=f32)
        classes.append(jnp.concatenate([both[0:64], both[64:128]], axis=1))
    classes = jnp.concatenate(classes, axis=0)
    for p in range(PEERS):
        out_ref[p] = jnp.concatenate([halves[p % 2], classes[p * 8 : p * 8 + 8]], axis=0).astype(bf16)


def half_rows(turned, h, colours):
    return [turned[qy * 16 + h * 8 : qy * 16 + h * 8 + 8, o, :] for o in range(colours) for qy in range(2)]


def grad_stack(grad, taps):
    lane = iota((8, PIX), 1)
    for kx in range(3):
        moved_x = shift_lanes(grad, 1 - kx)
        if kx == 0:
            moved_x = jnp.where(lane % EDGE != EDGE - 1, moved_x, 0.0)
        elif kx == 2:
            moved_x = jnp.where(lane % EDGE != 0, moved_x, 0.0)
        for ky in range(3):
            moved = shift_lanes(moved_x, (1 - ky) * EDGE)
            if ky == 0:
                moved = jnp.where(lane < PIX - EDGE, moved, 0.0)
            elif ky == 2:
                moved = jnp.where(lane >= EDGE, moved, 0.0)
            tap = 3 * ky + kx
            taps[tap * 8 : tap * 8 + 8, :] = moved


def split_bias(half):
    at = iota((HALF, LANES), 0) == BIAS_ROW
    lane = iota((HALF, LANES), 1)
    total = half + pltpu.roll(half, LANES - RGB, 1)
    high = total.astype(bf16).astype(f32)
    low = pltpu.roll(total - high, RGB, 1)
    pair = jnp.where(lane < RGB, high, jnp.where(lane < 2 * RGB, low, half))
    return jnp.where(at, pair, half)


def weight_grad_kernel(
    chunk, got_ref, feat_ref, ratio_ref, mats_ref, before_ref, after_ref, own_ref, out_ref, grad_ref, taps, turned
):
    sums = [got_ref[h].astype(f32) for h in range(2)]
    for n in range(2, PEERS):
        sums[n % 2] = sums[n % 2] + got_ref[n].astype(f32)
    turned[...] = jnp.zeros_like(turned)
    for h in range(2):
        for o in range(RGB):
            for qy in range(2):
                at = qy * 16 + h * 8
                piece = sums[h][o * 16 + qy * 8 : o * 16 + qy * 8 + 8] * ratio_ref[at : at + 8, :]
                turned[at : at + 8, o, :] = piece.astype(bf16).astype(f32)
    for r in range(ROWS):
        grad_ref[:, r * LANES : (r + 1) * LANES] = turned[r]
    core = own_ref[0] % 2
    images = [got_ref[2 * y + core].astype(f32)[GRAD_ROWS : GRAD_ROWS + 16] for y in range(8)]
    blended = blend_classes(jnp.concatenate(images, axis=0), mats_ref, before_ref, after_ref)
    grad = grad_ref[...]
    grad_stack(grad, taps)
    bias = lax.dot_general(
        jnp.ones((8, PIX), bf16), grad.astype(bf16), (((1,), (1,)), ((), ())), preferred_element_type=f32
    )
    total = jnp.zeros((TIN * CH, STACK), f32)
    for at in range(0, PIX, chunk):
        part = taps[:, at : at + chunk].astype(bf16)
        total += lax.dot_general(
            feat_ref[:, :, at : at + chunk].reshape(TIN * CH, chunk),
            part,
            (((1,), (1,)), ((), ())),
            preferred_element_type=f32,
        )
    rows = jnp.concatenate([total[t * CH : (t + 1) * CH].T for t in range(TIN)], axis=0)
    rows = jnp.concatenate([rows, jnp.zeros((TIN * STACK, LANES - CH), f32)], axis=1).astype(bf16)
    place = iota((4 * HALF, TIN * STACK), 0)
    source = iota((4 * HALF, TIN * STACK), 1)
    rank = jnp.where(source % 8 < RGB, (source // 8) * RGB + source % 8, -1)
    within = place % HALF
    main = (rank == (place // HALF) * MAIN + within) & (within < MAIN) & (place < 2 * HALF)
    offset = place - 2 * HALF - RGB * (rank - 2 * MAIN)
    side = (offset >= 0) & (offset < RGB) & (place >= 2 * HALF) & (rank >= 2 * MAIN)
    pick = jnp.where(main | side, 1.0, 0.0).astype(bf16)
    chosen = jnp.dot(pick, rows, preferred_element_type=f32)
    bias_wide = jnp.concatenate([bias, jnp.zeros((8, LANES - 8), f32)], axis=1)[0:1]
    bias_wide = jnp.where(iota((1, LANES), 1) < RGB, bias_wide, 0.0)
    lane = iota((HALF, LANES), 1)
    at_bias = (iota((HALF, LANES), 0) == BIAS_ROW) & (lane < CH)
    halves = []
    for h in range(2):
        front = chosen[h * HALF : (h + 1) * HALF]
        back = chosen[(2 + h) * HALF : (3 + h) * HALF]
        third = (h * HALF + iota((HALF, LANES), 0)) % 3
        tail = jnp.zeros((HALF, LANES), f32)
        for c in range(3):
            tail = jnp.where(third == c, pltpu.roll(back, CH - 32 * c, 1), tail)
        half = jnp.where(at_bias, bias_wide, jnp.where(lane < CH, front, tail))
        halves.append(split_bias(half))
    for p in range(PEERS):
        out_ref[p] = jnp.concatenate([halves[p % 2], blended[p * 8 : p * 8 + 8]], axis=0).astype(bf16)


def feature_grad_kernel(chunk, grad_ref, weight_ref, out_ref, taps, held):
    step = pl.program_id(0)

    @pl.when(step == 0)
    def _():
        stack_weights(weight_ref, held)
        grad_stack(grad_ref[...], taps)

    part = taps[:, pl.ds(pl.multiple_of(step * chunk, chunk), chunk)].astype(bf16)
    for t in range(TIN):
        out_ref[t] = lax.dot_general(
            held[t].astype(bf16), part, (((0,), (0,)), ((), ())), preferred_element_type=f32
        ).astype(bf16)


def decode_kernel(got_ref, own_ref, image_ref, turned):
    core = own_ref[0] % 2
    images = jnp.concatenate([got_ref[2 * y + core].astype(f32)[HALF : HALF + 16] for y in range(8)], axis=0)
    block = jnp.concatenate([images[:, 0:64], images[:, 64:128]], axis=0).astype(bf16)
    row = iota((BOTH, LANES), 0)
    lane = iota((BOTH, LANES), 1)
    k = (row % 16) * 8 + (row // 16) % 8
    spot = ((k // 32) % 2) * 64 + (row // SLOTS) * 32 + k % 32
    for h in range(2):
        lanes = onehot((lane == spot) & (k // 64 == h))
        tile = lax.dot_general(block, lanes, (((0,), (0,)), ((), ())), preferred_element_type=f32)
        for o in range(RGB):
            for qy in range(2):
                turned[qy * 16 + h * 8 : qy * 16 + h * 8 + 8, o, :] = tile[o * 16 + qy * 8 : o * 16 + qy * 8 + 8]
    for r in range(ROWS):
        image_ref[:, r * LANES : (r + 1) * LANES] = turned[r, 0:RGB, :].astype(bf16)


def sum_z_kernel(got_ref, out_ref):
    slabs = [got_ref[p].astype(f32) for p in range(PEERS)]
    half = slabs[0][0:HALF]
    for slab in slabs[1:]:
        half = half + slab[0:HALF]
    half = split_bias(half)
    images = swap_rows([slab[HALF : HALF + 8] for slab in slabs])
    for t in range(PEERS):
        out_ref[t] = jnp.concatenate([half, images[(t // 2) * 16 : (t // 2) * 16 + 16]], axis=0).astype(bf16)


def sum_y_kernel(got_ref, out_ref):
    halves = []
    for h in range(2):
        half = got_ref[h].astype(f32)[0:HALF]
        for y in range(1, 8):
            half = half + got_ref[2 * y + h].astype(f32)[0:HALF]
        halves.append(split_bias(half))
    both = jnp.concatenate(halves, axis=0).astype(bf16)
    for n in range(out_ref.shape[0]):
        out_ref[n] = both


def finish_kernel(scale, got_ref, weight_ref, bias_ref, held, others):
    total = got_ref[0].astype(f32)
    for n in range(1, got_ref.shape[0]):
        total = total + got_ref[n].astype(f32)
    held[...] = total * scale
    bias = held[BIAS_ROW : BIAS_ROW + 1, :]
    bias_ref[...] = bias[:, 0:RGB] + bias[:, RGB : 2 * RGB]
    count = TIN * TAPS * RGB - 2 * MAIN
    lane = iota((count, LANES), 1)
    tail = jnp.zeros((count, LANES), f32)
    for c in range(3):
        turned = pltpu.roll(held[pl.ds(c, count, stride=3), :], (32 + 32 * c) % LANES, 1)
        tail = jnp.where(lane // 32 == c, turned, tail)
    others[0:count, :] = tail
    for n in range(TIN * TAPS):
        at = n * RGB
        if at < 2 * MAIN:
            at = (at // MAIN) * HALF + at % MAIN
            value = held[at : at + RGB, 0:CH]
        else:
            at -= 2 * MAIN
            value = others[at : at + RGB, 0:CH]
        weight_ref[n // TAPS, n % TAPS] = value


VM = pl.BlockSpec(memory_space=pltpu.VMEM)
SM = pl.BlockSpec(memory_space=pltpu.SMEM)
HBM = pl.BlockSpec(memory_space=pltpu.HBM)
LIMIT = 40 * 1024 * 1024


def call(body, out_shape, in_specs, scratch=(), flops=1 << 20, size=1 << 17, name=None, limit=LIMIT, **rest):
    return pl.pallas_call(
        body,
        out_shape=out_shape,
        in_specs=in_specs,
        scratch_shapes=list(scratch),
        compiler_params=pltpu.CompilerParams(vmem_limit_bytes=limit),
        cost_estimate=pl.CostEstimate(flops=flops, bytes_accessed=size, transcendentals=0),
        name=name,
        **rest,
    )


def exchange(rows, axes):
    return lax.all_to_all(rows, axes, 0, 0, tiled=True)


def message(peers, rows):
    return jax.ShapeDtypeStruct((peers, rows, LANES), bf16)


def per_device(features, conv_weight, bias, blend_profile, tile_ids, reward_grad):
    chunk = 1024
    conv_flops = 2 * STACK * TIN * CH * PIX
    own = lax.axis_index(("y", "z", "c")).reshape(1).astype(jnp.int32)
    feats = jnp.transpose(features[0, 0], (1, 0, 2))
    args = (feats, conv_weight, bias, reward_grad[0, 0], tile_ids, blend_profile)
    here = [pltpu.with_memory_space_constraint(x, pltpu.HBM) for x in args]
    rows, route, mats, before, after, ratio, feats_held = call(
        functools.partial(conv_kernel, 2 * chunk),
        (
            pltpu.VMEM((PEERS, GRAD_ROWS + 8, LANES), bf16),
            pltpu.VMEM((3 * BOTH, BOTH), bf16),
            pltpu.VMEM((9 * SLOTS, SLOTS), bf16),
            pltpu.VMEM((8, LANES), f32),
            pltpu.VMEM((SLOTS, LANES), f32),
            pltpu.VMEM((ROWS, LANES), f32),
            pltpu.VMEM((TIN, CH, PIX), bf16),
        ),
        [HBM, HBM, HBM, HBM, HBM, HBM, SM],
        [
            pltpu.VMEM((TIN, TAPS, RGB, CH), bf16),
            pltpu.SMEM((RGB,), f32),
            pltpu.VMEM((RGB, PIX), bf16),
            pltpu.VMEM((1, SLOTS), jnp.int32),
            pltpu.SMEM((OV,), jnp.int32),
            pltpu.VMEM((TIN, STACK, CH), f32),
            pltpu.VMEM((STACK, PIX), f32),
            pltpu.VMEM((ROWS, 8, LANES), f32),
            pltpu.SemaphoreType.DMA((5,)),
            pltpu.SemaphoreType.DMA((PIX // (2 * chunk),)),
        ],
        conv_flops,
        1 << 22,
        "conv",
        out_specs=(VM,) * 7,
    )(*here, own)
    rows = exchange(rows, ("z", "c"))
    rows = call(
        route_kernel, message(PEERS, GRAD_ROWS + 16), [VM, VM], (), 1 << 27, 1 << 20, "route", out_specs=VM
    )(rows, route)
    rows = exchange(rows, ("y", "c"))
    rows, grad_rows = call(
        functools.partial(weight_grad_kernel, chunk),
        (message(PEERS, HALF + 8), jax.ShapeDtypeStruct((8, PIX), f32)),
        [VM, VM, VM, VM, VM, VM, SM],
        [pltpu.VMEM((STACK, PIX), f32), pltpu.VMEM((ROWS, 8, LANES), f32)],
        conv_flops,
        1 << 22,
        "weight_grad",
        out_specs=(VM, VM),
    )(rows, feats_held, ratio, mats, before, after, own)

    feature_rows = call(
        functools.partial(feature_grad_kernel, chunk),
        jax.ShapeDtypeStruct((TIN, CH, PIX), bf16),
        [
            pl.BlockSpec((8, PIX), lambda i: (0, 0)),
            pl.BlockSpec((TIN, TAPS, RGB, CH), lambda i: (0, 0, 0, 0)),
        ],
        [pltpu.VMEM((STACK, PIX), f32), pltpu.VMEM((TIN, STACK, CH), f32)],
        conv_flops,
        1 << 22,
        "feature_grad",
        grid=(PIX // chunk,),
        out_specs=pl.BlockSpec((TIN, CH, chunk), lambda i: (0, 0, i)),
    )(grad_rows, conv_weight)
    feature_grad = jnp.transpose(feature_rows, (1, 0, 2))[None, None]

    rows = exchange(rows, ("z", "c"))
    rows = call(sum_z_kernel, message(PEERS, HALF + 16), [VM], name="sum_z", out_specs=VM)(rows)
    rows = exchange(rows, ("y", "c"))
    decoded = call(
        decode_kernel,
        jax.ShapeDtypeStruct((RGB, PIX), bf16),
        [VM, SM],
        [pltpu.VMEM((ROWS, 8, LANES), f32)],
        name="decode",
        out_specs=VM,
    )(rows, own)
    rows = call(sum_y_kernel, message(4, 2 * HALF), [VM], name="sum_y", out_specs=VM)(rows)
    rows = exchange(rows, "clip")
    rows, decoded, feature_grad = lax.optimization_barrier((rows, decoded, feature_grad))
    scale = 1.0 / math.sqrt(4 * SLOTS * PIX)
    weight_grad, bias_grad = call(
        functools.partial(finish_kernel, scale),
        (
            jax.ShapeDtypeStruct((TIN, TAPS, RGB, CH), f32),
            jax.ShapeDtypeStruct((1, RGB), f32),
        ),
        [VM],
        [pltpu.VMEM((2 * HALF, LANES), f32), pltpu.VMEM((24, LANES), f32)],
        name="finish",
        out_specs=(VM, VM),
    )(rows)
    return (decoded[None, None], feature_grad, weight_grad, bias_grad.reshape(RGB))


def solution(mesh):
    parts = Mesh(mesh.devices.reshape(8, 8, 2, 4), ("y", "z", "c", "clip"))
    tile = ("y", "z", "c")
    return jax.shard_map(
        per_device,
        mesh=parts,
        in_specs=(
            P("clip", tile, None, None, None),
            P(),
            P(),
            P(),
            P("clip", None),
            P("clip", tile, None, None),
        ),
        out_specs=(P("clip", tile, None, None), P("clip", tile, None, None, None), P(), P()),
        check_vma=False,
    )
```

time: 87.7 us -> 82.8 us (0.944)
  waiting for transfers between devices: 3.9 us -> 0.47 us
  blocking collectives: 68.5 us -> 66.7 us
    all_to_all x1, waiting for transfers between devices: 3.9 us -> 0.47 us  [exchange(): return lax.all_to_all(rows, axes, 0, 0, tiled=True)]
    all_to_all x4, blocking collectives: 68.5 us -> 66.7 us  [exchange(): return lax.all_to_all(rows, axes, 0, 0, tiled=True)]
  transfers between devices with their start and end apart: 1 -> 1, of which waited for: 1 -> 1; matrix products, arithmetic and copies ran while one was open for 0% -> 0% of each run, Pallas kernels for 4% -> 5%
where the time goes in v4:
time: 82.8 us; the launch traced here: 82.4 us
  blocking collectives  66.7 us (81%)
  Pallas kernels  10.6 us (13%)
  starting transfers between devices  4.01 us (5%)
    all_to_all x4, blocking collectives, exchange(): return lax.all_to_all(rows, axes, 0, 0, tiled=True)  66.7 us
    all_to_all x1, starting transfers between devices, exchange(): return lax.all_to_all(rows, axes, 0, 0, tiled=True)  4.01 us
    pallas_call x1, Pallas kernels, per_device(): call(functools.partial(feature_grad_kernel, chunk), jax.ShapeDtypeStruct(...  2.95 us
    pallas_call x1, Pallas kernels, per_device(): call(functools.partial(conv_kernel, 2 * chunk), (pltpu.VMEM((PEERS, GRAD_...  2.66 us
    pallas_call x1, Pallas kernels, per_device(): call(functools.partial(weight_grad_kernel, chunk), (message(PEERS, HALF +...  1.7 us
  transfers between devices with their start and end apart: 1, of which 1 were waited for; matrix products, arithmetic and copies ran while one was open for 0% of the time, Pallas kernels for 5%

profile of v4, /device:TPU:1, one launch (start us, length us, event | category | flops | bytes accessed | tf_op | source)
XLA Modules:
  0.0 82.4 jit_solution(12253353409732879502)
XLA Ops:
  0.6 2.7 %conv.1 = (bf16[16,56,128]{2,1,0:T(8,128)(2,1)S(1)}, bf16[768,256]{1,0:T(8,128)(2,1)S(1)}, bf16[1152,128]{1,0:T(8,128)(2,1)S(1)}, f32[8,128]{1,0:T(8,128)S(1)}, ...) custom-call(bf16[3,96,4096]{2,1,0:T(8,128)(2,1)} %bitcast.10, ...), custom_call_target="tpu_custom_call" | custom-call | flops 169869312 | bytes 4194304 | tf_op jit(solution)/shard_map/conv/pallas_call | solution.py:499
  3.3 22.7 %all_to_all.25.got_ref = bf16[16,56,128]{2,1,0:T(8,128)(2,1)S(1)} all-to-all(bf16[16,56,128]{2,1,0:T(8,128)(2,1)S(1)} %get-tuple-element.18), channel_id=1, replica_groups=mesh['y'=8,'z'=8,'c'=2,'clip'=4] {'z','c'}, dimensions={0} | all-to-all | bytes 458752 | tf_op jit(solution)/shard_map/all_to_all | solution.py:485
  26.0 0.5 route.1
  26.5 18.7 %all_to_all.26.got_ref = bf16[16,64,128]{2,1,0:T(8,128)(2,1)S(1)} all-to-all(bf16[16,64,128]{2,1,0:T(8,128)(2,1)S(1)} %route.1), channel_id=1, replica_groups=mesh['y'=8,'z'=8,'c'=2,'clip'=4] {'y','c'}, dimensions={0} | all-to-all | bytes 524288 | tf_op jit(solution)/shard_map/all_to_all | solution.py:485
  45.2 0.0 copy-start
  45.2 1.7 %weight_grad.1 = (bf16[16,40,128]{2,1,0:T(8,128)(2,1)S(1)}, f32[8,4096]{1,0:T(8,128)S(1)}) custom-call(bf16[16,64,128]{2,1,0:T(8,128)(2,1)S(1)} %all_to_all.26.got_ref, bf16[3,96,4096]{2,1,0:T(8,128)(2,1)S(1)} %get-tuple-element.20.feat_ref, f32[32,128]{1,0:T(8,128)S(1)} %get-tuple-element.21.ratio_ref, bf16[1152,128]{1,0:T(8,128)(2,1)S(1)} %get-tuple-element.22.mats_ref, ...), custom_call_target="tpu_custom_call" | custom-call | flops 169869312 | bytes 4194304 | tf_op jit(solution)/shard_map/weight_grad/pallas_call | solution.py:533
  47.0 12.3 %all_to_all.27.got_ref = bf16[16,40,128]{2,1,0:T(8,128)(2,1)S(1)} all-to-all(bf16[16,40,128]{2,1,0:T(8,128)(2,1)S(1)} %get-tuple-element.25), channel_id=1, replica_groups=mesh['y'=8,'z'=8,'c'=2,'clip'=4] {'z','c'}, dimensions={0} | all-to-all | bytes 327680 | tf_op jit(solution)/shard_map/all_to_all | solution.py:485
  59.3 0.2 sum_z.1
  59.4 13.0 %all_to_all.28.got_ref = bf16[16,48,128]{2,1,0:T(8,128)(2,1)S(1)} all-to-all(bf16[16,48,128]{2,1,0:T(8,128)(2,1)S(1)} %sum_z.1), channel_id=1, replica_groups=mesh['y'=8,'z'=8,'c'=2,'clip'=4] {'y','c'}, dimensions={0} | all-to-all | bytes 393216 | tf_op jit(solution)/shard_map/all_to_all | solution.py:485
  72.4 0.8 sum_y.1
  73.2 4.0 %all-to-all-start.4 = ((bf16[4,64,128]{2,1,0:T(8,128)(2,1)}), bf16[4,64,128]{2,1,0:T(8,128)(2,1)S(1)}, u32[]{:S(2)}, u32[]{:S(2)}) async-start(bf16[4,64,128]{2,1,0:T(8,128)(2,1)} %sum_y.1), calls=%async_computation.4 | async-start | bytes 131072 | tf_op jit(solution)/shard_map/all_to_all | solution.py:485
  77.2 0.0 copy-done
  77.2 3.0 %feature_grad.1 = bf16[3,96,4096]{2,1,0:T(8,128)(2,1)} custom-call(f32[8,4096]{1,0:T(8,128)S(1)} %get-tuple-element.26.grad_ref, bf16[3,9,3,96]{3,2,1,0:T(4,128)(2,1)S(1)} %copy-done), custom_call_target="tpu_custom_call" | custom-call | flops 169869312 | bytes 4194304 | tf_op jit(solution)/shard_map/feature_grad/pallas_call | solution.py:544
  80.2 1.1 %decode.1 = bf16[3,4096]{1,0:T(4,128)(2,1)} custom-call(bf16[16,48,128]{2,1,0:T(8,128)(2,1)S(1)} %all_to_all.28.got_ref, s32[1]{0:T(128)} %bitcast.3.own_ref), custom_call_target="tpu_custom_call" | custom-call | flops 1048576 | bytes 131072 | tf_op jit(solution)/shard_map/decode/pallas_call | solution.py:563
  81.3 0.5 all-to-all-done.4.got_ref
  81.7 0.7 finish.1
Async XLA Ops:
  45.2 32.0 %copy-start = (bf16[3,9,3,96]{3,2,1,0:T(4,128)(2,1)S(1)}, bf16[3,9,3,96]{3,2,1,0:T(4,128)(2,1)}, u32[]{:S(2)}) copy-start(bf16[3,9,3,96]{3,2,1,0:T(4,128)(2,1)} %weight_ref.1) | copy-start | bytes 46660
  73.2 8.5 %all-to-all-start.4 = ((bf16[4,64,128]{2,1,0:T(8,128)(2,1)}), bf16[4,64,128]{2,1,0:T(8,128)(2,1)S(1)}, u32[]{:S(2)}, u32[]{:S(2)}) async-start(bf16[4,64,128]{2,1,0:T(8,128)(2,1)} %sum_y.1), calls=%async_computation.4 | async-start | bytes 131072 | tf_op jit(solution)/shard_map/all_to_all | solution.py:485

commit v5 on v4

--- a/solution.py
+++ b/solution.py
@@ -91,9 +91,18 @@
         mats_ref[n * BOTH : (n + 1) * BOTH, :] = onehot(have == key)
 
 
-def class_prep(ids, profile_ref, k, mats_ref, before_ref, after_ref):
+def class_prep(ids, profile_ref, y, z, c, mats_ref, before_ref, after_ref):
+    k = (2 * z + c) * 8 + y
     place = iota((SLOTS, SLOTS), 0)
-    spread = iota((SLOTS, SLOTS), 1) == (place % 8) * 16 + place // 8
+    leaves = (4 * (((place // 8) % 2) ^ c) + place % 4) * 16 + (place // 16) * 2 + (place // 4) % 2
+    spread = iota((SLOTS, SLOTS), 1) == leaves
+    place = iota((SLOTS, SLOTS), 1)
+    comes = (place // 16) * 16 + (place % 8) * 2 + (((place // 8) % 2) ^ (y // 4))
+    come = jnp.dot(
+        jnp.broadcast_to(ids, (8, SLOTS)).astype(bf16),
+        onehot(iota((SLOTS, SLOTS), 0) == comes),
+        preferred_element_type=f32,
+    )[0:1]
     own = jnp.sum(jnp.where(spread, jnp.broadcast_to(ids, (SLOTS, SLOTS)), 0.0), axis=1, keepdims=True)
     row = jnp.floor(own * (1.0 / TX))
     col = own - row * TX
@@ -101,7 +110,7 @@
     left = jnp.where(col > 0.5, own - 1.0, -9999.0)
     n = 0
     for key in (own, left, right):
-        gap = ids - key
+        gap = come - key
         for step in (0.0, -float(TX), float(TX)):
             mats_ref[n * SLOTS : (n + 1) * SLOTS, :] = onehot(gap == step)
             n += 1
@@ -140,13 +149,15 @@
     ratio_ref[...] = fx * fy / ((fx + col_there * fx_other) * (fy + row_there * fy_other))
 
 
-def swap_rows(slabs):
+def pass_on(slabs, core):
     block = jnp.concatenate(slabs, axis=0)
-    row = iota((SLOTS, SLOTS), 0)
-    return pick_rows(iota((SLOTS, SLOTS), 1) == (row % 16) * 8 + row // 16, block)
-
-
-def route_kernel(got_ref, mats_ref, out_ref):
+    place = iota((SLOTS, SLOTS), 0)
+    y = place // 16
+    peer = (place % 8) * 2 + (core ^ (y // 4))
+    return pick_rows(iota((SLOTS, SLOTS), 1) == peer * 8 + ((place // 8) % 2) * 4 + y % 4, block)
+
+
+def route_kernel(got_ref, mats_ref, own_ref, out_ref):
     slabs = [got_ref[p].astype(f32) for p in range(PEERS)]
     east = iota((BOTH, LANES), 1) % EDGE >= OV
     totals = []
@@ -157,10 +168,10 @@
         ]
         side = jnp.where(east, pltpu.roll(part[2], OV, 1), pltpu.roll(part[1], LANES - OV, 1))
         totals.append(part[0] + side)
-    images = swap_rows([slab[GRAD_ROWS : GRAD_ROWS + 8] for slab in slabs])
+    images = pass_on([slab[GRAD_ROWS : GRAD_ROWS + 8] for slab in slabs], own_ref[0] % 2)
     for t in range(PEERS):
         rows = [total[t * 16 : t * 16 + 16] for total in totals]
-        rows.append(images[(t // 2) * 16 : (t // 2) * 16 + 16])
+        rows.append(images[t * 8 : t * 8 + 8])
         out_ref[t] = jnp.concatenate(rows, axis=0).astype(bf16)
 
 
@@ -207,6 +218,7 @@
     after_ref,
     ratio_ref,
     feats,
+    stacked_ref,
     weight_ref,
     bias_ref,
     grad_ref,
@@ -231,11 +243,13 @@
         move.wait()
     stack_weights(weight_ref, held)
     kernels = [held[t].astype(bf16) for t in range(TIN)]
+    for t in range(TIN):
+        stacked_ref[t] = kernels[t]
     ids = ids_ref[...].astype(f32)
     own = own_ref[0]
     y, z, c = own // 16, (own // 2) % 8, own % 2
     route_prep(ids, y, z, route_ref)
-    class_prep(ids, profile_ref, (2 * z + c) * 8 + y, mats_ref, before_ref, after_ref)
+    class_prep(ids, profile_ref, y, z, c, mats_ref, before_ref, after_ref)
     ratio_prep(ids, profile_ref, own, ratio_ref)
     taps[0:8, :] = jnp.zeros((8, PIX), f32)
     taps[0:RGB, :] = grad_ref[...].astype(f32)
@@ -276,7 +290,8 @@
     for r in range(ROWS):
         turned[r] = image[:, r * LANES : (r + 1) * LANES]
     place = iota((LANES, LANES), 0)
-    lanes = onehot(iota((LANES, LANES), 1) == ((place // 32) % 2) * 64 + (place // 64) * 32 + place % 32)
+    k = (((place // 16) % 4) * 2 + (place // 4) % 2) * 8 + 4 * (((place // 8) % 2) ^ c) + place % 4
+    lanes = onehot(iota((LANES, LANES), 1) == (k // 32) * 64 + (place // 64) * 32 + k % 32)
     classes = []
     for h in range(2):
         block = half_rows(turned, h, RGB) + [jnp.zeros((16, LANES), f32)]
@@ -321,7 +336,7 @@
 
 
 def weight_grad_kernel(
-    chunk, got_ref, feat_ref, ratio_ref, mats_ref, before_ref, after_ref, own_ref, out_ref, grad_ref, taps, turned
+    chunk, got_ref, feat_ref, ratio_ref, mats_ref, before_ref, after_ref, out_ref, stack_ref, taps, turned
 ):
     sums = [got_ref[h].astype(f32) for h in range(2)]
     for n in range(2, PEERS):
@@ -333,12 +348,9 @@
                 at = qy * 16 + h * 8
                 piece = sums[h][o * 16 + qy * 8 : o * 16 + qy * 8 + 8] * ratio_ref[at : at + 8, :]
                 turned[at : at + 8, o, :] = piece.astype(bf16).astype(f32)
-    for r in range(ROWS):
-        grad_ref[:, r * LANES : (r + 1) * LANES] = turned[r]
-    core = own_ref[0] % 2
-    images = [got_ref[2 * y + core].astype(f32)[GRAD_ROWS : GRAD_ROWS + 16] for y in range(8)]
+    grad = jnp.concatenate([turned[r] for r in range(ROWS)], axis=1)
+    images = [got_ref[n].astype(f32)[GRAD_ROWS : GRAD_ROWS + 8] for n in range(PEERS)]
     blended = blend_classes(jnp.concatenate(images, axis=0), mats_ref, before_ref, after_ref)
-    grad = grad_ref[...]
     grad_stack(grad, taps)
     bias = lax.dot_general(
         jnp.ones((8, PIX), bf16), grad.astype(bf16), (((1,), (1,)), ((), ())), preferred_element_type=f32
@@ -346,6 +358,7 @@
     total = jnp.zeros((TIN * CH, STACK), f32)
     for at in range(0, PIX, chunk):
         part = taps[:, at : at + chunk].astype(bf16)
+        stack_ref[:, at : at + chunk] = part
         total += lax.dot_general(
             feat_ref[:, :, at : at + chunk].reshape(TIN * CH, chunk),
             part,
@@ -381,28 +394,19 @@
         out_ref[p] = jnp.concatenate([halves[p % 2], blended[p * 8 : p * 8 + 8]], axis=0).astype(bf16)
 
 
-def feature_grad_kernel(chunk, grad_ref, weight_ref, out_ref, taps, held):
-    step = pl.program_id(0)
-
-    @pl.when(step == 0)
-    def _():
-        stack_weights(weight_ref, held)
-        grad_stack(grad_ref[...], taps)
-
-    part = taps[:, pl.ds(pl.multiple_of(step * chunk, chunk), chunk)].astype(bf16)
+def feature_grad_kernel(stack_ref, weight_ref, out_ref):
     for t in range(TIN):
         out_ref[t] = lax.dot_general(
-            held[t].astype(bf16), part, (((0,), (0,)), ((), ())), preferred_element_type=f32
+            weight_ref[t], stack_ref[...], (((0,), (0,)), ((), ())), preferred_element_type=f32
         ).astype(bf16)
 
 
 def decode_kernel(got_ref, own_ref, image_ref, turned):
-    core = own_ref[0] % 2
-    images = jnp.concatenate([got_ref[2 * y + core].astype(f32)[HALF : HALF + 16] for y in range(8)], axis=0)
+    images = jnp.concatenate([got_ref[n].astype(f32)[HALF : HALF + 8] for n in range(PEERS)], axis=0)
     block = jnp.concatenate([images[:, 0:64], images[:, 64:128]], axis=0).astype(bf16)
     row = iota((BOTH, LANES), 0)
     lane = iota((BOTH, LANES), 1)
-    k = (row % 16) * 8 + (row // 16) % 8
+    k = ((row % 8) * 2 + (((row // 8) % 2) ^ (own_ref[0] // 64))) * 8 + (row // 16) % 8
     spot = ((k // 32) % 2) * 64 + (row // SLOTS) * 32 + k % 32
     for h in range(2):
         lanes = onehot((lane == spot) & (k // 64 == h))
@@ -414,15 +418,15 @@
         image_ref[:, r * LANES : (r + 1) * LANES] = turned[r, 0:RGB, :].astype(bf16)
 
 
-def sum_z_kernel(got_ref, out_ref):
+def sum_z_kernel(got_ref, own_ref, out_ref):
     slabs = [got_ref[p].astype(f32) for p in range(PEERS)]
     half = slabs[0][0:HALF]
     for slab in slabs[1:]:
         half = half + slab[0:HALF]
     half = split_bias(half)
-    images = swap_rows([slab[HALF : HALF + 8] for slab in slabs])
+    images = pass_on([slab[HALF : HALF + 8] for slab in slabs], own_ref[0] % 2)
     for t in range(PEERS):
-        out_ref[t] = jnp.concatenate([half, images[(t // 2) * 16 : (t // 2) * 16 + 16]], axis=0).astype(bf16)
+        out_ref[t] = jnp.concatenate([half, images[t * 8 : t * 8 + 8]], axis=0).astype(bf16)
 
 
 def sum_y_kernel(got_ref, out_ref):
@@ -496,7 +500,7 @@
     feats = jnp.transpose(features[0, 0], (1, 0, 2))
     args = (feats, conv_weight, bias, reward_grad[0, 0], tile_ids, blend_profile)
     here = [pltpu.with_memory_space_constraint(x, pltpu.HBM) for x in args]
-    rows, route, mats, before, after, ratio, feats_held = call(
+    rows, route, mats, before, after, ratio, feats_held, weights_held = call(
         functools.partial(conv_kernel, 2 * chunk),
         (
             pltpu.VMEM((PEERS, GRAD_ROWS + 8, LANES), bf16),
@@ -506,6 +510,7 @@
             pltpu.VMEM((SLOTS, LANES), f32),
             pltpu.VMEM((ROWS, LANES), f32),
             pltpu.VMEM((TIN, CH, PIX), bf16),
+            pltpu.VMEM((TIN, STACK, CH), bf16),
         ),
         [HBM, HBM, HBM, HBM, HBM, HBM, SM],
         [
@@ -523,42 +528,42 @@
         conv_flops,
         1 << 22,
         "conv",
-        out_specs=(VM,) * 7,
+        out_specs=(VM,) * 8,
     )(*here, own)
     rows = exchange(rows, ("z", "c"))
     rows = call(
-        route_kernel, message(PEERS, GRAD_ROWS + 16), [VM, VM], (), 1 << 27, 1 << 20, "route", out_specs=VM
-    )(rows, route)
+        route_kernel, message(PEERS, GRAD_ROWS + 8), [VM, VM, SM], (), 1 << 27, 1 << 20, "route", out_specs=VM
+    )(rows, route, own)
     rows = exchange(rows, ("y", "c"))
-    rows, grad_rows = call(
+    rows, stack = call(
         functools.partial(weight_grad_kernel, chunk),
-        (message(PEERS, HALF + 8), jax.ShapeDtypeStruct((8, PIX), f32)),
-        [VM, VM, VM, VM, VM, VM, SM],
+        (message(PEERS, HALF + 8), jax.ShapeDtypeStruct((STACK, PIX), bf16)),
+        [VM, VM, VM, VM, VM, VM],
         [pltpu.VMEM((STACK, PIX), f32), pltpu.VMEM((ROWS, 8, LANES), f32)],
         conv_flops,
         1 << 22,
         "weight_grad",
         out_specs=(VM, VM),
-    )(rows, feats_held, ratio, mats, before, after, own)
+    )(rows, feats_held, ratio, mats, before, after)
 
     feature_rows = call(
-        functools.partial(feature_grad_kernel, chunk),
+        feature_grad_kernel,
         jax.ShapeDtypeStruct((TIN, CH, PIX), bf16),
         [
-            pl.BlockSpec((8, PIX), lambda i: (0, 0)),
-            pl.BlockSpec((TIN, TAPS, RGB, CH), lambda i: (0, 0, 0, 0)),
+            pl.BlockSpec((STACK, chunk), lambda i: (0, i)),
+            pl.BlockSpec((TIN, STACK, CH), lambda i: (0, 0, 0)),
         ],
-        [pltpu.VMEM((STACK, PIX), f32), pltpu.VMEM((TIN, STACK, CH), f32)],
+        (),
         conv_flops,
         1 << 22,
         "feature_grad",
         grid=(PIX // chunk,),
         out_specs=pl.BlockSpec((TIN, CH, chunk), lambda i: (0, 0, i)),
-    )(grad_rows, conv_weight)
+    )(stack, weights_held)
     feature_grad = jnp.transpose(feature_rows, (1, 0, 2))[None, None]
 
     rows = exchange(rows, ("z", "c"))
-    rows = call(sum_z_kernel, message(PEERS, HALF + 16), [VM], name="sum_z", out_specs=VM)(rows)
+    rows = call(sum_z_kernel, message(PEERS, HALF + 8), [VM, SM], name="sum_z", out_specs=VM)(rows, own)
     rows = exchange(rows, ("y", "c"))
     decoded = call(
         decode_kernel,

time: 82.8 us -> 81.6 us (0.986)
  blocking collectives: 66.7 us -> 65.3 us
    all_to_all x4, blocking collectives: 66.7 us -> 65.3 us  [exchange(): return lax.all_to_all(rows, axes, 0, 0, tiled=True)]
where the time goes in v5:
time: 81.6 us; the launch traced here: 81.2 us
  blocking collectives  65.3 us (80%)
  Pallas kernels  10.4 us (13%)
  starting transfers between devices  4.02 us (5%)
    all_to_all x4, blocking collectives, exchange(): return lax.all_to_all(rows, axes, 0, 0, tiled=True)  65.3 us
    all_to_all x1, starting transfers between devices, exchange(): return lax.all_to_all(rows, axes, 0, 0, tiled=True)  4.02 us
    pallas_call x1, Pallas kernels, per_device(): call(feature_grad_kernel, jax.ShapeDtypeStruct((TIN, CH, PIX), bf16), [pl...  2.69 us
    pallas_call x1, Pallas kernels, per_device(): call(functools.partial(conv_kernel, 2 * chunk), (pltpu.VMEM((PEERS, GRAD_...  2.69 us
    pallas_call x1, Pallas kernels, per_device(): call(functools.partial(weight_grad_kernel, chunk), (message(PEERS, HALF +...  1.73 us
  transfers between devices with their start and end apart: 1, of which 1 were waited for; matrix products, arithmetic and copies ran while one was open for 0% of the time, Pallas kernels for 5%

profile of v5, /device:TPU:1, one launch (start us, length us, event | category | flops | bytes accessed | tf_op | source)
XLA Modules:
  0.0 81.2 jit_solution(18337534680420593685)
XLA Ops:
  0.6 2.7 %conv.1 = (bf16[16,56,128]{2,1,0:T(8,128)(2,1)S(1)}, bf16[768,256]{1,0:T(8,128)(2,1)S(1)}, bf16[1152,128]{1,0:T(8,128)(2,1)S(1)}, f32[8,128]{1,0:T(8,128)S(1)}, ...) custom-call(bf16[3,96,4096]{2,1,0:T(8,128)(2,1)} %bitcast.10, ...), custom_call_target="tpu_custom_call" | custom-call | flops 169869312 | bytes 4194304 | tf_op jit(solution)/shard_map/conv/pallas_call | solution.py:503
  3.3 22.7 %all_to_all.25.got_ref = bf16[16,56,128]{2,1,0:T(8,128)(2,1)S(1)} all-to-all(bf16[16,56,128]{2,1,0:T(8,128)(2,1)S(1)} %get-tuple-element.19), channel_id=1, replica_groups=mesh['y'=8,'z'=8,'c'=2,'clip'=4] {'z','c'}, dimensions={0} | all-to-all | bytes 458752 | tf_op jit(solution)/shard_map/all_to_all | solution.py:489
  26.0 0.5 route.1
  26.5 18.1 %all_to_all.26.got_ref = bf16[16,56,128]{2,1,0:T(8,128)(2,1)S(1)} all-to-all(bf16[16,56,128]{2,1,0:T(8,128)(2,1)S(1)} %route.1), channel_id=1, replica_groups=mesh['y'=8,'z'=8,'c'=2,'clip'=4] {'y','c'}, dimensions={0} | all-to-all | bytes 458752 | tf_op jit(solution)/shard_map/all_to_all | solution.py:489
  44.6 1.7 %weight_grad.1 = (bf16[16,40,128]{2,1,0:T(8,128)(2,1)S(1)}, bf16[72,4096]{1,0:T(8,128)(2,1)S(1)}) custom-call(bf16[16,56,128]{2,1,0:T(8,128)(2,1)S(1)} %all_to_all.26.got_ref, bf16[3,96,4096]{2,1,0:T(8,128)(2,1)S(1)} %get-tuple-element.21.feat_ref, f32[32,128]{1,0:T(8,128)S(1)} %get-tuple-element.22.ratio_ref, ...), custom_call_target="tpu_custom_call" | custom-call | flops 169869312 | bytes 4194304 | tf_op jit(solution)/shard_map/weight_grad/pallas_call | solution.py:538
  46.4 12.3 %all_to_all.27.got_ref = bf16[16,40,128]{2,1,0:T(8,128)(2,1)S(1)} all-to-all(bf16[16,40,128]{2,1,0:T(8,128)(2,1)S(1)} %get-tuple-element.26), channel_id=1, replica_groups=mesh['y'=8,'z'=8,'c'=2,'clip'=4] {'z','c'}, dimensions={0} | all-to-all | bytes 327680 | tf_op jit(solution)/shard_map/all_to_all | solution.py:489
  58.6 0.2 sum_z.1
  58.8 12.3 %all_to_all.28.got_ref = bf16[16,40,128]{2,1,0:T(8,128)(2,1)S(1)} all-to-all(bf16[16,40,128]{2,1,0:T(8,128)(2,1)S(1)} %sum_z.1), channel_id=1, replica_groups=mesh['y'=8,'z'=8,'c'=2,'clip'=4] {'y','c'}, dimensions={0} | all-to-all | bytes 327680 | tf_op jit(solution)/shard_map/all_to_all | solution.py:489
  71.1 0.8 sum_y.1
  71.9 4.0 %all-to-all-start.4 = ((bf16[4,64,128]{2,1,0:T(8,128)(2,1)}), bf16[4,64,128]{2,1,0:T(8,128)(2,1)S(1)}, u32[]{:S(2)}, u32[]{:S(2)}) async-start(bf16[4,64,128]{2,1,0:T(8,128)(2,1)} %sum_y.1), calls=%async_computation.4 | async-start | bytes 131072 | tf_op jit(solution)/shard_map/all_to_all | solution.py:489
  75.9 2.7 %feature_grad.1 = bf16[3,96,4096]{2,1,0:T(8,128)(2,1)} custom-call(bf16[72,4096]{1,0:T(8,128)(2,1)S(1)} %get-tuple-element.27.stack_ref, bf16[3,72,96]{2,1,0:T(8,128)(2,1)S(1)} %get-tuple-element.28.weight_ref), custom_call_target="tpu_custom_call" | custom-call | flops 169869312 | bytes 4194304 | tf_op jit(solution)/shard_map/feature_grad/pallas_call | solution.py:549
  78.6 1.1 %decode.1 = bf16[3,4096]{1,0:T(4,128)(2,1)} custom-call(bf16[16,40,128]{2,1,0:T(8,128)(2,1)S(1)} %all_to_all.28.got_ref, s32[1]{0:T(128)} %bitcast.3.own_ref), custom_call_target="tpu_custom_call" | custom-call | flops 1048576 | bytes 131072 | tf_op jit(solution)/shard_map/decode/pallas_call | solution.py:568
  79.7 0.8 all-to-all-done.4.got_ref
  80.5 0.7 finish.1
Async XLA Ops:
  71.9 8.6 %all-to-all-start.4 = ((bf16[4,64,128]{2,1,0:T(8,128)(2,1)}), bf16[4,64,128]{2,1,0:T(8,128)(2,1)S(1)}, u32[]{:S(2)}, u32[]{:S(2)}) async-start(bf16[4,64,128]{2,1,0:T(8,128)(2,1)} %sum_y.1), calls=%async_computation.4 | async-start | bytes 131072 | tf_op jit(solution)/shard_map/all_to_all | solution.py:489

commit v6 on v5

--- a/solution.py
+++ b/solution.py
@@ -23,18 +23,20 @@
 BOTH = 2 * SLOTS
 TAPS = 9
 STACK = TAPS * 8
-HALF = 32
-MAIN = 30
-BIAS_ROW = 30
+PARTS = 4
+PART = 16
+MAIN = 15
+BIAS_ROW = 15
 
 BOTH = 2 * SLOTS
 TAPS = 9
 STACK = TAPS * 8
 PEERS = 16
 GRAD_ROWS = RGB * 16
-HALF = 32
-MAIN = 30
-BIAS_ROW = 30
+PARTS = 4
+PART = 16
+MAIN = 15
+BIAS_ROW = 15
 
 f32 = jnp.float32
 bf16 = jnp.bfloat16
@@ -325,14 +327,14 @@
             taps[tap * 8 : tap * 8 + 8, :] = moved
 
 
-def split_bias(half):
-    at = iota((HALF, LANES), 0) == BIAS_ROW
-    lane = iota((HALF, LANES), 1)
-    total = half + pltpu.roll(half, LANES - RGB, 1)
+def split_bias(part):
+    at = iota((PART, LANES), 0) == BIAS_ROW
+    lane = iota((PART, LANES), 1)
+    total = part + pltpu.roll(part, LANES - RGB, 1)
     high = total.astype(bf16).astype(f32)
     low = pltpu.roll(total - high, RGB, 1)
-    pair = jnp.where(lane < RGB, high, jnp.where(lane < 2 * RGB, low, half))
-    return jnp.where(at, pair, half)
+    pair = jnp.where(lane < RGB, high, jnp.where(lane < 2 * RGB, low, part))
+    return jnp.where(at, pair, part)
 
 
 def weight_grad_kernel(
@@ -367,31 +369,27 @@
         )
     rows = jnp.concatenate([total[t * CH : (t + 1) * CH].T for t in range(TIN)], axis=0)
     rows = jnp.concatenate([rows, jnp.zeros((TIN * STACK, LANES - CH), f32)], axis=1).astype(bf16)
-    place = iota((4 * HALF, TIN * STACK), 0)
-    source = iota((4 * HALF, TIN * STACK), 1)
+    every = PARTS * PART
+    place = iota((2 * every, TIN * STACK), 0)
+    source = iota((2 * every, TIN * STACK), 1)
     rank = jnp.where(source % 8 < RGB, (source // 8) * RGB + source % 8, -1)
-    within = place % HALF
-    main = (rank == (place // HALF) * MAIN + within) & (within < MAIN) & (place < 2 * HALF)
-    offset = place - 2 * HALF - RGB * (rank - 2 * MAIN)
-    side = (offset >= 0) & (offset < RGB) & (place >= 2 * HALF) & (rank >= 2 * MAIN)
-    pick = jnp.where(main | side, 1.0, 0.0).astype(bf16)
-    chosen = jnp.dot(pick, rows, preferred_element_type=f32)
+    within = place % PART
+    main = (rank == (place // PART) * MAIN + within) & (within < MAIN) & (place < every)
+    offset = place - every - RGB * (rank - PARTS * MAIN)
+    side = (offset >= 0) & (offset < RGB) & (place >= every) & (rank >= PARTS * MAIN)
+    chosen = jnp.dot(onehot(main | side), rows, preferred_element_type=f32)
     bias_wide = jnp.concatenate([bias, jnp.zeros((8, LANES - 8), f32)], axis=1)[0:1]
     bias_wide = jnp.where(iota((1, LANES), 1) < RGB, bias_wide, 0.0)
-    lane = iota((HALF, LANES), 1)
-    at_bias = (iota((HALF, LANES), 0) == BIAS_ROW) & (lane < CH)
-    halves = []
-    for h in range(2):
-        front = chosen[h * HALF : (h + 1) * HALF]
-        back = chosen[(2 + h) * HALF : (3 + h) * HALF]
-        third = (h * HALF + iota((HALF, LANES), 0)) % 3
-        tail = jnp.zeros((HALF, LANES), f32)
-        for c in range(3):
-            tail = jnp.where(third == c, pltpu.roll(back, CH - 32 * c, 1), tail)
-        half = jnp.where(at_bias, bias_wide, jnp.where(lane < CH, front, tail))
-        halves.append(split_bias(half))
+    lane = iota((every, LANES), 1)
+    third = iota((every, LANES), 0) % 3
+    tail = jnp.zeros((every, LANES), f32)
+    for c in range(3):
+        tail = jnp.where(third == c, pltpu.roll(chosen[every:], CH - 32 * c, 1), tail)
+    packed = jnp.where(lane < CH, chosen[:every], tail)
+    packed = jnp.where((iota((every, LANES), 0) % PART == BIAS_ROW) & (lane < CH), bias_wide, packed)
+    parts = [split_bias(packed[q * PART : (q + 1) * PART]) for q in range(PARTS)]
     for p in range(PEERS):
-        out_ref[p] = jnp.concatenate([halves[p % 2], blended[p * 8 : p * 8 + 8]], axis=0).astype(bf16)
+        out_ref[p] = jnp.concatenate([parts[p % PARTS], blended[p * 8 : p * 8 + 8]], axis=0).astype(bf16)
 
 
 def feature_grad_kernel(stack_ref, weight_ref, out_ref):
@@ -402,7 +400,7 @@
 
 
 def decode_kernel(got_ref, own_ref, image_ref, turned):
-    images = jnp.concatenate([got_ref[n].astype(f32)[HALF : HALF + 8] for n in range(PEERS)], axis=0)
+    images = jnp.concatenate([got_ref[n].astype(f32)[PART : PART + 8] for n in range(PEERS)], axis=0)
     block = jnp.concatenate([images[:, 0:64], images[:, 64:128]], axis=0).astype(bf16)
     row = iota((BOTH, LANES), 0)
     lane = iota((BOTH, LANES), 1)
@@ -420,35 +418,36 @@
 
 def sum_z_kernel(got_ref, own_ref, out_ref):
     slabs = [got_ref[p].astype(f32) for p in range(PEERS)]
-    half = slabs[0][0:HALF]
+    part = slabs[0][0:PART]
     for slab in slabs[1:]:
-        half = half + slab[0:HALF]
-    half = split_bias(half)
-    images = pass_on([slab[HALF : HALF + 8] for slab in slabs], own_ref[0] % 2)
+        part = part + slab[0:PART]
+    part = split_bias(part)
+    images = pass_on([slab[PART : PART + 8] for slab in slabs], own_ref[0] % 2)
     for t in range(PEERS):
-        out_ref[t] = jnp.concatenate([half, images[t * 8 : t * 8 + 8]], axis=0).astype(bf16)
+        out_ref[t] = jnp.concatenate([part, images[t * 8 : t * 8 + 8]], axis=0).astype(bf16)
 
 
 def sum_y_kernel(got_ref, out_ref):
-    halves = []
-    for h in range(2):
-        half = got_ref[h].astype(f32)[0:HALF]
+    parts = []
+    for c in range(2):
+        part = got_ref[c].astype(f32)[0:PART]
         for y in range(1, 8):
-            half = half + got_ref[2 * y + h].astype(f32)[0:HALF]
-        halves.append(split_bias(half))
-    both = jnp.concatenate(halves, axis=0).astype(bf16)
+            part = part + got_ref[2 * y + c].astype(f32)[0:PART]
+        parts.append(split_bias(part))
+    both = jnp.concatenate(parts, axis=0).astype(bf16)
     for n in range(out_ref.shape[0]):
         out_ref[n] = both
 
 
 def finish_kernel(scale, got_ref, weight_ref, bias_ref, held, others):
-    total = got_ref[0].astype(f32)
-    for n in range(1, got_ref.shape[0]):
-        total = total + got_ref[n].astype(f32)
-    held[...] = total * scale
+    for z in range(2):
+        total = got_ref[4 * z].astype(f32)
+        for n in range(1, 4):
+            total = total + got_ref[4 * z + n].astype(f32)
+        held[2 * PART * z : 2 * PART * (z + 1), :] = total * scale
     bias = held[BIAS_ROW : BIAS_ROW + 1, :]
     bias_ref[...] = bias[:, 0:RGB] + bias[:, RGB : 2 * RGB]
-    count = TIN * TAPS * RGB - 2 * MAIN
+    count = TIN * TAPS * RGB - PARTS * MAIN
     lane = iota((count, LANES), 1)
     tail = jnp.zeros((count, LANES), f32)
     for c in range(3):
@@ -457,11 +456,11 @@
     others[0:count, :] = tail
     for n in range(TIN * TAPS):
         at = n * RGB
-        if at < 2 * MAIN:
-            at = (at // MAIN) * HALF + at % MAIN
+        if at < PARTS * MAIN:
+            at = (at // MAIN) * PART + at % MAIN
             value = held[at : at + RGB, 0:CH]
         else:
-            at -= 2 * MAIN
+            at -= PARTS * MAIN
             value = others[at : at + RGB, 0:CH]
         weight_ref[n // TAPS, n % TAPS] = value
 
@@ -496,7 +495,7 @@
 def per_device(features, conv_weight, bias, blend_profile, tile_ids, reward_grad):
     chunk = 1024
     conv_flops = 2 * STACK * TIN * CH * PIX
-    own = lax.axis_index(("y", "z", "c")).reshape(1).astype(jnp.int32)
+    own = lax.axis_index(("y", "z_hi", "z_lo", "c")).reshape(1).astype(jnp.int32)
     feats = jnp.transpose(features[0, 0], (1, 0, 2))
     args = (feats, conv_weight, bias, reward_grad[0, 0], tile_ids, blend_profile)
     here = [pltpu.with_memory_space_constraint(x, pltpu.HBM) for x in args]
@@ -530,14 +529,14 @@
         "conv",
         out_specs=(VM,) * 8,
     )(*here, own)
-    rows = exchange(rows, ("z", "c"))
+    rows = exchange(rows, ("z_hi", "z_lo", "c"))
     rows = call(
         route_kernel, message(PEERS, GRAD_ROWS + 8), [VM, VM, SM], (), 1 << 27, 1 << 20, "route", out_specs=VM
     )(rows, route, own)
     rows = exchange(rows, ("y", "c"))
     rows, stack = call(
         functools.partial(weight_grad_kernel, chunk),
-        (message(PEERS, HALF + 8), jax.ShapeDtypeStruct((STACK, PIX), bf16)),
+        (message(PEERS, PART + 8), jax.ShapeDtypeStruct((STACK, PIX), bf16)),
         [VM, VM, VM, VM, VM, VM],
         [pltpu.VMEM((STACK, PIX), f32), pltpu.VMEM((ROWS, 8, LANES), f32)],
         conv_flops,
@@ -562,8 +561,8 @@
     )(stack, weights_held)
     feature_grad = jnp.transpose(feature_rows, (1, 0, 2))[None, None]
 
-    rows = exchange(rows, ("z", "c"))
-    rows = call(sum_z_kernel, message(PEERS, HALF + 8), [VM, SM], name="sum_z", out_specs=VM)(rows, own)
+    rows = exchange(rows, ("z_hi", "z_lo", "c"))
+    rows = call(sum_z_kernel, message(PEERS, PART + 8), [VM, SM], name="sum_z", out_specs=VM)(rows, own)
     rows = exchange(rows, ("y", "c"))
     decoded = call(
         decode_kernel,
@@ -573,8 +572,8 @@
         name="decode",
         out_specs=VM,
     )(rows, own)
-    rows = call(sum_y_kernel, message(4, 2 * HALF), [VM], name="sum_y", out_specs=VM)(rows)
-    rows = exchange(rows, "clip")
+    rows = call(sum_y_kernel, message(8, 2 * PART), [VM], name="sum_y", out_specs=VM)(rows)
+    rows = exchange(rows, ("z_lo", "clip"))
     rows, decoded, feature_grad = lax.optimization_barrier((rows, decoded, feature_grad))
     scale = 1.0 / math.sqrt(4 * SLOTS * PIX)
     weight_grad, bias_grad = call(
@@ -584,7 +583,7 @@
             jax.ShapeDtypeStruct((1, RGB), f32),
         ),
         [VM],
-        [pltpu.VMEM((2 * HALF, LANES), f32), pltpu.VMEM((24, LANES), f32)],
+        [pltpu.VMEM((PARTS * PART, LANES), f32), pltpu.VMEM((24, LANES), f32)],
         name="finish",
         out_specs=(VM, VM),
     )(rows)
@@ -592,8 +591,8 @@
 
 
 def solution(mesh):
-    parts = Mesh(mesh.devices.reshape(8, 8, 2, 4), ("y", "z", "c", "clip"))
-    tile = ("y", "z", "c")
+    parts = Mesh(mesh.devices.reshape(8, 4, 2, 2, 4), ("y", "z_hi", "z_lo", "c", "clip"))
+    tile = ("y", "z_hi", "z_lo", "c")
     return jax.shard_map(
         per_device,
         mesh=parts,

time: 81.6 us -> 79.9 us (0.979)
  blocking collectives: 65.3 us -> 63 us
    all_to_all x4, blocking collectives: 65.3 us -> 63 us  [exchange(): return lax.all_to_all(rows, axes, 0, 0, tiled=True)]
where the time goes in v6:
time: 79.9 us; the launch traced here: 79.5 us
  blocking collectives  63 us (79%)
  Pallas kernels  10.4 us (13%)
  starting transfers between devices  4.02 us (5%)
  waiting for transfers between devices  1.42 us (2%)
    all_to_all x4, blocking collectives, exchange(): return lax.all_to_all(rows, axes, 0, 0, tiled=True)  63 us
    all_to_all x1, starting transfers between devices, exchange(): return lax.all_to_all(rows, axes, 0, 0, tiled=True)  4.02 us
    pallas_call x1, Pallas kernels, per_device(): call(feature_grad_kernel, jax.ShapeDtypeStruct((TIN, CH, PIX), bf16), [pl...  2.7 us
    pallas_call x1, Pallas kernels, per_device(): call(functools.partial(conv_kernel, 2 * chunk), (pltpu.VMEM((PEERS, GRAD_...  2.68 us
    pallas_call x1, Pallas kernels, per_device(): call(functools.partial(weight_grad_kernel, chunk), (message(PEERS, PART +...  1.73 us
  transfers between devices with their start and end apart: 1, of which 1 were waited for; matrix products, arithmetic and copies ran while one was open for 0% of the time, Pallas kernels for 5%

profile of v6, /device:TPU:1, one launch (start us, length us, event | category | flops | bytes accessed | tf_op | source)
XLA Modules:
  0.0 79.5 jit_solution(467027044612721415)
XLA Ops:
  0.6 2.7 %conv.1 = (bf16[16,56,128]{2,1,0:T(8,128)(2,1)S(1)}, bf16[768,256]{1,0:T(8,128)(2,1)S(1)}, bf16[1152,128]{1,0:T(8,128)(2,1)S(1)}, f32[8,128]{1,0:T(8,128)S(1)}, ...) custom-call(bf16[3,96,4096]{2,1,0:T(8,128)(2,1)} %bitcast.10, ...), custom_call_target="tpu_custom_call" | custom-call | flops 169869312 | bytes 4194304 | tf_op jit(solution)/shard_map/conv/pallas_call | solution.py:502
  3.3 22.7 %all_to_all.25.got_ref = bf16[16,56,128]{2,1,0:T(8,128)(2,1)S(1)} all-to-all(bf16[16,56,128]{2,1,0:T(8,128)(2,1)S(1)} %get-tuple-element.19), channel_id=1, replica_groups=mesh['y'=8,'z_hi'=4,'z_lo'=2,'c'=2,'clip'=4] {'z_hi','z_lo','c'}, dimensions={0} | all-to-all | bytes 458752 | tf_op jit(solution)/shard_map/all_to_all | solution.py:488
  26.0 0.5 route.1
  26.5 18.1 %all_to_all.26.got_ref = bf16[16,56,128]{2,1,0:T(8,128)(2,1)S(1)} all-to-all(bf16[16,56,128]{2,1,0:T(8,128)(2,1)S(1)} %route.1), channel_id=1, replica_groups=mesh['y'=8,'z_hi'=4,'z_lo'=2,'c'=2,'clip'=4] {'y','c'}, dimensions={0} | all-to-all | bytes 458752 | tf_op jit(solution)/shard_map/all_to_all | solution.py:488
  44.6 1.7 %weight_grad.1 = (bf16[16,24,128]{2,1,0:T(8,128)(2,1)S(1)}, bf16[72,4096]{1,0:T(8,128)(2,1)S(1)}) custom-call(bf16[16,56,128]{2,1,0:T(8,128)(2,1)S(1)} %all_to_all.26.got_ref, bf16[3,96,4096]{2,1,0:T(8,128)(2,1)S(1)} %get-tuple-element.21.feat_ref, f32[32,128]{1,0:T(8,128)S(1)} %get-tuple-element.22.ratio_ref, ...), custom_call_target="tpu_custom_call" | custom-call | flops 169869312 | bytes 4194304 | tf_op jit(solution)/shard_map/weight_grad/pallas_call | solution.py:537
  46.3 11.1 %all_to_all.27.got_ref = bf16[16,24,128]{2,1,0:T(8,128)(2,1)S(1)} all-to-all(bf16[16,24,128]{2,1,0:T(8,128)(2,1)S(1)} %get-tuple-element.26), channel_id=1, replica_groups=mesh['y'=8,'z_hi'=4,'z_lo'=2,'c'=2,'clip'=4] {'z_hi','z_lo','c'}, dimensions={0} | all-to-all | bytes 196608 | tf_op jit(solution)/shard_map/all_to_all | solution.py:488
  57.5 0.2 sum_z.1
  57.7 11.1 %all_to_all.28.got_ref = bf16[16,24,128]{2,1,0:T(8,128)(2,1)S(1)} all-to-all(bf16[16,24,128]{2,1,0:T(8,128)(2,1)S(1)} %sum_z.1), channel_id=1, replica_groups=mesh['y'=8,'z_hi'=4,'z_lo'=2,'c'=2,'clip'=4] {'y','c'}, dimensions={0} | all-to-all | bytes 196608 | tf_op jit(solution)/shard_map/all_to_all | solution.py:488
  68.8 0.8 sum_y.1
  69.6 4.0 %all-to-all-start.4 = ((bf16[8,32,128]{2,1,0:T(8,128)(2,1)}), bf16[8,32,128]{2,1,0:T(8,128)(2,1)S(1)}, u32[]{:S(2)}, u32[]{:S(2)}) async-start(bf16[8,32,128]{2,1,0:T(8,128)(2,1)} %sum_y.1), calls=%async_computation.4 | async-start | bytes 131072 | tf_op jit(solution)/shard_map/all_to_all | solution.py:488
  73.6 2.7 %feature_grad.1 = bf16[3,96,4096]{2,1,0:T(8,128)(2,1)} custom-call(bf16[72,4096]{1,0:T(8,128)(2,1)S(1)} %get-tuple-element.27.stack_ref, bf16[3,72,96]{2,1,0:T(8,128)(2,1)S(1)} %get-tuple-element.28.weight_ref), custom_call_target="tpu_custom_call" | custom-call | flops 169869312 | bytes 4194304 | tf_op jit(solution)/shard_map/feature_grad/pallas_call | solution.py:548
  76.3 1.1 %decode.1 = bf16[3,4096]{1,0:T(4,128)(2,1)} custom-call(bf16[16,24,128]{2,1,0:T(8,128)(2,1)S(1)} %all_to_all.28.got_ref, s32[1]{0:T(128)} %bitcast.3.own_ref), custom_call_target="tpu_custom_call" | custom-call | flops 1048576 | bytes 131072 | tf_op jit(solution)/shard_map/decode/pallas_call | solution.py:567
  77.4 1.4 %all-to-all-done.4.got_ref = bf16[8,32,128]{2,1,0:T(8,128)(2,1)S(1)} async-done(((bf16[8,32,128]{2,1,0:T(8,128)(2,1)}), bf16[8,32,128]{2,1,0:T(8,128)(2,1)S(1)}, u32[]{:S(2)}, u32[]{:S(2)}) %all-to-all-start.4) | async-done | bytes 65568 | tf_op jit(solution)/shard_map/all_to_all | solution.py:488
  78.8 0.7 finish.1
Async XLA Ops:
  69.6 9.2 %all-to-all-start.4 = ((bf16[8,32,128]{2,1,0:T(8,128)(2,1)}), bf16[8,32,128]{2,1,0:T(8,128)(2,1)S(1)}, u32[]{:S(2)}, u32[]{:S(2)}) async-start(bf16[8,32,128]{2,1,0:T(8,128)(2,1)} %sum_y.1), calls=%async_computation.4 | async-start | bytes 131072 | tf_op jit(solution)/shard_map/all_to_all | solution.py:488

commit v7 on v6

--- a/solution.py
+++ b/solution.py
@@ -32,7 +32,23 @@
 TAPS = 9
 STACK = TAPS * 8
 PEERS = 16
-GRAD_ROWS = RGB * 16
+WIDE = 32
+SLAB = 16
+GRADS = 12
+FLAT = WIDE * SLAB
+PARTS = 4
+PART = 16
+MAIN = 15
+BIAS_ROW = 15
+
+BOTH = 2 * SLOTS
+TAPS = 9
+STACK = TAPS * 8
+PEERS = 16
+WIDE = 32
+SLAB = 16
+GRADS = 12
+FLAT = WIDE * SLAB
 PARTS = 4
 PART = 16
 MAIN = 15
@@ -71,26 +87,43 @@
     return jnp.minimum(room, 1.0)
 
 
-def route_prep(ids, y, z, mats_ref):
-    row = iota((BOTH, 1), 0)
-    place = iota((BOTH, SLOTS), 0) // 16
-    to_slot = (place // 2) * 16 + z * 2 + place % 2
-    spread = iota((BOTH, SLOTS), 1) == to_slot
-    target = jnp.sum(jnp.where(spread, jnp.broadcast_to(ids, (BOTH, SLOTS)), 0.0), axis=1, keepdims=True)
-    from_slot = y * 16 + iota((SLOTS, BOTH), 1) // 16
+def ids_at(ids, slots):
+    spread = onehot(iota(slots.shape, 1) == slots)
+    wide = jnp.broadcast_to(ids, (8, SLOTS)).astype(bf16)
+    return lax.dot_general(spread, wide, (((1,), (1,)), ((), ())), preferred_element_type=f32)[:, 0:1]
+
+
+def route_prep(ids, y, z, c, mats_ref, gather_ref):
+    y_lo, y_hi, z_lo, z_hi = y % 2, y // 2, z % 2, z // 2
+    place = iota((FLAT, SLOTS), 0) // SLAB
+    target = ids_at(ids, (place // 4) * 16 + z_hi * 4 + place % 4)
+    from_slot = y_hi * WIDE + iota((SLOTS, FLAT), 1) // SLAB
     source = jnp.dot(
         jnp.broadcast_to(ids, (8, SLOTS)).astype(bf16),
-        onehot(iota((SLOTS, BOTH), 0) == from_slot),
+        onehot(iota((SLOTS, FLAT), 0) == from_slot),
         preferred_element_type=f32,
     )[0:1]
-    col = target - jnp.floor(target * (1.0 / TX)) * TX
-    lane = iota((1, BOTH), 1)
-    want = target + (TX * ((row // 8) % 2) + 1024 * (row % 8)).astype(f32)
-    have = source + (TX * ((lane // 8) % 2) + 1024 * (lane % 8)).astype(f32)
-    right = jnp.where(col < TX - 1.5, want + 1.0, -9999.0)
-    left = jnp.where(col > 0.5, want - 1.0, -9999.0)
+    row = iota((FLAT, 1), 0)
+    col = iota((1, FLAT), 1)
+    part = lambda at: (TX * ((at // 2) % 2) + 1024 * (2 * ((at % SLAB) // 4) + at % 2)).astype(f32)
+    image = lambda at: 100000.0 + at.astype(f32)
+    peer = row // SLAB
+    sender = (y_lo ^ ((peer // 4) % 2)) * 16 + (row % 4) * 4 + (z_lo ^ ((peer // 2) % 2)) * 2 + (c ^ (peer % 2))
+    is_grad = row % SLAB < GRADS
+    want = jnp.where(is_grad, target + part(row), image(sender * SLAB + GRADS + peer // 8))
+    have = jnp.where(col % SLAB < GRADS, source + part(col), image(col))
+    across = target - jnp.floor(target * (1.0 / TX)) * TX
+    blocked = jnp.where(is_grad, 0.0, 99.0)
+    right = jnp.where(across + blocked < TX - 1.5, want + 1.0, -9999.0)
+    left = jnp.where(across - blocked > 0.5, want - 1.0, -9999.0)
     for n, key in enumerate((want, left, right)):
-        mats_ref[n * BOTH : (n + 1) * BOTH, :] = onehot(have == key)
+        mats_ref[n * FLAT : (n + 1) * FLAT, :] = onehot(have == key)
+    row = iota((BOTH, 1), 0)
+    r, o = row // 8, row % 8
+    key = jnp.where(o < RGB, ((r // 2) % 8) * SLAB + o * 4 + (r // 16) * 2 + r % 2, -1)
+    gather_ref[0:BOTH, :] = onehot(col % SLOTS == key)
+    row = iota((SLOTS, 1), 0)
+    gather_ref[BOTH : BOTH + SLOTS, :] = onehot(col == (row // 4) * SLAB + GRADS + row % 4)
 
 
 def class_prep(ids, profile_ref, y, z, c, mats_ref, before_ref, after_ref):
@@ -99,7 +132,7 @@
     leaves = (4 * (((place // 8) % 2) ^ c) + place % 4) * 16 + (place // 16) * 2 + (place // 4) % 2
     spread = iota((SLOTS, SLOTS), 1) == leaves
     place = iota((SLOTS, SLOTS), 1)
-    comes = (place // 16) * 16 + (place % 8) * 2 + (((place // 8) % 2) ^ (y // 4))
+    comes = ((place // 16) ^ (y % 2)) * 16 + (place % 4) * 4 + (((place // 8) % 2) ^ (z % 2)) * 2 + (((place // 4) % 2) ^ c)
     come = jnp.dot(
         jnp.broadcast_to(ids, (8, SLOTS)).astype(bf16),
         onehot(iota((SLOTS, SLOTS), 0) == comes),
@@ -159,22 +192,13 @@
     return pick_rows(iota((SLOTS, SLOTS), 1) == peer * 8 + ((place // 8) % 2) * 4 + y % 4, block)
 
 
-def route_kernel(got_ref, mats_ref, own_ref, out_ref):
-    slabs = [got_ref[p].astype(f32) for p in range(PEERS)]
-    east = iota((BOTH, LANES), 1) % EDGE >= OV
-    totals = []
-    for o in range(RGB):
-        block = jnp.concatenate([slab[o * 16 : o * 16 + 16] for slab in slabs], axis=0).astype(bf16)
-        part = [
-            jnp.dot(mats_ref[n * BOTH : (n + 1) * BOTH, :], block, preferred_element_type=f32) for n in range(3)
-        ]
-        side = jnp.where(east, pltpu.roll(part[2], OV, 1), pltpu.roll(part[1], LANES - OV, 1))
-        totals.append(part[0] + side)
-    images = pass_on([slab[GRAD_ROWS : GRAD_ROWS + 8] for slab in slabs], own_ref[0] % 2)
-    for t in range(PEERS):
-        rows = [total[t * 16 : t * 16 + 16] for total in totals]
-        rows.append(images[t * 8 : t * 8 + 8])
-        out_ref[t] = jnp.concatenate(rows, axis=0).astype(bf16)
+def route_kernel(got_ref, mats_ref, out_ref):
+    block = got_ref[...].reshape(FLAT, LANES)
+    every = jnp.dot(mats_ref[...], block, preferred_element_type=f32)
+    here, left, right = (every[n * FLAT : (n + 1) * FLAT] for n in range(3))
+    east = iota((FLAT, LANES), 1) % EDGE >= OV
+    total = here + jnp.where(east, pltpu.roll(right, OV, 1), pltpu.roll(left, LANES - OV, 1))
+    out_ref[...] = total.astype(bf16).reshape(WIDE, SLAB, LANES)
 
 
 def blend_classes(images, mats_ref, before_ref, after_ref):
@@ -183,14 +207,11 @@
     low = (source - high.astype(f32)).astype(bf16)
     lane = iota((SLOTS, LANES), 1)
     south = (lane // 8) % 2 == 1
+    every = jnp.dot(mats_ref[...], jnp.concatenate([high, low], axis=1), preferred_element_type=f32)
+    every = every[:, :LANES] + every[:, LANES:]
     columns = []
     for d in range(3):
-        part = []
-        for step in range(3):
-            mat = mats_ref[(3 * d + step) * SLOTS : (3 * d + step + 1) * SLOTS, :]
-            part.append(
-                jnp.dot(mat, high, preferred_element_type=f32) + jnp.dot(mat, low, preferred_element_type=f32)
-            )
+        part = [every[(3 * d + step) * SLOTS : (3 * d + step + 1) * SLOTS] for step in range(3)]
         across = jnp.where(south, part[1], part[2])
         columns.append(part[0] + jnp.where(south, pltpu.roll(across, 8, 1), pltpu.roll(across, LANES - 8, 1)))
     total = columns[0] + pltpu.roll(jnp.where(lane >= 64, columns[1], columns[2]), 64, 1)
@@ -215,6 +236,7 @@
     own_ref,
     out_ref,
     route_ref,
+    gather_ref,
     mats_ref,
     before_ref,
     after_ref,
@@ -250,16 +272,16 @@
     ids = ids_ref[...].astype(f32)
     own = own_ref[0]
     y, z, c = own // 16, (own // 2) % 8, own % 2
-    route_prep(ids, y, z, route_ref)
+    route_prep(ids, y, z, c, route_ref, gather_ref)
     class_prep(ids, profile_ref, y, z, c, mats_ref, before_ref, after_ref)
     ratio_prep(ids, profile_ref, own, ratio_ref)
     taps[0:8, :] = jnp.zeros((8, PIX), f32)
     taps[0:RGB, :] = grad_ref[...].astype(f32)
-    halves = []
-    for r in range(ROWS):
-        turned[r] = taps[0:8, r * LANES : (r + 1) * LANES]
-    for h in range(2):
-        halves.append(jnp.concatenate(half_rows(turned, h, RGB), axis=0))
+    grads = jnp.concatenate([taps[0:8, r * LANES : (r + 1) * LANES] for r in range(ROWS)], axis=0)
+    row = iota((SLOTS, BOTH), 0)
+    part = row % SLAB
+    at = ((part // 2) % 2) * 128 + (row // SLAB) * 16 + (part % 2) * 8 + part // 4
+    eighths = pick_rows((iota((SLOTS, BOTH), 1) == at) & (part < GRADS), grads)
     for n in range(PIX // chunk):
         copies[n].wait()
         total = jnp.zeros((STACK, chunk), f32)
@@ -292,17 +314,22 @@
     for r in range(ROWS):
         turned[r] = image[:, r * LANES : (r + 1) * LANES]
     place = iota((LANES, LANES), 0)
-    k = (((place // 16) % 4) * 2 + (place // 4) % 2) * 8 + 4 * (((place // 8) % 2) ^ c) + place % 4
-    lanes = onehot(iota((LANES, LANES), 1) == (k // 32) * 64 + (place // 64) * 32 + k % 32)
+    lanes = onehot(iota((LANES, LANES), 1) == ((place // 32) % 2) * 64 + (place // 64) * 32 + place % 32)
     classes = []
     for h in range(2):
         block = half_rows(turned, h, RGB) + [jnp.zeros((16, LANES), f32)]
         block = jnp.concatenate(block, axis=0).astype(bf16)
         both = lax.dot_general(lanes, block, (((1,), (1,)), ((), ())), preferred_element_type=f32)
         classes.append(jnp.concatenate([both[0:64], both[64:128]], axis=1))
-    classes = jnp.concatenate(classes, axis=0)
-    for p in range(PEERS):
-        out_ref[p] = jnp.concatenate([halves[p % 2], classes[p * 8 : p * 8 + 8]], axis=0).astype(bf16)
+    row = iota((FLAT, SLOTS), 0)
+    peer = row // SLAB
+    z_to = (peer // 4) % 4 * 2 + (((peer // 2) % 2) ^ (z % 2))
+    k = (2 * z_to + ((peer % 2) ^ c)) * 8 + (row % 4) * 2 + ((peer // 16) ^ (y % 2))
+    images = pick_rows((iota((FLAT, SLOTS), 1) == k) & (row % SLAB >= GRADS), jnp.concatenate(classes, axis=0))
+    for p in range(WIDE):
+        e = (p // 16) * 4 + p % 4
+        slab = images[p * SLAB : (p + 1) * SLAB] + eighths[e * SLAB : (e + 1) * SLAB]
+        out_ref[p] = slab.astype(bf16)
 
 
 def half_rows(turned, h, colours):
@@ -338,24 +365,22 @@
 
 
 def weight_grad_kernel(
-    chunk, got_ref, feat_ref, ratio_ref, mats_ref, before_ref, after_ref, out_ref, stack_ref, taps, turned
+    chunk, got_ref, feat_ref, ratio_ref, gather_ref, mats_ref, before_ref, after_ref, out_ref, stack_ref, taps
 ):
-    sums = [got_ref[h].astype(f32) for h in range(2)]
-    for n in range(2, PEERS):
-        sums[n % 2] = sums[n % 2] + got_ref[n].astype(f32)
-    turned[...] = jnp.zeros_like(turned)
-    for h in range(2):
-        for o in range(RGB):
-            for qy in range(2):
-                at = qy * 16 + h * 8
-                piece = sums[h][o * 16 + qy * 8 : o * 16 + qy * 8 + 8] * ratio_ref[at : at + 8, :]
-                turned[at : at + 8, o, :] = piece.astype(bf16).astype(f32)
-    grad = jnp.concatenate([turned[r] for r in range(ROWS)], axis=1)
-    images = [got_ref[n].astype(f32)[GRAD_ROWS : GRAD_ROWS + 8] for n in range(PEERS)]
-    blended = blend_classes(jnp.concatenate(images, axis=0), mats_ref, before_ref, after_ref)
+    every = jnp.dot(gather_ref[...], got_ref[...].reshape(FLAT, LANES), preferred_element_type=f32)
+    pieces = []
+    for r in range(ROWS):
+        piece = every[r * 8 : r * 8 + 8] * ratio_ref[r : r + 1, :]
+        pieces.append(piece.astype(bf16).astype(f32))
+    grad = jnp.concatenate(pieces, axis=1)
+    blended = blend_classes(every[BOTH : BOTH + SLOTS], mats_ref, before_ref, after_ref)
     grad_stack(grad, taps)
-    bias = lax.dot_general(
-        jnp.ones((8, PIX), bf16), grad.astype(bf16), (((1,), (1,)), ((), ())), preferred_element_type=f32
+    summed = pieces[0]
+    for piece in pieces[1:]:
+        summed = summed + piece
+    diagonal = iota((8, LANES), 0) == iota((8, LANES), 1)
+    bias = jnp.sum(
+        jnp.where(diagonal, jnp.sum(summed, axis=1, keepdims=True), 0.0), axis=0, keepdims=True
     )
     total = jnp.zeros((TIN * CH, STACK), f32)
     for at in range(0, PIX, chunk):
@@ -378,15 +403,13 @@
     offset = place - every - RGB * (rank - PARTS * MAIN)
     side = (offset >= 0) & (offset < RGB) & (place >= every) & (rank >= PARTS * MAIN)
     chosen = jnp.dot(onehot(main | side), rows, preferred_element_type=f32)
-    bias_wide = jnp.concatenate([bias, jnp.zeros((8, LANES - 8), f32)], axis=1)[0:1]
-    bias_wide = jnp.where(iota((1, LANES), 1) < RGB, bias_wide, 0.0)
     lane = iota((every, LANES), 1)
     third = iota((every, LANES), 0) % 3
     tail = jnp.zeros((every, LANES), f32)
     for c in range(3):
         tail = jnp.where(third == c, pltpu.roll(chosen[every:], CH - 32 * c, 1), tail)
     packed = jnp.where(lane < CH, chosen[:every], tail)
-    packed = jnp.where((iota((every, LANES), 0) % PART == BIAS_ROW) & (lane < CH), bias_wide, packed)
+    packed = jnp.where((iota((every, LANES), 0) % PART == BIAS_ROW) & (lane < CH), bias, packed)
     parts = [split_bias(packed[q * PART : (q + 1) * PART]) for q in range(PARTS)]
     for p in range(PEERS):
         out_ref[p] = jnp.concatenate([parts[p % PARTS], blended[p * 8 : p * 8 + 8]], axis=0).astype(bf16)
@@ -495,15 +518,16 @@
 def per_device(features, conv_weight, bias, blend_profile, tile_ids, reward_grad):
     chunk = 1024
     conv_flops = 2 * STACK * TIN * CH * PIX
-    own = lax.axis_index(("y", "z_hi", "z_lo", "c")).reshape(1).astype(jnp.int32)
+    own = lax.axis_index(("y_hi", "y_lo", "z_hi", "z_lo", "c")).reshape(1).astype(jnp.int32)
     feats = jnp.transpose(features[0, 0], (1, 0, 2))
     args = (feats, conv_weight, bias, reward_grad[0, 0], tile_ids, blend_profile)
     here = [pltpu.with_memory_space_constraint(x, pltpu.HBM) for x in args]
-    rows, route, mats, before, after, ratio, feats_held, weights_held = call(
+    rows, route, gather, mats, before, after, ratio, feats_held, weights_held = call(
         functools.partial(conv_kernel, 2 * chunk),
         (
-            pltpu.VMEM((PEERS, GRAD_ROWS + 8, LANES), bf16),
-            pltpu.VMEM((3 * BOTH, BOTH), bf16),
+            pltpu.VMEM((WIDE, SLAB, LANES), bf16),
+            pltpu.VMEM((3 * FLAT, FLAT), bf16),
+            pltpu.VMEM((BOTH + SLOTS, FLAT), bf16),
             pltpu.VMEM((9 * SLOTS, SLOTS), bf16),
             pltpu.VMEM((8, LANES), f32),
             pltpu.VMEM((SLOTS, LANES), f32),
@@ -527,23 +551,23 @@
         conv_flops,
         1 << 22,
         "conv",
-        out_specs=(VM,) * 8,
+        out_specs=(VM,) * 9,
     )(*here, own)
-    rows = exchange(rows, ("z_hi", "z_lo", "c"))
+    rows = exchange(rows, ("y_lo", "z_hi", "z_lo", "c"))
     rows = call(
-        route_kernel, message(PEERS, GRAD_ROWS + 8), [VM, VM, SM], (), 1 << 27, 1 << 20, "route", out_specs=VM
-    )(rows, route, own)
-    rows = exchange(rows, ("y", "c"))
+        route_kernel, message(WIDE, SLAB), [VM, VM], (), 1 << 28, 1 << 21, "route", out_specs=VM
+    )(rows, route)
+    rows = exchange(rows, ("y_hi", "y_lo", "z_lo", "c"))
     rows, stack = call(
         functools.partial(weight_grad_kernel, chunk),
         (message(PEERS, PART + 8), jax.ShapeDtypeStruct((STACK, PIX), bf16)),
-        [VM, VM, VM, VM, VM, VM],
-        [pltpu.VMEM((STACK, PIX), f32), pltpu.VMEM((ROWS, 8, LANES), f32)],
+        [VM] * 7,
+        [pltpu.VMEM((STACK, PIX), f32)],
         conv_flops,
         1 << 22,
         "weight_grad",
         out_specs=(VM, VM),
-    )(rows, feats_held, ratio, mats, before, after)
+    )(rows, feats_held, ratio, gather, mats, before, after)
 
     feature_rows = call(
         feature_grad_kernel,
@@ -563,7 +587,7 @@
 
     rows = exchange(rows, ("z_hi", "z_lo", "c"))
     rows = call(sum_z_kernel, message(PEERS, PART + 8), [VM, SM], name="sum_z", out_specs=VM)(rows, own)
-    rows = exchange(rows, ("y", "c"))
+    rows = exchange(rows, ("y_hi", "y_lo", "c"))
     decoded = call(
         decode_kernel,
         jax.ShapeDtypeStruct((RGB, PIX), bf16),
@@ -591,8 +615,8 @@
 
 
 def solution(mesh):
-    parts = Mesh(mesh.devices.reshape(8, 4, 2, 2, 4), ("y", "z_hi", "z_lo", "c", "clip"))
-    tile = ("y", "z_hi", "z_lo", "c")
+    parts = Mesh(mesh.devices.reshape(4, 2, 4, 2, 2, 4), ("y_hi", "y_lo", "z_hi", "z_lo", "c", "clip"))
+    tile = ("y_hi", "y_lo", "z_hi", "z_lo", "c")
     return jax.shard_map(
         per_device,
         mesh=parts,

time: 79.9 us -> 78.9 us (0.987)
  blocking collectives: 63 us -> 60.7 us
  Pallas kernels: 10.4 us -> 11.9 us
    all_to_all x4, blocking collectives: 63 us -> 60.7 us  [exchange(): return lax.all_to_all(rows, axes, 0, 0, tiled=True)]
    pallas_call x2, Pallas kernels: 3.21 us -> 4.42 us  [the longest x1 3.77 us: per_device(): call(functools.partial(conv_kernel, 2 * chunk), (pltpu.VMEM((WIDE, SLAB,...]
where the time goes in v7:
time: 78.9 us; the launch traced here: 78.6 us
  blocking collectives  60.7 us (77%)
  Pallas kernels  11.9 us (15%)
  starting transfers between devices  4.02 us (5%)
  waiting for transfers between devices  1.41 us (2%)
    all_to_all x4, blocking collectives, exchange(): return lax.all_to_all(rows, axes, 0, 0, tiled=True)  60.7 us
    all_to_all x1, starting transfers between devices, exchange(): return lax.all_to_all(rows, axes, 0, 0, tiled=True)  4.02 us
    pallas_call x1, Pallas kernels, per_device(): call(functools.partial(conv_kernel, 2 * chunk), (pltpu.VMEM((WIDE, SLAB,...  3.77 us
    pallas_call x1, Pallas kernels, per_device(): call(feature_grad_kernel, jax.ShapeDtypeStruct((TIN, CH, PIX), bf16), [pl...  2.7 us
    pallas_call x1, Pallas kernels, per_device(): call(functools.partial(weight_grad_kernel, chunk), (message(PEERS, PART +...  1.98 us
  transfers between devices with their start and end apart: 1, of which 1 were waited for; matrix products, arithmetic and copies ran while one was open for 0% of the time, Pallas kernels for 5%

profile of v7, /device:TPU:1, one launch (start us, length us, event | category | flops | bytes accessed | tf_op | source)
XLA Modules:
  0.0 78.6 jit_solution(2120949835947986507)
XLA Ops:
  0.6 3.8 %conv.1 = (bf16[32,16,128]{2,1,0:T(8,128)(2,1)S(1)}, bf16[1536,512]{1,0:T(8,128)(2,1)S(1)}, bf16[384,512]{1,0:T(8,128)(2,1)S(1)}, bf16[1152,128]{1,0:T(8,128)(2,...) custom-call(bf16[3,96,4096]{2,1,0:T(8,128)(2,1)} %bitcast.10, ...), custom_call_target="tpu_custom_call" | custom-call | flops 169869312 | bytes 4194304 | tf_op jit(solution)/shard_map/conv/pallas_call | solution.py:525
  4.4 21.7 %all_to_all.25.got_ref = bf16[32,16,128]{2,1,0:T(8,128)(2,1)S(1)} all-to-all(bf16[32,16,128]{2,1,0:T(8,128)(2,1)S(1)} %get-tuple-element.20), channel_id=1, replica_groups=mesh['y_hi'=4,'y_lo'=2,'z_hi'=4,'z_lo'=2,'c'=2,'clip'=4] {'y_lo','z_hi',..., dimensions={0} | all-to-all | bytes 262144 | tf_op jit(solution)/shard_map/all_to_all | solution.py:511
  26.1 0.6 route.1
  26.8 16.3 %all_to_all.26.got_ref = bf16[32,16,128]{2,1,0:T(8,128)(2,1)S(1)} all-to-all(bf16[32,16,128]{2,1,0:T(8,128)(2,1)S(1)} %route.1), channel_id=1, replica_groups=mesh['y_hi'=4,'y_lo'=2,'z_hi'=4,'z_lo'=2,'c'=2,'clip'=4] {'y_hi','y_lo',..., dimensions={0} | all-to-all | bytes 262144 | tf_op jit(solution)/shard_map/all_to_all | solution.py:511
  43.1 2.0 %weight_grad.1 = (bf16[16,24,128]{2,1,0:T(8,128)(2,1)S(1)}, bf16[72,4096]{1,0:T(8,128)(2,1)S(1)}) custom-call(bf16[32,16,128]{2,1,0:T(8,128)(2,1)S(1)} %all_to_all.26.got_ref, bf16[3,96,4096]{2,1,0:T(8,128)(2,1)S(1)} %get-tuple-element.22.feat_ref, f32[32,128]{1,0:T(8,128)S(1)} %get-tuple-element.23.ratio_ref, ...), custom_call_target="tpu_custom_call" | custom-call | flops 169869312 | bytes 4194304 | tf_op jit(solution)/shard_map/weight_grad/pallas_call | solution.py:561
  45.1 11.7 %all_to_all.27.got_ref = bf16[16,24,128]{2,1,0:T(8,128)(2,1)S(1)} all-to-all(bf16[16,24,128]{2,1,0:T(8,128)(2,1)S(1)} %get-tuple-element.28), channel_id=1, replica_groups=mesh['y_hi'=4,'y_lo'=2,'z_hi'=4,'z_lo'=2,'c'=2,'clip'=4] {'z_hi','z_lo',..., dimensions={0} | all-to-all | bytes 196608 | tf_op jit(solution)/shard_map/all_to_all | solution.py:511
  56.7 0.2 sum_z.1
  56.9 11.0 %all_to_all.28.got_ref = bf16[16,24,128]{2,1,0:T(8,128)(2,1)S(1)} all-to-all(bf16[16,24,128]{2,1,0:T(8,128)(2,1)S(1)} %sum_z.1), channel_id=1, replica_groups=mesh['y_hi'=4,'y_lo'=2,'z_hi'=4,'z_lo'=2,'c'=2,'clip'=4] {'y_hi','y_lo',..., dimensions={0} | all-to-all | bytes 196608 | tf_op jit(solution)/shard_map/all_to_all | solution.py:511
  67.9 0.8 sum_y.1
  68.7 4.0 %all-to-all-start.4 = ((bf16[8,32,128]{2,1,0:T(8,128)(2,1)}), bf16[8,32,128]{2,1,0:T(8,128)(2,1)S(1)}, u32[]{:S(2)}, u32[]{:S(2)}) async-start(bf16[8,32,128]{2,1,0:T(8,128)(2,1)} %sum_y.1), calls=%async_computation.4 | async-start | bytes 131072 | tf_op jit(solution)/shard_map/all_to_all | solution.py:511
  72.7 2.7 %feature_grad.1 = bf16[3,96,4096]{2,1,0:T(8,128)(2,1)} custom-call(bf16[72,4096]{1,0:T(8,128)(2,1)S(1)} %get-tuple-element.29.stack_ref, bf16[3,72,96]{2,1,0:T(8,128)(2,1)S(1)} %get-tuple-element.30.weight_ref), custom_call_target="tpu_custom_call" | custom-call | flops 169869312 | bytes 4194304 | tf_op jit(solution)/shard_map/feature_grad/pallas_call | solution.py:572
  75.4 1.1 %decode.1 = bf16[3,4096]{1,0:T(4,128)(2,1)} custom-call(bf16[16,24,128]{2,1,0:T(8,128)(2,1)S(1)} %all_to_all.28.got_ref, s32[1]{0:T(128)} %bitcast.3.own_ref), custom_call_target="tpu_custom_call" | custom-call | flops 1048576 | bytes 131072 | tf_op jit(solution)/shard_map/decode/pallas_call | solution.py:591
  76.5 1.4 %all-to-all-done.4.got_ref = bf16[8,32,128]{2,1,0:T(8,128)(2,1)S(1)} async-done(((bf16[8,32,128]{2,1,0:T(8,128)(2,1)}), bf16[8,32,128]{2,1,0:T(8,128)(2,1)S(1)}, u32[]{:S(2)}, u32[]{:S(2)}) %all-to-all-start.4) | async-done | bytes 65568 | tf_op jit(solution)/shard_map/all_to_all | solution.py:511
  77.9 0.7 finish.1
Async XLA Ops:
  68.7 9.2 %all-to-all-start.4 = ((bf16[8,32,128]{2,1,0:T(8,128)(2,1)}), bf16[8,32,128]{2,1,0:T(8,128)(2,1)S(1)}, u32[]{:S(2)}, u32[]{:S(2)}) async-start(bf16[8,32,128]{2,1,0:T(8,128)(2,1)} %sum_y.1), calls=%async_computation.4 | async-start | bytes 131072 | tf_op jit(solution)/shard_map/all_to_all | solution.py:511

commit v8 on v7

--- a/solution.py
+++ b/solution.py
@@ -95,35 +95,32 @@
 
 def route_prep(ids, y, z, c, mats_ref, gather_ref):
     y_lo, y_hi, z_lo, z_hi = y % 2, y // 2, z % 2, z // 2
-    place = iota((FLAT, SLOTS), 0) // SLAB
+    place = iota((SLOTS, SLOTS), 0) // 4
     target = ids_at(ids, (place // 4) * 16 + z_hi * 4 + place % 4)
-    from_slot = y_hi * WIDE + iota((SLOTS, FLAT), 1) // SLAB
+    col = iota((1, SLOTS), 1)
     source = jnp.dot(
         jnp.broadcast_to(ids, (8, SLOTS)).astype(bf16),
-        onehot(iota((SLOTS, FLAT), 0) == from_slot),
+        onehot(iota((SLOTS, SLOTS), 0) == y_hi * WIDE + col // 4),
         preferred_element_type=f32,
     )[0:1]
-    row = iota((FLAT, 1), 0)
+    row = iota((SLOTS, 1), 0)
+    want = target + (TX * ((row // 2) % 2) + 1024 * (row % 2)).astype(f32)
+    have = source + (TX * ((col // 2) % 2) + 1024 * (col % 2)).astype(f32)
+    across = target - jnp.floor(target * (1.0 / TX)) * TX
+    right = jnp.where(across < TX - 1.5, want + 1.0, -9999.0)
+    left = jnp.where(across > 0.5, want - 1.0, -9999.0)
+    for n, key in enumerate((want, left, right)):
+        mats_ref[n * SLOTS : (n + 1) * SLOTS, :] = onehot(have == key)
+    peer = col // 4
+    to_y = (col % 4) * 2 + (y_lo ^ (peer // 16))
+    to_peer = to_y * 4 + (z_lo ^ ((peer // 2) % 2)) * 2 + (c ^ (peer % 2))
+    to_row = to_peer * 4 + (peer // 4) % 4
+    mats_ref[3 * SLOTS : 4 * SLOTS, :] = onehot(iota((SLOTS, SLOTS), 0) == to_row)
     col = iota((1, FLAT), 1)
-    part = lambda at: (TX * ((at // 2) % 2) + 1024 * (2 * ((at % SLAB) // 4) + at % 2)).astype(f32)
-    image = lambda at: 100000.0 + at.astype(f32)
-    peer = row // SLAB
-    sender = (y_lo ^ ((peer // 4) % 2)) * 16 + (row % 4) * 4 + (z_lo ^ ((peer // 2) % 2)) * 2 + (c ^ (peer % 2))
-    is_grad = row % SLAB < GRADS
-    want = jnp.where(is_grad, target + part(row), image(sender * SLAB + GRADS + peer // 8))
-    have = jnp.where(col % SLAB < GRADS, source + part(col), image(col))
-    across = target - jnp.floor(target * (1.0 / TX)) * TX
-    blocked = jnp.where(is_grad, 0.0, 99.0)
-    right = jnp.where(across + blocked < TX - 1.5, want + 1.0, -9999.0)
-    left = jnp.where(across - blocked > 0.5, want - 1.0, -9999.0)
-    for n, key in enumerate((want, left, right)):
-        mats_ref[n * FLAT : (n + 1) * FLAT, :] = onehot(have == key)
-    row = iota((BOTH, 1), 0)
-    r, o = row // 8, row % 8
-    key = jnp.where(o < RGB, ((r // 2) % 8) * SLAB + o * 4 + (r // 16) * 2 + r % 2, -1)
-    gather_ref[0:BOTH, :] = onehot(col % SLOTS == key)
-    row = iota((SLOTS, 1), 0)
-    gather_ref[BOTH : BOTH + SLOTS, :] = onehot(col == (row // 4) * SLAB + GRADS + row % 4)
+    peer, at = col // SLAB, col % SLAB
+    grad_row = (((at // 2) % 2) * 16 + (peer % 8) * 2 + at % 2) * 8 + at // 4
+    to_row = jnp.where(at < GRADS, grad_row, BOTH + peer * 4 + at - GRADS)
+    gather_ref[...] = onehot(iota((BOTH + SLOTS, FLAT), 0) == to_row)
 
 
 def class_prep(ids, profile_ref, y, z, c, mats_ref, before_ref, after_ref):
@@ -193,12 +190,19 @@
 
 
 def route_kernel(got_ref, mats_ref, out_ref):
-    block = got_ref[...].reshape(FLAT, LANES)
-    every = jnp.dot(mats_ref[...], block, preferred_element_type=f32)
-    here, left, right = (every[n * FLAT : (n + 1) * FLAT] for n in range(3))
-    east = iota((FLAT, LANES), 1) % EDGE >= OV
-    total = here + jnp.where(east, pltpu.roll(right, OV, 1), pltpu.roll(left, LANES - OV, 1))
-    out_ref[...] = total.astype(bf16).reshape(WIDE, SLAB, LANES)
+    slabs = [got_ref[p].astype(f32) for p in range(WIDE)]
+    blocks = [jnp.concatenate([slab[4 * o : 4 * o + 4] for slab in slabs], axis=0) for o in range(RGB + 1)]
+    every = jnp.dot(
+        mats_ref[0 : 3 * SLOTS, :], jnp.concatenate(blocks[:RGB], axis=1).astype(bf16), preferred_element_type=f32
+    )
+    east = iota((SLOTS, LANES), 1) % EDGE >= OV
+    totals = []
+    for o in range(RGB):
+        here, left, right = (every[n * SLOTS : (n + 1) * SLOTS, o * LANES : (o + 1) * LANES] for n in range(3))
+        totals.append(here + jnp.where(east, pltpu.roll(right, OV, 1), pltpu.roll(left, LANES - OV, 1)))
+    totals.append(jnp.dot(mats_ref[3 * SLOTS :, :], blocks[RGB].astype(bf16), preferred_element_type=f32))
+    for t in range(WIDE):
+        out_ref[t] = jnp.concatenate([total[4 * t : 4 * t + 4] for total in totals], axis=0).astype(bf16)
 
 
 def blend_classes(images, mats_ref, before_ref, after_ref):
@@ -251,6 +255,7 @@
     held,
     taps,
     turned,
+    place_ref,
     small_sems,
     sems,
 ):
@@ -278,10 +283,13 @@
     taps[0:8, :] = jnp.zeros((8, PIX), f32)
     taps[0:RGB, :] = grad_ref[...].astype(f32)
     grads = jnp.concatenate([taps[0:8, r * LANES : (r + 1) * LANES] for r in range(ROWS)], axis=0)
-    row = iota((SLOTS, BOTH), 0)
-    part = row % SLAB
-    at = ((part // 2) % 2) * 128 + (row // SLAB) * 16 + (part % 2) * 8 + part // 4
-    eighths = pick_rows((iota((SLOTS, BOTH), 1) == at) & (part < GRADS), grads)
+    col = iota((1, BOTH), 1)
+    r, o = col // 8, col % 8
+    to_row = jnp.where(o < RGB, ((r // 2) % 8) * SLAB + o * 4 + (r // 16) * 2 + r % 2, -1)
+    eighths = pick_rows(iota((SLOTS, BOTH), 0) == to_row, grads)
+    k = iota((1, SLOTS), 1)
+    peer = ((k % 2) ^ (y % 2)) * 16 + (k // 32) * 4 + (((k // 16) % 2) ^ (z % 2)) * 2 + (((k // 8) % 2) ^ c)
+    place_ref[...] = onehot(iota((FLAT, SLOTS), 0) == peer * SLAB + GRADS + (k % 8) // 2)
     for n in range(PIX // chunk):
         copies[n].wait()
         total = jnp.zeros((STACK, chunk), f32)
@@ -321,11 +329,8 @@
         block = jnp.concatenate(block, axis=0).astype(bf16)
         both = lax.dot_general(lanes, block, (((1,), (1,)), ((), ())), preferred_element_type=f32)
         classes.append(jnp.concatenate([both[0:64], both[64:128]], axis=1))
-    row = iota((FLAT, SLOTS), 0)
-    peer = row // SLAB
-    z_to = (peer // 4) % 4 * 2 + (((peer // 2) % 2) ^ (z % 2))
-    k = (2 * z_to + ((peer % 2) ^ c)) * 8 + (row % 4) * 2 + ((peer // 16) ^ (y % 2))
-    images = pick_rows((iota((FLAT, SLOTS), 1) == k) & (row % SLAB >= GRADS), jnp.concatenate(classes, axis=0))
+    classes = jnp.concatenate(classes, axis=0).astype(bf16)
+    images = jnp.dot(place_ref[...], classes, preferred_element_type=f32)
     for p in range(WIDE):
         e = (p // 16) * 4 + p % 4
         slab = images[p * SLAB : (p + 1) * SLAB] + eighths[e * SLAB : (e + 1) * SLAB]
@@ -526,7 +531,7 @@
         functools.partial(conv_kernel, 2 * chunk),
         (
             pltpu.VMEM((WIDE, SLAB, LANES), bf16),
-            pltpu.VMEM((3 * FLAT, FLAT), bf16),
+            pltpu.VMEM((4 * SLOTS, SLOTS), bf16),
             pltpu.VMEM((BOTH + SLOTS, FLAT), bf16),
             pltpu.VMEM((9 * SLOTS, SLOTS), bf16),
             pltpu.VMEM((8, LANES), f32),
@@ -545,6 +550,7 @@
             pltpu.VMEM((TIN, STACK, CH), f32),
             pltpu.VMEM((STACK, PIX), f32),
             pltpu.VMEM((ROWS, 8, LANES), f32),
+            pltpu.VMEM((FLAT, SLOTS), bf16),
             pltpu.SemaphoreType.DMA((5,)),
             pltpu.SemaphoreType.DMA((PIX // (2 * chunk),)),
         ],

time: 78.9 us -> 78 us (0.989)
  Pallas kernels: 11.9 us -> 10.9 us
where the time goes in v8:
time: 78 us; the launch traced here: 77.7 us
  blocking collectives  60.7 us (78%)
  Pallas kernels  10.9 us (14%)
  starting transfers between devices  4.02 us (5%)
  waiting for transfers between devices  1.42 us (2%)
    all_to_all x4, blocking collectives, exchange(): return lax.all_to_all(rows, axes, 0, 0, tiled=True)  60.7 us
    all_to_all x1, starting transfers between devices, exchange(): return lax.all_to_all(rows, axes, 0, 0, tiled=True)  4.02 us
    pallas_call x1, Pallas kernels, per_device(): call(functools.partial(conv_kernel, 2 * chunk), (pltpu.VMEM((WIDE, SLAB,...  3.15 us
    pallas_call x1, Pallas kernels, per_device(): call(feature_grad_kernel, jax.ShapeDtypeStruct((TIN, CH, PIX), bf16), [pl...  2.7 us
    pallas_call x1, Pallas kernels, per_device(): call(functools.partial(weight_grad_kernel, chunk), (message(PEERS, PART +...  1.99 us
  transfers between devices with their start and end apart: 1, of which 1 were waited for; matrix products, arithmetic and copies ran while one was open for 0% of the time, Pallas kernels for 5%

profile of v8, /device:TPU:1, one launch (start us, length us, event | category | flops | bytes accessed | tf_op | source)
XLA Modules:
  0.0 77.7 jit_solution(15806305491191197223)
XLA Ops:
  0.6 3.2 %conv.1 = (bf16[32,16,128]{2,1,0:T(8,128)(2,1)S(1)}, bf16[512,128]{1,0:T(8,128)(2,1)S(1)}, bf16[384,512]{1,0:T(8,128)(2,1)S(1)}, bf16[1152,128]{1,0:T(8,128)(2,1...) custom-call(bf16[3,96,4096]{2,1,0:T(8,128)(2,1)} %bitcast.10, ...), custom_call_target="tpu_custom_call" | custom-call | flops 169869312 | bytes 4194304 | tf_op jit(solution)/shard_map/conv/pallas_call | solution.py:530
  3.8 21.7 %all_to_all.25.got_ref = bf16[32,16,128]{2,1,0:T(8,128)(2,1)S(1)} all-to-all(bf16[32,16,128]{2,1,0:T(8,128)(2,1)S(1)} %get-tuple-element.20), channel_id=1, replica_groups=mesh['y_hi'=4,'y_lo'=2,'z_hi'=4,'z_lo'=2,'c'=2,'clip'=4] {'y_lo','z_hi',..., dimensions={0} | all-to-all | bytes 262144 | tf_op jit(solution)/shard_map/all_to_all | solution.py:516
  25.5 0.3 route.1
  25.8 16.3 %all_to_all.26.got_ref = bf16[32,16,128]{2,1,0:T(8,128)(2,1)S(1)} all-to-all(bf16[32,16,128]{2,1,0:T(8,128)(2,1)S(1)} %route.1), channel_id=1, replica_groups=mesh['y_hi'=4,'y_lo'=2,'z_hi'=4,'z_lo'=2,'c'=2,'clip'=4] {'y_hi','y_lo',..., dimensions={0} | all-to-all | bytes 262144 | tf_op jit(solution)/shard_map/all_to_all | solution.py:516
  42.1 2.0 %weight_grad.1 = (bf16[16,24,128]{2,1,0:T(8,128)(2,1)S(1)}, bf16[72,4096]{1,0:T(8,128)(2,1)S(1)}) custom-call(bf16[32,16,128]{2,1,0:T(8,128)(2,1)S(1)} %all_to_all.26.got_ref, bf16[3,96,4096]{2,1,0:T(8,128)(2,1)S(1)} %get-tuple-element.22.feat_ref, f32[32,128]{1,0:T(8,128)S(1)} %get-tuple-element.23.ratio_ref, ...), custom_call_target="tpu_custom_call" | custom-call | flops 169869312 | bytes 4194304 | tf_op jit(solution)/shard_map/weight_grad/pallas_call | solution.py:567
  44.1 11.7 %all_to_all.27.got_ref = bf16[16,24,128]{2,1,0:T(8,128)(2,1)S(1)} all-to-all(bf16[16,24,128]{2,1,0:T(8,128)(2,1)S(1)} %get-tuple-element.28), channel_id=1, replica_groups=mesh['y_hi'=4,'y_lo'=2,'z_hi'=4,'z_lo'=2,'c'=2,'clip'=4] {'z_hi','z_lo',..., dimensions={0} | all-to-all | bytes 196608 | tf_op jit(solution)/shard_map/all_to_all | solution.py:516
  55.8 0.2 sum_z.1
  56.0 11.0 %all_to_all.28.got_ref = bf16[16,24,128]{2,1,0:T(8,128)(2,1)S(1)} all-to-all(bf16[16,24,128]{2,1,0:T(8,128)(2,1)S(1)} %sum_z.1), channel_id=1, replica_groups=mesh['y_hi'=4,'y_lo'=2,'z_hi'=4,'z_lo'=2,'c'=2,'clip'=4] {'y_hi','y_lo',..., dimensions={0} | all-to-all | bytes 196608 | tf_op jit(solution)/shard_map/all_to_all | solution.py:516
  67.0 0.8 %sum_y.1 = bf16[8,32,128]{2,1,0:T(8,128)(2,1)} custom-call(bf16[16,24,128]{2,1,0:T(8,128)(2,1)S(1)} %all_to_all.28.got_ref), custom_call_target="tpu_custom_call" | custom-call | flops 1048576 | bytes 131072 | tf_op jit(solution)/shard_map/sum_y/pallas_call | solution.py:605
  67.8 4.0 %all-to-all-start.4 = ((bf16[8,32,128]{2,1,0:T(8,128)(2,1)}), bf16[8,32,128]{2,1,0:T(8,128)(2,1)S(1)}, u32[]{:S(2)}, u32[]{:S(2)}) async-start(bf16[8,32,128]{2,1,0:T(8,128)(2,1)} %sum_y.1), calls=%async_computation.4 | async-start | bytes 131072 | tf_op jit(solution)/shard_map/all_to_all | solution.py:516
  71.8 2.7 %feature_grad.1 = bf16[3,96,4096]{2,1,0:T(8,128)(2,1)} custom-call(bf16[72,4096]{1,0:T(8,128)(2,1)S(1)} %get-tuple-element.29.stack_ref, bf16[3,72,96]{2,1,0:T(8,128)(2,1)S(1)} %get-tuple-element.30.weight_ref), custom_call_target="tpu_custom_call" | custom-call | flops 169869312 | bytes 4194304 | tf_op jit(solution)/shard_map/feature_grad/pallas_call | solution.py:578
  74.5 1.1 %decode.1 = bf16[3,4096]{1,0:T(4,128)(2,1)} custom-call(bf16[16,24,128]{2,1,0:T(8,128)(2,1)S(1)} %all_to_all.28.got_ref, s32[1]{0:T(128)} %bitcast.3.own_ref), custom_call_target="tpu_custom_call" | custom-call | flops 1048576 | bytes 131072 | tf_op jit(solution)/shard_map/decode/pallas_call | solution.py:597
  75.6 1.4 %all-to-all-done.4.got_ref = bf16[8,32,128]{2,1,0:T(8,128)(2,1)S(1)} async-done(((bf16[8,32,128]{2,1,0:T(8,128)(2,1)}), bf16[8,32,128]{2,1,0:T(8,128)(2,1)S(1)}, u32[]{:S(2)}, u32[]{:S(2)}) %all-to-all-start.4) | async-done | bytes 65568 | tf_op jit(solution)/shard_map/all_to_all | solution.py:516
  77.0 0.7 finish.1
Async XLA Ops:
  67.8 9.2 %all-to-all-start.4 = ((bf16[8,32,128]{2,1,0:T(8,128)(2,1)}), bf16[8,32,128]{2,1,0:T(8,128)(2,1)S(1)}, u32[]{:S(2)}, u32[]{:S(2)}) async-start(bf16[8,32,128]{2,1,0:T(8,128)(2,1)} %sum_y.1), calls=%async_computation.4 | async-start | bytes 131072 | tf_op jit(solution)/shard_map/all_to_all | solution.py:516

commit v9 on v8

--- a/solution.py
+++ b/solution.py
@@ -93,7 +93,7 @@
     return lax.dot_general(spread, wide, (((1,), (1,)), ((), ())), preferred_element_type=f32)[:, 0:1]
 
 
-def route_prep(ids, y, z, c, mats_ref, gather_ref):
+def route_prep(ids, y, z, c, mats_ref):
     y_lo, y_hi, z_lo, z_hi = y % 2, y // 2, z % 2, z // 2
     place = iota((SLOTS, SLOTS), 0) // 4
     target = ids_at(ids, (place // 4) * 16 + z_hi * 4 + place % 4)
@@ -116,11 +116,6 @@
     to_peer = to_y * 4 + (z_lo ^ ((peer // 2) % 2)) * 2 + (c ^ (peer % 2))
     to_row = to_peer * 4 + (peer // 4) % 4
     mats_ref[3 * SLOTS : 4 * SLOTS, :] = onehot(iota((SLOTS, SLOTS), 0) == to_row)
-    col = iota((1, FLAT), 1)
-    peer, at = col // SLAB, col % SLAB
-    grad_row = (((at // 2) % 2) * 16 + (peer % 8) * 2 + at % 2) * 8 + at // 4
-    to_row = jnp.where(at < GRADS, grad_row, BOTH + peer * 4 + at - GRADS)
-    gather_ref[...] = onehot(iota((BOTH + SLOTS, FLAT), 0) == to_row)
 
 
 def class_prep(ids, profile_ref, y, z, c, mats_ref, before_ref, after_ref):
@@ -240,7 +235,6 @@
     own_ref,
     out_ref,
     route_ref,
-    gather_ref,
     mats_ref,
     before_ref,
     after_ref,
@@ -277,7 +271,7 @@
     ids = ids_ref[...].astype(f32)
     own = own_ref[0]
     y, z, c = own // 16, (own // 2) % 8, own % 2
-    route_prep(ids, y, z, c, route_ref, gather_ref)
+    route_prep(ids, y, z, c, route_ref)
     class_prep(ids, profile_ref, y, z, c, mats_ref, before_ref, after_ref)
     ratio_prep(ids, profile_ref, own, ratio_ref)
     taps[0:8, :] = jnp.zeros((8, PIX), f32)
@@ -370,15 +364,21 @@
 
 
 def weight_grad_kernel(
-    chunk, got_ref, feat_ref, ratio_ref, gather_ref, mats_ref, before_ref, after_ref, out_ref, stack_ref, taps
+    chunk, got_ref, feat_ref, ratio_ref, mats_ref, before_ref, after_ref, out_ref, stack_ref, taps, added
 ):
-    every = jnp.dot(gather_ref[...], got_ref[...].reshape(FLAT, LANES), preferred_element_type=f32)
+    slabs = [got_ref[n].astype(f32) for n in range(WIDE)]
+    for e in range(8):
+        added[e * SLAB : (e + 1) * SLAB, :] = slabs[e] + slabs[e + 8] + slabs[e + 16] + slabs[e + 24]
+    added[SLOTS:, :] = jnp.zeros((32, LANES), f32)
+    colour = iota((8, LANES), 0) < RGB
     pieces = []
     for r in range(ROWS):
-        piece = every[r * 8 : r * 8 + 8] * ratio_ref[r : r + 1, :]
-        pieces.append(piece.astype(bf16).astype(f32))
+        first = ((r // 2) % 8) * SLAB + (r // 16) * 2 + r % 2
+        piece = added[pl.ds(first, 8, stride=4), :] * ratio_ref[r : r + 1, :]
+        pieces.append(jnp.where(colour, piece, 0.0).astype(bf16).astype(f32))
     grad = jnp.concatenate(pieces, axis=1)
-    blended = blend_classes(every[BOTH : BOTH + SLOTS], mats_ref, before_ref, after_ref)
+    images = jnp.concatenate([slab[GRADS:] for slab in slabs], axis=0)
+    blended = blend_classes(images, mats_ref, before_ref, after_ref)
     grad_stack(grad, taps)
     summed = pieces[0]
     for piece in pieces[1:]:
@@ -527,12 +527,11 @@
     feats = jnp.transpose(features[0, 0], (1, 0, 2))
     args = (feats, conv_weight, bias, reward_grad[0, 0], tile_ids, blend_profile)
     here = [pltpu.with_memory_space_constraint(x, pltpu.HBM) for x in args]
-    rows, route, gather, mats, before, after, ratio, feats_held, weights_held = call(
+    rows, route, mats, before, after, ratio, feats_held, weights_held = call(
         functools.partial(conv_kernel, 2 * chunk),
         (
             pltpu.VMEM((WIDE, SLAB, LANES), bf16),
             pltpu.VMEM((4 * SLOTS, SLOTS), bf16),
-            pltpu.VMEM((BOTH + SLOTS, FLAT), bf16),
             pltpu.VMEM((9 * SLOTS, SLOTS), bf16),
             pltpu.VMEM((8, LANES), f32),
             pltpu.VMEM((SLOTS, LANES), f32),
@@ -557,7 +556,7 @@
         conv_flops,
         1 << 22,
         "conv",
-        out_specs=(VM,) * 9,
+        out_specs=(VM,) * 8,
     )(*here, own)
     rows = exchange(rows, ("y_lo", "z_hi", "z_lo", "c"))
     rows = call(
@@ -567,13 +566,13 @@
     rows, stack = call(
         functools.partial(weight_grad_kernel, chunk),
         (message(PEERS, PART + 8), jax.ShapeDtypeStruct((STACK, PIX), bf16)),
-        [VM] * 7,
-        [pltpu.VMEM((STACK, PIX), f32)],
+        [VM] * 6,
+        [pltpu.VMEM((STACK, PIX), f32), pltpu.VMEM((SLOTS + 32, LANES), f32)],
         conv_flops,
         1 << 22,
         "weight_grad",
         out_specs=(VM, VM),
-    )(rows, feats_held, ratio, gather, mats, before, after)
+    )(rows, feats_held, ratio, mats, before, after)
 
     feature_rows = call(
         feature_grad_kernel,

time: 78 us -> 77.5 us (level)
  no operation moved by 1% of the time
where the time goes in v9:
time: 77.5 us; the launch traced here: 77.1 us
  blocking collectives  60.7 us (78%)
  Pallas kernels  10.3 us (13%)
  starting transfers between devices  4.02 us (5%)
  waiting for transfers between devices  1.42 us (2%)
    all_to_all x4, blocking collectives, exchange(): return lax.all_to_all(rows, axes, 0, 0, tiled=True)  60.7 us
    all_to_all x1, starting transfers between devices, exchange(): return lax.all_to_all(rows, axes, 0, 0, tiled=True)  4.02 us
    pallas_call x1, Pallas kernels, per_device(): call(functools.partial(conv_kernel, 2 * chunk), (pltpu.VMEM((WIDE, SLAB,...  3 us
    pallas_call x1, Pallas kernels, per_device(): call(feature_grad_kernel, jax.ShapeDtypeStruct((TIN, CH, PIX), bf16), [pl...  2.69 us
    pallas_call x1, Pallas kernels, per_device(): call(functools.partial(weight_grad_kernel, chunk), (message(PEERS, PART +...  1.55 us
  transfers between devices with their start and end apart: 1, of which 1 were waited for; matrix products, arithmetic and copies ran while one was open for 0% of the time, Pallas kernels for 5%

profile of v9, /device:TPU:1, one launch (start us, length us, event | category | flops | bytes accessed | tf_op | source)
XLA Modules:
  0.0 77.1 jit_solution(15143310862330775220)
XLA Ops:
  0.6 3.0 %conv.1 = (bf16[32,16,128]{2,1,0:T(8,128)(2,1)S(1)}, bf16[512,128]{1,0:T(8,128)(2,1)S(1)}, bf16[1152,128]{1,0:T(8,128)(2,1)S(1)}, f32[8,128]{1,0:T(8,128)S(1)}, ...) custom-call(bf16[3,96,4096]{2,1,0:T(8,128)(2,1)} %bitcast.10, ...), custom_call_target="tpu_custom_call" | custom-call | flops 169869312 | bytes 4194304 | tf_op jit(solution)/shard_map/conv/pallas_call | solution.py:530
  3.7 21.7 %all_to_all.25.got_ref = bf16[32,16,128]{2,1,0:T(8,128)(2,1)S(1)} all-to-all(bf16[32,16,128]{2,1,0:T(8,128)(2,1)S(1)} %get-tuple-element.19), channel_id=1, replica_groups=mesh['y_hi'=4,'y_lo'=2,'z_hi'=4,'z_lo'=2,'c'=2,'clip'=4] {'y_lo','z_hi',..., dimensions={0} | all-to-all | bytes 262144 | tf_op jit(solution)/shard_map/all_to_all | solution.py:516
  25.3 0.3 route.1
  25.7 16.3 %all_to_all.26.got_ref = bf16[32,16,128]{2,1,0:T(8,128)(2,1)S(1)} all-to-all(bf16[32,16,128]{2,1,0:T(8,128)(2,1)S(1)} %route.1), channel_id=1, replica_groups=mesh['y_hi'=4,'y_lo'=2,'z_hi'=4,'z_lo'=2,'c'=2,'clip'=4] {'y_hi','y_lo',..., dimensions={0} | all-to-all | bytes 262144 | tf_op jit(solution)/shard_map/all_to_all | solution.py:516
  42.0 1.6 %weight_grad.1 = (bf16[16,24,128]{2,1,0:T(8,128)(2,1)S(1)}, bf16[72,4096]{1,0:T(8,128)(2,1)S(1)}) custom-call(bf16[32,16,128]{2,1,0:T(8,128)(2,1)S(1)} %all_to_all.26.got_ref, bf16[3,96,4096]{2,1,0:T(8,128)(2,1)S(1)} %get-tuple-element.21.feat_ref, f32[32,128]{1,0:T(8,128)S(1)} %get-tuple-element.22.ratio_ref, ...), custom_call_target="tpu_custom_call" | custom-call | flops 169869312 | bytes 4194304 | tf_op jit(solution)/shard_map/weight_grad/pallas_call | solution.py:566
  43.6 11.7 %all_to_all.27.got_ref = bf16[16,24,128]{2,1,0:T(8,128)(2,1)S(1)} all-to-all(bf16[16,24,128]{2,1,0:T(8,128)(2,1)S(1)} %get-tuple-element.26), channel_id=1, replica_groups=mesh['y_hi'=4,'y_lo'=2,'z_hi'=4,'z_lo'=2,'c'=2,'clip'=4] {'z_hi','z_lo',..., dimensions={0} | all-to-all | bytes 196608 | tf_op jit(solution)/shard_map/all_to_all | solution.py:516
  55.2 0.2 sum_z.1
  55.4 11.0 %all_to_all.28.got_ref = bf16[16,24,128]{2,1,0:T(8,128)(2,1)S(1)} all-to-all(bf16[16,24,128]{2,1,0:T(8,128)(2,1)S(1)} %sum_z.1), channel_id=1, replica_groups=mesh['y_hi'=4,'y_lo'=2,'z_hi'=4,'z_lo'=2,'c'=2,'clip'=4] {'y_hi','y_lo',..., dimensions={0} | all-to-all | bytes 196608 | tf_op jit(solution)/shard_map/all_to_all | solution.py:516
  66.4 0.8 %sum_y.1 = bf16[8,32,128]{2,1,0:T(8,128)(2,1)} custom-call(bf16[16,24,128]{2,1,0:T(8,128)(2,1)S(1)} %all_to_all.28.got_ref), custom_call_target="tpu_custom_call" | custom-call | flops 1048576 | bytes 131072 | tf_op jit(solution)/shard_map/sum_y/pallas_call | solution.py:604
  67.2 4.0 %all-to-all-start.4 = ((bf16[8,32,128]{2,1,0:T(8,128)(2,1)}), bf16[8,32,128]{2,1,0:T(8,128)(2,1)S(1)}, u32[]{:S(2)}, u32[]{:S(2)}) async-start(bf16[8,32,128]{2,1,0:T(8,128)(2,1)} %sum_y.1), calls=%async_computation.4 | async-start | bytes 131072 | tf_op jit(solution)/shard_map/all_to_all | solution.py:516
  71.2 2.7 %feature_grad.1 = bf16[3,96,4096]{2,1,0:T(8,128)(2,1)} custom-call(bf16[72,4096]{1,0:T(8,128)(2,1)S(1)} %get-tuple-element.27.stack_ref, bf16[3,72,96]{2,1,0:T(8,128)(2,1)S(1)} %get-tuple-element.28.weight_ref), custom_call_target="tpu_custom_call" | custom-call | flops 169869312 | bytes 4194304 | tf_op jit(solution)/shard_map/feature_grad/pallas_call | solution.py:577
  73.9 1.1 %decode.1 = bf16[3,4096]{1,0:T(4,128)(2,1)} custom-call(bf16[16,24,128]{2,1,0:T(8,128)(2,1)S(1)} %all_to_all.28.got_ref, s32[1]{0:T(128)} %bitcast.3.own_ref), custom_call_target="tpu_custom_call" | custom-call | flops 1048576 | bytes 131072 | tf_op jit(solution)/shard_map/decode/pallas_call | solution.py:596
  75.0 1.4 %all-to-all-done.4.got_ref = bf16[8,32,128]{2,1,0:T(8,128)(2,1)S(1)} async-done(((bf16[8,32,128]{2,1,0:T(8,128)(2,1)}), bf16[8,32,128]{2,1,0:T(8,128)(2,1)S(1)}, u32[]{:S(2)}, u32[]{:S(2)}) %all-to-all-start.4) | async-done | bytes 65568 | tf_op jit(solution)/shard_map/all_to_all | solution.py:516
  76.4 0.7 finish.1
Async XLA Ops:
  67.2 9.2 %all-to-all-start.4 = ((bf16[8,32,128]{2,1,0:T(8,128)(2,1)}), bf16[8,32,128]{2,1,0:T(8,128)(2,1)S(1)}, u32[]{:S(2)}, u32[]{:S(2)}) async-start(bf16[8,32,128]{2,1,0:T(8,128)(2,1)} %sum_y.1), calls=%async_computation.4 | async-start | bytes 131072 | tf_op jit(solution)/shard_map/all_to_all | solution.py:516

commit v10 on v9

--- a/solution.py
+++ b/solution.py
@@ -283,7 +283,7 @@
     eighths = pick_rows(iota((SLOTS, BOTH), 0) == to_row, grads)
     k = iota((1, SLOTS), 1)
     peer = ((k % 2) ^ (y % 2)) * 16 + (k // 32) * 4 + (((k // 16) % 2) ^ (z % 2)) * 2 + (((k // 8) % 2) ^ c)
-    place_ref[...] = onehot(iota((FLAT, SLOTS), 0) == peer * SLAB + GRADS + (k % 8) // 2)
+    place_ref[...] = onehot(iota((SLOTS, SLOTS), 0) == peer * 4 + (k % 8) // 2)
     for n in range(PIX // chunk):
         copies[n].wait()
         total = jnp.zeros((STACK, chunk), f32)
@@ -327,8 +327,8 @@
     images = jnp.dot(place_ref[...], classes, preferred_element_type=f32)
     for p in range(WIDE):
         e = (p // 16) * 4 + p % 4
-        slab = images[p * SLAB : (p + 1) * SLAB] + eighths[e * SLAB : (e + 1) * SLAB]
-        out_ref[p] = slab.astype(bf16)
+        slab = [eighths[e * SLAB : e * SLAB + GRADS], images[4 * p : 4 * p + 4]]
+        out_ref[p] = jnp.concatenate(slab, axis=0).astype(bf16)
 
 
 def half_rows(turned, h, colours):
@@ -549,7 +549,7 @@
             pltpu.VMEM((TIN, STACK, CH), f32),
             pltpu.VMEM((STACK, PIX), f32),
             pltpu.VMEM((ROWS, 8, LANES), f32),
-            pltpu.VMEM((FLAT, SLOTS), bf16),
+            pltpu.VMEM((SLOTS, SLOTS), bf16),
             pltpu.SemaphoreType.DMA((5,)),
             pltpu.SemaphoreType.DMA((PIX // (2 * chunk),)),
         ],

time: 77.5 us -> 77.4 us (level)
  no operation moved by 1% of the time
where the time goes in v10:
time: 77.4 us; the launch traced here: 77.1 us
  blocking collectives  60.7 us (78%)
  Pallas kernels  10.3 us (13%)
  starting transfers between devices  4.02 us (5%)
  waiting for transfers between devices  1.41 us (2%)
    all_to_all x4, blocking collectives, exchange(): return lax.all_to_all(rows, axes, 0, 0, tiled=True)  60.7 us
    all_to_all x1, starting transfers between devices, exchange(): return lax.all_to_all(rows, axes, 0, 0, tiled=True)  4.02 us
    pallas_call x1, Pallas kernels, per_device(): call(functools.partial(conv_kernel, 2 * chunk), (pltpu.VMEM((WIDE, SLAB,...  2.94 us
    pallas_call x1, Pallas kernels, per_device(): call(feature_grad_kernel, jax.ShapeDtypeStruct((TIN, CH, PIX), bf16), [pl...  2.71 us
    pallas_call x1, Pallas kernels, per_device(): call(functools.partial(weight_grad_kernel, chunk), (message(PEERS, PART +...  1.56 us
  transfers between devices with their start and end apart: 1, of which 1 were waited for; matrix products, arithmetic and copies ran while one was open for 0% of the time, Pallas kernels for 5%

profile of v10, /device:TPU:1, one launch (start us, length us, event | category | flops | bytes accessed | tf_op | source)
XLA Modules:
  0.0 77.1 jit_solution(2591928091661050817)
XLA Ops:
  0.6 2.9 %conv.1 = (bf16[32,16,128]{2,1,0:T(8,128)(2,1)S(1)}, bf16[512,128]{1,0:T(8,128)(2,1)S(1)}, bf16[1152,128]{1,0:T(8,128)(2,1)S(1)}, f32[8,128]{1,0:T(8,128)S(1)}, ...) custom-call(bf16[3,96,4096]{2,1,0:T(8,128)(2,1)} %bitcast.10, ...), custom_call_target="tpu_custom_call" | custom-call | flops 169869312 | bytes 4194304 | tf_op jit(solution)/shard_map/conv/pallas_call | solution.py:530
  3.6 21.7 %all_to_all.25.got_ref = bf16[32,16,128]{2,1,0:T(8,128)(2,1)S(1)} all-to-all(bf16[32,16,128]{2,1,0:T(8,128)(2,1)S(1)} %get-tuple-element.19), channel_id=1, replica_groups=mesh['y_hi'=4,'y_lo'=2,'z_hi'=4,'z_lo'=2,'c'=2,'clip'=4] {'y_lo','z_hi',..., dimensions={0} | all-to-all | bytes 262144 | tf_op jit(solution)/shard_map/all_to_all | solution.py:516
  25.3 0.3 route.1
  25.6 16.3 %all_to_all.26.got_ref = bf16[32,16,128]{2,1,0:T(8,128)(2,1)S(1)} all-to-all(bf16[32,16,128]{2,1,0:T(8,128)(2,1)S(1)} %route.1), channel_id=1, replica_groups=mesh['y_hi'=4,'y_lo'=2,'z_hi'=4,'z_lo'=2,'c'=2,'clip'=4] {'y_hi','y_lo',..., dimensions={0} | all-to-all | bytes 262144 | tf_op jit(solution)/shard_map/all_to_all | solution.py:516
  41.9 1.6 %weight_grad.1 = (bf16[16,24,128]{2,1,0:T(8,128)(2,1)S(1)}, bf16[72,4096]{1,0:T(8,128)(2,1)S(1)}) custom-call(bf16[32,16,128]{2,1,0:T(8,128)(2,1)S(1)} %all_to_all.26.got_ref, bf16[3,96,4096]{2,1,0:T(8,128)(2,1)S(1)} %get-tuple-element.21.feat_ref, f32[32,128]{1,0:T(8,128)S(1)} %get-tuple-element.22.ratio_ref, ...), custom_call_target="tpu_custom_call" | custom-call | flops 169869312 | bytes 4194304 | tf_op jit(solution)/shard_map/weight_grad/pallas_call | solution.py:566
  43.5 11.7 %all_to_all.27.got_ref = bf16[16,24,128]{2,1,0:T(8,128)(2,1)S(1)} all-to-all(bf16[16,24,128]{2,1,0:T(8,128)(2,1)S(1)} %get-tuple-element.26), channel_id=1, replica_groups=mesh['y_hi'=4,'y_lo'=2,'z_hi'=4,'z_lo'=2,'c'=2,'clip'=4] {'z_hi','z_lo',..., dimensions={0} | all-to-all | bytes 196608 | tf_op jit(solution)/shard_map/all_to_all | solution.py:516
  55.2 0.2 sum_z.1
  55.3 11.0 %all_to_all.28.got_ref = bf16[16,24,128]{2,1,0:T(8,128)(2,1)S(1)} all-to-all(bf16[16,24,128]{2,1,0:T(8,128)(2,1)S(1)} %sum_z.1), channel_id=1, replica_groups=mesh['y_hi'=4,'y_lo'=2,'z_hi'=4,'z_lo'=2,'c'=2,'clip'=4] {'y_hi','y_lo',..., dimensions={0} | all-to-all | bytes 196608 | tf_op jit(solution)/shard_map/all_to_all | solution.py:516
  66.3 0.8 %sum_y.1 = bf16[8,32,128]{2,1,0:T(8,128)(2,1)} custom-call(bf16[16,24,128]{2,1,0:T(8,128)(2,1)S(1)} %all_to_all.28.got_ref), custom_call_target="tpu_custom_call" | custom-call | flops 1048576 | bytes 131072 | tf_op jit(solution)/shard_map/sum_y/pallas_call | solution.py:604
  67.1 4.0 %all-to-all-start.4 = ((bf16[8,32,128]{2,1,0:T(8,128)(2,1)}), bf16[8,32,128]{2,1,0:T(8,128)(2,1)S(1)}, u32[]{:S(2)}, u32[]{:S(2)}) async-start(bf16[8,32,128]{2,1,0:T(8,128)(2,1)} %sum_y.1), calls=%async_computation.4 | async-start | bytes 131072 | tf_op jit(solution)/shard_map/all_to_all | solution.py:516
  71.1 2.7 %feature_grad.1 = bf16[3,96,4096]{2,1,0:T(8,128)(2,1)} custom-call(bf16[72,4096]{1,0:T(8,128)(2,1)S(1)} %get-tuple-element.27.stack_ref, bf16[3,72,96]{2,1,0:T(8,128)(2,1)S(1)} %get-tuple-element.28.weight_ref), custom_call_target="tpu_custom_call" | custom-call | flops 169869312 | bytes 4194304 | tf_op jit(solution)/shard_map/feature_grad/pallas_call | solution.py:577
  73.8 1.1 %decode.1 = bf16[3,4096]{1,0:T(4,128)(2,1)} custom-call(bf16[16,24,128]{2,1,0:T(8,128)(2,1)S(1)} %all_to_all.28.got_ref, s32[1]{0:T(128)} %bitcast.3.own_ref), custom_call_target="tpu_custom_call" | custom-call | flops 1048576 | bytes 131072 | tf_op jit(solution)/shard_map/decode/pallas_call | solution.py:596
  74.9 1.4 %all-to-all-done.4.got_ref = bf16[8,32,128]{2,1,0:T(8,128)(2,1)S(1)} async-done(((bf16[8,32,128]{2,1,0:T(8,128)(2,1)}), bf16[8,32,128]{2,1,0:T(8,128)(2,1)S(1)}, u32[]{:S(2)}, u32[]{:S(2)}) %all-to-all-start.4) | async-done | bytes 65568 | tf_op jit(solution)/shard_map/all_to_all | solution.py:516
  76.3 0.7 finish.1
Async XLA Ops:
  67.1 9.2 %all-to-all-start.4 = ((bf16[8,32,128]{2,1,0:T(8,128)(2,1)}), bf16[8,32,128]{2,1,0:T(8,128)(2,1)S(1)}, u32[]{:S(2)}, u32[]{:S(2)}) async-start(bf16[8,32,128]{2,1,0:T(8,128)(2,1)} %sum_y.1), calls=%async_computation.4 | async-start | bytes 131072 | tf_op jit(solution)/shard_map/all_to_all | solution.py:516
